TPU v7x, 32 devices: a whole 2x2x4 slice. The times are simulated.
32 devices in a mesh: hier: 8 (over z, x), row: 4 (over y, core).
Axes of the slice: x: 2, y: 2, z: 4, core: 2. Of those that a mesh axis runs over, the one named last changes fastest.
Arguments:
- state: bfloat16 [24, 2, 1024, 1024], P('hier', None, 'row'), may hold values from -6 to 6
- prev_slope: float32 [24, 2, 1024, 1024], P('hier', None, 'row'), may hold values from -6 to 6
- accumulated: float32 [24, 2, 1024, 1024], P('hier', None, 'row'), may hold values from -6 to 6
- hamiltonian: bfloat16 [2, 1024, 1024], P(None, 'row'), as said below
- couple_v: float32 [6, 1024], replicated, may hold values from -4 to 4
- coupling: float32 [2, 6], replicated, may hold values from 0.2 to 1
- damping: float32 [6], replicated, may hold values from 0.2 to 2
- occupation: int32 [24, 6], P('hier'), may hold values from 0 to 2, as said below
- parents: int32 [24, 6], P('hier'), may hold values from -1 to 23, as said below
- children: int32 [24, 6], P('hier'), may hold values from -1 to 22, as said below
Outputs:
- slope: float32 [24, 2, 1024, 1024], P('hier', None, 'row')
- accumulated_out: float32 [24, 2, 1024, 1024], P('hier', None, 'row')
Inputs may be any that keep to these rules, and one draw needn't show every extreme that they name: `occupation`: row s is the index of the operator in slot s. The rows are the 24 indices of smallest total among all indices of 6 entries with total at most 4, taken by total and then lexicographically; the all-zero index stands in the last slot, the others in a slot order drawn from the seed; the set is closed under lowering one entry. `parents`: entry (s, k) is the slot whose index equals slot s's index with entry k lowered by one, or -1 where entry k of slot s is 0. `children`: entry (s, k) is the slot whose index equals slot s's index with entry k raised by one, or -1 where that index is not among the 24. `hamiltonian`: Hermitian: the real part is symmetric, the imaginary part antisymmetric.
All inputs are finite; a program needn't handle non-finite values.
Results may differ from a plain program's by a relative error of at most 0.0029.
Values may be sent and summed in bfloat16 or wider, within the bound.
No kernel may reach another device: no remote copies, remote signals or barrier semaphores. Data moves between devices by JAX's collectives and lax.ppermute only.
A program may use at most 320 MiB of HBM per device.

v0:
```python
import functools

import jax
import jax.numpy as jnp
import numpy as np
from jax import lax
from jax.experimental import pallas as pl
from jax.experimental.pallas import tpu as pltpu
from jax.sharding import PartitionSpec as P

step_size = 0.5
highest_total = 4
row_tile = 16
pieces = 2
MIB = 1024 * 1024
f32 = jnp.float32
bf16 = jnp.bfloat16


def index_rows(slots, modes):
    entries = [()]
    for _ in range(modes):
        entries = [
            entry + (level,)
            for entry in entries
            for level in range(highest_total + 1)
            if sum(entry) + level <= highest_total
        ]
    return sorted(entries, key=lambda entry: (sum(entry), entry))[:slots]


def coupled_to(rows):
    lookup = {entry: place for place, entry in enumerate(rows)}
    result = []
    for entry in rows:
        terms = []
        for mode, level in enumerate(entry):
            raised = entry[:mode] + (level + 1,) + entry[mode + 1 :]
            if raised in lookup:
                terms.append((lookup[raised], mode, True, 1))
            if level > 0:
                lowered = entry[:mode] + (level - 1,) + entry[mode + 1 :]
                terms.append((lookup[lowered], mode, False, level))
        result.append(terms)
    return result


def smaller_class(rows):
    classes = [[c for c, entry in enumerate(rows) if sum(entry) % 2 == rest] for rest in (0, 1)]
    return min(classes, key=len)


def params(megabytes):
    return pltpu.CompilerParams(vmem_limit_bytes=megabytes * MIB)


def whole():
    return pl.BlockSpec(memory_space=pltpu.VMEM)


def anywhere():
    return pl.BlockSpec(memory_space=pl.ANY)


def scalars():
    return pl.BlockSpec(memory_space=pltpu.SMEM)


def swap(array, axis, size, bit):
    return lax.ppermute(array, axis, [(i, i ^ bit) for i in range(size)])


def tie(arrays):
    return lax.optimization_barrier(arrays)


def row_bits(size):
    return [1 << i for i in reversed(range(size.bit_length() - 1))]


def tree(array, size, bits):
    parts = {0: array}
    for bit in bits:
        for mask in list(parts):
            parts[mask ^ bit] = swap(parts[mask], "row", size, bit)
    return parts


def section_kernel(where, state, slope, section, *chunks):
    value = (state[...].astype(f32) + (0.5 * step_size) * slope[...]).astype(bf16)
    section[...] = value
    width = chunks[0].shape[-1]
    for b, chunk in enumerate(chunks):
        columns = pl.ds(pl.multiple_of((where[0] ^ b) * width, 128), width)
        chunk[...] = section[:, :, :, columns]


def make_section(p, split, state, prev_slope, place, group):
    ops, parts, rows, columns = state.shape
    height, width = rows // split, columns // group
    block = pl.BlockSpec((1, parts, height, columns), lambda a, _: (a, 0, p, 0))
    out = pl.BlockSpec((1, parts, height, columns), lambda a, _: (a, 0, 0, 0))
    chunk = pl.BlockSpec((1, parts, height, width), lambda a, _: (a, 0, 0, 0))
    section, *chunks = pl.pallas_call(
        section_kernel,
        grid_spec=pltpu.PrefetchScalarGridSpec(
            num_scalar_prefetch=1,
            grid=(ops,),
            in_specs=[block, block],
            out_specs=[out] + [chunk] * group,
        ),
        out_shape=[jax.ShapeDtypeStruct((ops, parts, height, columns), bf16)]
        + [jax.ShapeDtypeStruct((ops, parts, height, width), bf16)] * group,
        compiler_params=params(60 if p == 0 else 16),
        cost_estimate=pl.CostEstimate(flops=1, bytes_accessed=1, transcendentals=0),
        name="section",
    )(place, state, prev_slope)
    return section, chunks


def fill_factors(vrows, vcols, coupling, factors):
    modes = vrows.shape[0]
    for k in range(modes):
        first = vrows[k]
        second = vcols[k : k + 1, :]
        diff = first - second
        factors[k] = diff
        factors[modes + k] = coupling[0, k] * diff
        factors[2 * modes + k] = coupling[1, k] * (first + second)


def add_terms(terms, places, held, factors, modes, rows, real, imag):
    for other, mode, child, count in terms:
        place = places[other]
        x_real = held[place, 0, rows, :].astype(f32)
        x_imag = held[place, 1, rows, :].astype(f32)
        if child:
            diff = factors[mode, rows, :]
            real = real + diff * x_imag
            imag = imag - diff * x_real
        else:
            first = factors[modes + mode, rows, :]
            second = factors[2 * modes + mode, rows, :]
            if count != 1:
                first, second = count * first, count * second
            real = real + (first * x_imag + second * x_real)
            imag = imag + (second * x_imag - first * x_real)
    return real, imag


def partial_kernel(links, sides, group, places, coupling, vrows, vcols, *refs):
    chunks, out, held, factors, sems = refs[:group], *refs[group:]
    modes = vrows.shape[0]
    height, width = held.shape[2:]
    ops = chunks[0].shape[0]
    empty = group * ops
    loads = [
        pltpu.make_async_copy(chunk, held.at[pl.ds(b * ops, ops)], sems.at[b])
        for b, chunk in enumerate(chunks)
    ]
    for load in loads:
        load.start()
    fill_factors(vrows, vcols, coupling, factors)
    held[empty] = jnp.zeros(held.shape[1:], bf16)
    for load in loads:
        load.wait()
    for u, c in enumerate(sides):

        @pl.when(places[c] < empty)
        def _():
            out[u] = held[places[c]]

        @pl.when(places[c] == empty)
        def _():
            @pl.loop(0, height // row_tile)
            def _(i):
                rows = pl.ds(pl.multiple_of(i * row_tile, row_tile), row_tile)
                zero = jnp.zeros((row_tile, width), f32)
                real, imag = add_terms(links[c], places, held, factors, modes, rows, zero, zero)
                out[u, 0, rows, :] = real.astype(bf16)
                out[u, 1, rows, :] = imag.astype(bf16)


def coupled_kernel(links, sides, group, places, coupling, vrows, vcols, *refs):
    chunks, received, outs = refs[:group], refs[group], refs[group + 1 : 2 * group + 1]
    held, done, factors, spots, sems = refs[2 * group + 1 :]
    modes = vrows.shape[0]
    height, width = held.shape[2:]
    ops = chunks[0].shape[0]
    empty = group * ops
    loads = [
        pltpu.make_async_copy(chunk, held.at[pl.ds(b * ops, ops)], sems.at[b])
        for b, chunk in enumerate(chunks)
    ]
    loads.append(
        pltpu.make_async_copy(received, held.at[pl.ds(empty + 1, len(sides))], sems.at[group])
    )
    for load in loads:
        load.start()
    fill_factors(vrows, vcols, coupling, factors)
    held[empty] = jnp.zeros(held.shape[1:], bf16)
    for c in range(len(links)):
        spots[c] = places[c]
    for u, c in enumerate(sides):
        spots[c] = jnp.where(places[c] == empty, empty + 1 + u, places[c])
    for load in loads:
        load.wait()
    for c in range(len(links)):

        @pl.when(places[c] < empty)
        def _():
            @pl.loop(0, height // row_tile)
            def _(i):
                rows = pl.ds(pl.multiple_of(i * row_tile, row_tile), row_tile)
                if c in sides:
                    u = empty + 1 + sides.index(c)
                    real, imag = held[u, 0, rows, :].astype(f32), held[u, 1, rows, :].astype(f32)
                else:
                    real = imag = jnp.zeros((row_tile, width), f32)
                real, imag = add_terms(links[c], spots, held, factors, modes, rows, real, imag)
                done[places[c], 0, rows, :] = real.astype(bf16)
                done[places[c], 1, rows, :] = imag.astype(bf16)

    stores = [
        pltpu.make_async_copy(done.at[pl.ds(b * ops, ops)], out, sems.at[group + 1 + b])
        for b, out in enumerate(outs)
    ]
    for store in stores:
        store.start()
    for store in stores:
        store.wait()


def coupling_scratch(entries, height, width, modes):
    return [pltpu.VMEM((entries, 2, height, width), bf16)], [pltpu.VMEM((3 * modes, height, width), f32)]


def make_partial(chunks, places, coupling, vrows, vcols, links, sides):
    group = len(chunks)
    ops, _, height, width = chunks[0].shape
    held, factors = coupling_scratch(group * ops + 1, height, width, vrows.shape[0])
    size = height * width
    return pl.pallas_call(
        functools.partial(partial_kernel, links, sides, group),
        in_specs=[scalars(), scalars()] + [whole()] * 2 + [anywhere()] * group,
        out_specs=whole(),
        out_shape=jax.ShapeDtypeStruct((len(sides), 2, height, width), bf16),
        scratch_shapes=held + factors + [pltpu.SemaphoreType.DMA((group,))],
        compiler_params=params(12),
        cost_estimate=pl.CostEstimate(
            flops=40 * len(sides) * size,
            bytes_accessed=4 * size * (group * ops + len(sides)),
            transcendentals=0,
        ),
        name="partial_sums",
    )(places, coupling, vrows, vcols, *chunks)


def make_coupled(chunks, received, places, coupling, vrows, vcols, links, sides):
    group = len(chunks)
    ops, _, height, width = chunks[0].shape
    held, factors = coupling_scratch(group * ops + 1 + len(sides), height, width, vrows.shape[0])
    size = height * width
    return pl.pallas_call(
        functools.partial(coupled_kernel, links, sides, group),
        in_specs=[scalars(), scalars()] + [whole()] * 2 + [anywhere()] * (1 + group),
        out_specs=[anywhere()] * group,
        out_shape=[jax.ShapeDtypeStruct(chunks[0].shape, bf16)] * group,
        scratch_shapes=held
        + [pltpu.VMEM((group * ops, 2, height, width), bf16)]
        + factors
        + [pltpu.SMEM((len(links),), jnp.int32), pltpu.SemaphoreType.DMA((2 * group + 1,))],
        compiler_params=params(16),
        cost_estimate=pl.CostEstimate(
            flops=40 * group * ops * size,
            bytes_accessed=4 * size * (2 * group * ops + len(sides)),
            transcendentals=0,
        ),
        name="coupling_sums",
    )(places, coupling, vrows, vcols, *chunks, received)


def complex_rows(left, right):
    _, height, depth = left.shape
    left = left.reshape(2 * height, depth)
    first = jnp.dot(left, right[0], preferred_element_type=f32)
    second = jnp.dot(left, right[1], preferred_element_type=f32)
    return first[:height] - second[height:], second[:height] + first[height:]


def right_kernel(split, count, where, decay, *refs):
    sections, h_parts, (out, h_all) = refs[:split], refs[split:-2], refs[-2:]
    j, a = pl.program_id(0), pl.program_id(1)
    rows, tile = h_parts[0].shape[1:]
    height = sections[0].shape[2]

    @pl.when(a == 0)
    def _():
        for b in range(count):
            place = pl.ds(pl.multiple_of((where[0] ^ b) * rows, row_tile), rows)
            h_all[:, place, :] = h_parts[b][...]

    columns = pl.ds(pl.multiple_of(j * tile, 128), tile)
    lost = decay[a]
    for p, section in enumerate(sections):
        real, imag = complex_rows(section[a], h_all)
        here = slice(p * height, (p + 1) * height)
        out[0, 0, here, :] = -imag - lost * section[a, 0, :, columns].astype(f32)
        out[0, 1, here, :] = real - lost * section[a, 1, :, columns].astype(f32)


def make_right(sections, h_parts, place, decay):
    ops, _, height, columns = sections[0].shape
    split, count = len(sections), len(h_parts)
    rows, tile = height * split, min(columns, 512)
    held = pl.BlockSpec((ops, 2, height, columns), lambda j, a: (0, 0, 0, 0))
    return pl.pallas_call(
        functools.partial(right_kernel, split, count),
        grid=(columns // tile, ops),
        in_specs=[scalars(), scalars()]
        + [held] * split
        + [pl.BlockSpec((2, rows, tile), lambda j, a: (0, 0, j))] * count,
        out_specs=pl.BlockSpec((1, 2, rows, tile), lambda j, a: (a, 0, 0, j)),
        out_shape=jax.ShapeDtypeStruct((ops, 2, rows, columns), f32),
        scratch_shapes=[pltpu.VMEM((2, count * rows, tile), bf16)],
        compiler_params=params(24),
        cost_estimate=pl.CostEstimate(
            flops=8 * ops * rows * columns * columns,
            bytes_accessed=4 * columns * (columns + 3 * ops * rows),
            transcendentals=0,
        ),
        name="right_products",
    )(place, decay, *sections, *h_parts)


def left_kernel(count, where, h_own, base, *refs):
    s_parts, (out, s_all) = refs[:count], refs[count:]
    height = s_parts[0].shape[2]
    for b in range(count):
        place = pl.ds(pl.multiple_of((where[0] ^ b) * height, row_tile), height)
        s_all[:, place, :] = s_parts[b][0]
    real, imag = complex_rows(h_own[...], s_all)
    out[0, 0] = base[0, 0] + imag
    out[0, 1] = base[0, 1] - real


def make_left(s_parts, h_columns, base, place):
    ops, _, height, columns = s_parts[0].shape
    count, rows, tile = len(s_parts), base.shape[2], min(columns, 512)
    block = pl.BlockSpec((1, 2, rows, tile), lambda j, a: (a, 0, 0, j))
    return pl.pallas_call(
        functools.partial(left_kernel, count),
        grid=(columns // tile, ops),
        in_specs=[
            scalars(),
            pl.BlockSpec(h_columns.shape, lambda j, a: (0, 0, 0)),
            block,
        ]
        + [pl.BlockSpec((1, 2, height, tile), lambda j, a: (a, 0, 0, j))] * count,
        out_specs=block,
        out_shape=jax.ShapeDtypeStruct(base.shape, f32),
        scratch_shapes=[pltpu.VMEM((2, count * height, tile), bf16)],
        compiler_params=params(16),
        cost_estimate=pl.CostEstimate(
            flops=8 * ops * rows * columns * count * height,
            bytes_accessed=4 * ops * columns * (count * height + 4 * rows),
            transcendentals=0,
        ),
        name="left_products",
    )(place, h_columns, base, *s_parts)


def final_kernel(group, count, where, h_own, base, accumulated, *refs):
    s_parts, sums = refs[:count], refs[count : count + group]
    slope, total, s_all = refs[-3:]
    a, j = pl.program_id(0), pl.program_id(1)
    height, tile, width = s_parts[0].shape[2], slope.shape[3], sums[0].shape[3]
    for b in range(count):
        place = pl.ds(pl.multiple_of((where[1] ^ b) * height, row_tile), height)
        s_all[:, place, :] = s_parts[b][0]
    real, imag = complex_rows(h_own[...], s_all)
    slope[0, 0] = base[0, 0] + imag
    slope[0, 1] = base[0, 1] - real
    for b in range(group):
        first = (where[0] ^ b) * width - j * tile

        @pl.when(jnp.logical_and(first >= 0, first < tile))
        def _():
            columns = pl.ds(pl.multiple_of(first, 128), width)
            slope[0, :, :, columns] += sums[b][a].astype(f32)

    total[...] = accumulated[...] + (step_size / 3.0) * slope[...]


def make_final(p, split, base, accumulated, s_parts, h_columns, sums, places, earlier=()):
    ops, parts, rows, columns = base.shape
    group, count = len(sums), len(s_parts)
    height, tile = rows // split, min(columns, 512)
    block = pl.BlockSpec((1, parts, height, tile), lambda a, j, _: (a, 0, p, j))
    held = pl.BlockSpec(sums[0].shape, lambda a, j, _: (0, 0, 0, 0))
    own = pl.BlockSpec((2, height, h_columns.shape[2]), lambda a, j, _: (0, p, 0))
    part = pl.BlockSpec((1, parts, height, tile), lambda a, j, _: (a, 0, 0, j))
    inputs = [own, block, block] + [part] * count + [held] * group
    return pl.pallas_call(
        lambda *refs: final_kernel(
            group, count, *refs[: 1 + len(inputs)], *refs[1 + len(inputs) + len(earlier) :]
        ),
        grid_spec=pltpu.PrefetchScalarGridSpec(
            num_scalar_prefetch=1,
            grid=(ops, columns // tile),
            in_specs=inputs + [anywhere()] * len(earlier),
            out_specs=[block, block],
            scratch_shapes=[pltpu.VMEM((2, count * height, tile), bf16)],
        ),
        out_shape=[jax.ShapeDtypeStruct(base.shape, f32)] * 2,
        input_output_aliases={1 + len(inputs) + k: k for k in range(len(earlier))},
        compiler_params=params(16),
        cost_estimate=pl.CostEstimate(
            flops=8 * ops * height * columns * count * height,
            bytes_accessed=36 * base.size // split,
            transcendentals=0,
        ),
        name="outputs",
    )(places, h_columns, base, accumulated, *s_parts, *sums, *earlier)


def shards(
    hier,
    row,
    state,
    prev_slope,
    accumulated,
    hamiltonian,
    couple_v,
    coupling,
    damping,
    occupation,
    parents,
    children,
):
    ops, _, rows, columns = state.shape
    modes = occupation.shape[1]
    group = hier // 2
    width = columns // group
    split = pieces
    height = rows // split
    table = index_rows(hier * ops, modes)
    links, sides = coupled_to(table), smaller_class(table)

    hier_at, row_at = lax.axis_index("hier"), lax.axis_index("row")
    own = hier_at % group
    own_place, row_place = own.reshape(1).astype(jnp.int32), row_at.reshape(1).astype(jnp.int32)

    bits = row_bits(row)
    top, low = bits[0], bits[1:]

    def spread(p):
        return [chunks[p][0]] + [swap(chunks[p][b], "hier", hier, b) for b in range(1, group)]

    def partial(p):
        return make_partial(got[p], places, coupling, heres[p], vcols, links, sides)

    def coupled(p):
        return make_coupled(got[p], received[p], places, coupling, heres[p], vcols, links, sides)

    def gather_back(done):
        return [done[0]] + [swap(done[b], "hier", hier, b) for b in range(1, group)]

    def joined(near, across):
        far = {mask ^ top: part for mask, part in tree(across, row, low).items()}
        parts = {**near, **far}
        return [parts[b] for b in range(row)]

    got, sent, received, sums, outs = [], [], [], [], []

    half = [occupation] + [swap(occupation, "hier", hier, b) for b in range(1, group)]
    first, first_chunks = make_section(0, split, state, prev_slope, own_place, group)
    first, first_chunks, half, state, prev_slope, couple_v, hamiltonian = tie(
        (first, first_chunks, half, state, prev_slope, couple_v, hamiltonian)
    )

    h_top, h_near = swap(hamiltonian, "row", row, top), tree(hamiltonian, row, low)
    second, second_chunks = make_section(1, split, state, prev_slope, own_place, group)
    chunks, sections = [first_chunks, second_chunks], [first, second]
    got.append(spread(0))

    known = jnp.asarray(np.array(table, np.int32))
    found = jnp.concatenate(half, axis=0)
    same = jnp.all(found[None, :, :] == known[:, None, :], axis=2)
    spot = jnp.arange(group * ops, dtype=jnp.int32)[None, :]
    places = jnp.min(jnp.where(same, spot, group * ops), axis=1).astype(jnp.int32)
    vrows = lax.dynamic_slice_in_dim(couple_v, row_at * rows, rows, 1)[:, :, None]
    vcols = lax.dynamic_slice_in_dim(couple_v, own * width, width, 1)
    heres = [vrows[:, p * height : (p + 1) * height] for p in range(split)]
    decay = jnp.sum(half[0].astype(f32) * damping[None, :], axis=1)
    second, kept = tie((second, hamiltonian))
    sections[1] = second
    blocks = kept.reshape(2, rows, row, split, height)
    h_columns = [blocks[:, :, :, p].reshape(2, rows, row * height) for p in range(split)]
    got, chunks, sections, places, heres, vcols, decay, h_columns, h_top, h_near = tie(
        (got, chunks, sections, places, heres, vcols, decay, h_columns, h_top, h_near)
    )

    sent.append(partial(0))
    received.append(swap(sent[0], "hier", hier, group))
    got.append(spread(1))
    across = swap(sections[0], "row", row, top)
    got, received, across, sections, h_top, h_near = tie(
        (got, received, across, sections, h_top, h_near)
    )

    sent.append(partial(1))
    received.append(swap(sent[1], "hier", hier, group))
    last_across = swap(sections[1], "row", row, top)
    s_parts = joined(tree(sections[0], row, low), across)
    h_parts = joined(h_near, h_top)
    done, s_parts, h_parts = tie((coupled(0), s_parts, h_parts))
    sums.append(gather_back(done))
    base = make_right(sections, h_parts, row_place, decay)
    base = make_left(s_parts, h_columns[0], base, row_place)
    received, last_across, sums, base, sections = tie(
        (received, last_across, sums, base, sections)
    )

    s_parts = joined(tree(sections[1], row, low), last_across)
    sums.append(gather_back(coupled(1)))
    both = jnp.concatenate([own_place, row_place])
    for p in range(split):
        outs = make_final(
            p, split, base, accumulated, s_parts, h_columns[1], sums[p], both, outs
        )
    slope, total = outs
    return slope, total


def solution(mesh):
    return jax.shard_map(
        functools.partial(shards, mesh.shape["hier"], mesh.shape["row"]),
        mesh=mesh,
        in_specs=(
            P("hier", None, "row", None),
            P("hier", None, "row", None),
            P("hier", None, "row", None),
            P(None, "row", None),
            P(),
            P(),
            P(),
            P("hier", None),
            P("hier", None),
            P("hier", None),
        ),
        out_specs=(P("hier", None, "row", None), P("hier", None, "row", None)),
        check_vma=False,
    )
```

profile of v0, /device:TPU:0, one launch (start us, length us, event | category | flops | bytes accessed | tf_op | source)
XLA Modules:
  0.0 161.3 jit_solution(11347611751161663375)
XLA Ops:
  0.6 3.1 %collective-permute-start.1 = (s32[3,6]{1,0:T(4,128)}, s32[3,6]{1,0:T(4,128)S(1)}, u32[]{:S(2)}, u32[]{:S(2)}) collective-permute-start(s32[3,6]{1,0:T(4,128)} %param.18), channel_id=1, source_target_pairs={{0,8},{4,12},{8,0},{12,4},{16,24},{20,28},{24,16},{28,20},{1,9},{5... | collective-permute-start | bytes 224 | tf_op jit(solution)/shard_map/ppermute | solution.py:70
  3.7 1.5 collective-permute-start
  5.2 0.1 collective-permute-start.2
  5.3 5.2 %section.2 = (bf16[3,2,128,1024]{3,2,1,0:T(8,128)(2,1)}, bf16[3,2,128,256]{3,2,1,0:T(8,128)(2,1)}, bf16[3,2,128,256]{3,2,1,0:T(8,128)(2,1)}, bf16[3,2,128,256]{3,2,1,0:T(8,128)(2,1)}, bf16[3,2,128,256]{3,2,1,0:T(8,128)(2,1)}) custom-call(s32[1]{0:T(128)} %bitcast.where, bf16[3,2,256,1024]{3,2,1,0:T(8,128)(2,1)} %state.2, f32[3,2,256,1024]{3,2,1,0:T(8,128)} %slope.2), custom_call_target="tpu_custom_call" | custom-call | flops 1 | bytes 1 | tf_op jit(solution)/shard_map/section/pallas_call | solution.py:104
  10.5 0.0 collective-permute-done.1
  10.5 0.0 collective-permute-done
  10.5 0.1 collective-permute-start.7
  10.6 2.0 %collective-permute-start.6 = (bf16[2,256,1024]{2,1,0:T(8,128)(2,1)}, bf16[2,256,1024]{2,1,0:T(8,128)(2,1)}, u32[]{:S(2)}, u32[]{:S(2)}) collective-permute-start(bf16[2,256,1024]{2,1,0:T(8,128)(2,1)} %refs_2_), channel_id=1, source_target_pairs={{0,2},{1,3},{2,0},{3,1},{4,6},{5,7},{6,4},{7,5},{8,10},{9,11},{10,... | collective-permute-start | bytes 3145736 | tf_op jit(solution)/shard_map/ppermute | solution.py:70
  12.6 1.5 collective-permute-start.3
  14.1 1.6 collective-permute-start.4
  15.6 0.4 collective-permute-start.5
  16.1 2.8 %copy-done = f32[3,2,256,1024]{3,2,1,0:T(8,128)S(1)} copy-done((f32[3,2,256,1024]{3,2,1,0:T(8,128)S(1)}, f32[3,2,256,1024]{3,2,1,0:T(8,128)}, u32[]{:S(2)}) %copy-start) | copy-done | bytes 6291480
  18.8 1.3 section.3
  20.1 0.0 copy-start.2
  20.1 1.1 copy-done.2
  21.3 0.8 copy-done.4
  22.0 0.8 copy-done.12
  22.8 0.8 copy-done.13
  23.6 0.7 copy-done.14
  24.3 1.8 %reshape.18 = bf16[2,256,4,2,128]{4,3,2,1,0:T(2,128)(2,1)S(1)} reshape(bf16[2,256,1024]{2,1,0:T(8,128)(2,1)} %refs_2_) | data formatting | bytes 2097152 | tf_op jit(solution)/shard_map/reshape | solution.py:498
  26.1 0.0 copy-start.17
  26.1 0.0 copy-start.11
  26.2 6.8 %slice_reduce_fusion = (bf16[2,256,4,128]{3,2,1,0:T(4,128)(2,1)S(1)}, bf16[2,256,4,128]{3,2,1,0:T(4,128)(2,1)}) fusion(bf16[2,256,4,2,128]{4,3,2,1,0:T(2,128)(2,1)S(1)} %reshape.18), kind=kLoop, calls=%fused_computation | loop fusion | bytes 2097152 | tf_op jit(solution)/shard_map/slice | solution.py:499
  33.0 0.1 multiply_reduce_fusion.decay
  33.1 0.2 copy.24.vrows
  33.3 0.2 copy.23.vrows
  33.5 0.2 reshape_squeeze.7.refs_1_
  33.7 1.2 reshape_squeeze.6.h_own
  34.9 0.1 compare_reduce_fusion
  35.1 0.0 collective-permute-done.3.refs_1_
  35.1 1.5 collective-permute-done.6.refs_4_
  36.6 1.8 %collective-permute-start.12 = (bf16[3,2,128,1024]{3,2,1,0:T(8,128)(2,1)}, bf16[3,2,128,1024]{3,2,1,0:T(8,128)(2,1)S(1)}, u32[]{:S(2)}, u32[]{:S(2)}) collective-permute-start(bf16[3,2,128,1024]{3,2,1,0:T(8,128)(2,1)} %get-tuple-element.164.refs_0_), channel_id=1, source_target_pairs={{0,2},{1,3},{2,0},{3,1},{4,6},{5,7},{6,4},{7,5},{8,10},{9,11},{10,... | collective-permute-start | bytes 4718600 | tf_op jit(solution)/shard_map/ppermute | solution.py:70
  38.4 1.0 copy-done.7
  39.4 2.6 %partial_sums.2 = bf16[6,2,128,256]{3,2,1,0:T(8,128)(2,1)S(1)} custom-call(s32[24]{0:T(128)S(1)} %select_reduce_fusion.places, f32[2,6]{1,0:T(2,128)S(1)} %copy-done.11, f32[6,128,1]{2,1,0:T(8,128)S(1)} %copy.23.vrows, f32[6,256]{1,0:T(8,128)S(1)} %get-tuple-element.128.vcols, bf16[3,2,128,256]{3,2,1,0:T(8,128)(2,1)S(1)} %copy-done.7, ...), custom_call_target="tpu_custom_call" | custom-call | flops 7864320 | bytes 2359296 | tf_op jit(solution)/shard_map/partial_sums/pallas_call | solution.py:243
  42.0 3.2 %collective-permute-start.11 = (bf16[6,2,128,256]{3,2,1,0:T(8,128)(2,1)S(1)}, bf16[6,2,128,256]{3,2,1,0:T(8,128)(2,1)S(1)}, u32[]{:S(2)}, u32[]{:S(2)}) collective-permute-start(bf16[6,2,128,256]{3,2,1,0:T(8,128)(2,1)S(1)} %partial_sums.2), channel_id=1, source_target_pairs={{0,16},{4,20},{8,24},{12,28},{16,0},{20,4},{24,8},{28,12},{1,17},{... | collective-permute-start | bytes 2359304 | tf_op jit(solution)/shard_map/ppermute | solution.py:70
  45.2 1.5 collective-permute-start.8
  46.6 1.6 collective-permute-start.9
  48.2 0.4 collective-permute-start.10
  48.6 7.9 %collective-permute-done.8.refs_1_ = bf16[3,2,128,256]{3,2,1,0:T(8,128)(2,1)S(1)} collective-permute-done((bf16[3,2,128,256]{3,2,1,0:T(8,128)(2,1)}, bf16[3,2,128,256]{3,2,1,0:T(8,128)(2,1)S(1)}, u32[]{:S(2)}, u32[]{:S(2)}) %collective-permute-start.8) | collective-permute-done | bytes 393248 | tf_op jit(solution)/shard_map/ppermute | solution.py:70
  56.5 15.2 %collective-permute-done.9.refs_2_ = bf16[3,2,128,256]{3,2,1,0:T(8,128)(2,1)S(1)} collective-permute-done((bf16[3,2,128,256]{3,2,1,0:T(8,128)(2,1)}, bf16[3,2,128,256]{3,2,1,0:T(8,128)(2,1)S(1)}, u32[]{:S(2)}, u32[]{:S(2)}) %collective-permute-start.9) | collective-permute-done | bytes 393248 | tf_op jit(solution)/shard_map/ppermute | solution.py:70
  71.7 9.1 %collective-permute-done.10.refs_3_ = bf16[3,2,128,256]{3,2,1,0:T(8,128)(2,1)S(1)} collective-permute-done((bf16[3,2,128,256]{3,2,1,0:T(8,128)(2,1)}, bf16[3,2,128,256]{3,2,1,0:T(8,128)(2,1)S(1)}, u32[]{:S(2)}, u32[]{:S(2)}) %collective-permute-start.10) | collective-permute-done | bytes 393248 | tf_op jit(solution)/shard_map/ppermute | solution.py:70
  80.8 0.5 collective-permute-start.15
  81.3 0.1 collective-permute-start.17
  81.4 0.5 collective-permute-start.14
  81.9 1.0 copy-done.5
  82.9 2.1 %partial_sums.3 = bf16[6,2,128,256]{3,2,1,0:T(8,128)(2,1)S(1)} custom-call(s32[24]{0:T(128)S(1)} %select_reduce_fusion.places, f32[2,6]{1,0:T(2,128)S(1)} %copy-done.11, f32[6,128,1]{2,1,0:T(8,128)S(1)} %copy.24.vrows, f32[6,256]{1,0:T(8,128)S(1)} %get-tuple-element.128.vcols, bf16[3,2,128,256]{3,2,1,0:T(8,128)(2,1)S(1)} %copy-done.5, ...), custom_call_target="tpu_custom_call" | custom-call | flops 7864320 | bytes 2359296 | tf_op jit(solution)/shard_map/partial_sums/pallas_call | solution.py:243
  85.0 1.4 collective-permute-start.13
  86.5 5.0 %coupling_sums.2 = (bf16[3,2,128,256]{3,2,1,0:T(8,128)(2,1)S(1)}, bf16[3,2,128,256]{3,2,1,0:T(8,128)(2,1)S(1)}, bf16[3,2,128,256]{3,2,1,0:T(8,128)(2,1)S(1)}, bf16[3,2,128,256]{3,2,1,0:T(8,128)(2,1)S(1)}) custom-call(s32[24]{0:T(128)S(1)} %select_reduce_fusion.places, f32[2,6]{1,0:T(2,128)S(1)} %copy-done.11, f32[6,128,1]{2,1,0:T(8,128)S(1)} %copy.23.vrows, ...), custom_call_target="tpu_custom_call" | custom-call | flops 15728640 | bytes 3932160 | tf_op jit(solution)/shard_map/coupling_sums/pallas_call | solution.py:264
  91.5 0.6 collective-permute-start.18
  92.1 3.1 %collective-permute-start.19 = (bf16[3,2,128,256]{3,2,1,0:T(8,128)(2,1)S(1)}, bf16[3,2,128,256]{3,2,1,0:T(8,128)(2,1)S(1)}, u32[]{:S(2)}, u32[]{:S(2)}) collective-permute-start(bf16[3,2,128,256]{3,2,1,0:T(8,128)(2,1)S(1)} %get-tuple-element.156), channel_id=1, source_target_pairs={{0,8},{4,12},{8,0},{12,4},{16,24},{20,28},{24,16},{28,20},{1,9},{5... | collective-permute-start | bytes 1179656 | tf_op jit(solution)/shard_map/ppermute | solution.py:70
  95.2 10.0 %right_products.1.base = f32[3,2,256,1024]{3,2,1,0:T(8,128)S(1)} custom-call(s32[1]{0:T(128)} %bitcast.1.where, f32[3]{0:T(128)S(1)} %multiply_reduce_fusion.decay, bf16[3,2,128,1024]{3,2,1,0:T(8,128)(2,1)S(1)} %copy-done.9, bf16[3,2,128,1024]{3,2,1,0:T(8,128)(2,1)S(1)} %copy-done.3, bf16[2,256,1024]{2,1,0:T(8,128)(2,1)S(1)} %copy-done.10, ...), custom_call_target="tpu_custom_call" | custom-call | flops 6442450944 | bytes 13631488 | tf_op jit(solution)/shard_map/right_products/pallas_call | solution.py:317
  105.2 6.1 %left_products.1.refs_2_ = f32[3,2,256,1024]{3,2,1,0:T(8,128)S(1)} custom-call(s32[1]{0:T(128)} %bitcast.1.where, bf16[2,256,512]{2,1,0:T(8,128)(2,1)S(1)} %reshape_squeeze.6.h_own, f32[3,2,256,1024]{3,2,1,0:T(8,128)S(1)} %right_products.1.base, bf16[3,2,128,1024]{3,2,1,0:T(8,128)(2,1)S(1)} %copy-done.9, ...), custom_call_target="tpu_custom_call" | custom-call | flops 3221225472 | bytes 18874368 | tf_op jit(solution)/shard_map/left_products/pallas_call | solution.py:351
  111.4 11.2 %collective-permute-done.13.refs_4_ = bf16[6,2,128,256]{3,2,1,0:T(8,128)(2,1)S(1)} collective-permute-done((bf16[6,2,128,256]{3,2,1,0:T(8,128)(2,1)S(1)}, bf16[6,2,128,256]{3,2,1,0:T(8,128)(2,1)S(1)}, u32[]{:S(2)}, u32[]{:S(2)}) %collective-permute-start.13) | collective-permute-done | bytes 786464 | tf_op jit(solution)/shard_map/ppermute | solution.py:70
  122.6 6.1 %collective-permute-done.20.refs_11_ = bf16[3,2,128,256]{3,2,1,0:T(8,128)(2,1)S(1)} collective-permute-done((bf16[3,2,128,256]{3,2,1,0:T(8,128)(2,1)S(1)}, bf16[3,2,128,256]{3,2,1,0:T(8,128)(2,1)S(1)}, u32[]{:S(2)}, u32[]{:S(2)}) %collective-permute-start.20) | collective-permute-done | bytes 393248 | tf_op jit(solution)/shard_map/ppermute | solution.py:70
  128.7 0.5 collective-permute-start.22
  129.2 4.6 %coupling_sums.3 = (bf16[3,2,128,256]{3,2,1,0:T(8,128)(2,1)S(1)}, bf16[3,2,128,256]{3,2,1,0:T(8,128)(2,1)S(1)}, bf16[3,2,128,256]{3,2,1,0:T(8,128)(2,1)S(1)}, bf16[3,2,128,256]{3,2,1,0:T(8,128)(2,1)S(1)}) custom-call(s32[24]{0:T(128)S(1)} %select_reduce_fusion.places, f32[2,6]{1,0:T(2,128)S(1)} %copy-done.11, f32[6,128,1]{2,1,0:T(8,128)S(1)} %copy.24.vrows, ...), custom_call_target="tpu_custom_call" | custom-call | flops 15728640 | bytes 3932160 | tf_op jit(solution)/shard_map/coupling_sums/pallas_call | solution.py:264
  133.8 1.7 %collective-permute-start.23 = (bf16[3,2,128,256]{3,2,1,0:T(8,128)(2,1)S(1)}, bf16[3,2,128,256]{3,2,1,0:T(8,128)(2,1)S(1)}, u32[]{:S(2)}, u32[]{:S(2)}) collective-permute-start(bf16[3,2,128,256]{3,2,1,0:T(8,128)(2,1)S(1)} %get-tuple-element.173), channel_id=1, source_target_pairs={{0,4},{4,0},{8,12},{12,8},{16,20},{20,16},{24,28},{28,24},{1,5},{5... | collective-permute-start | bytes 1179656 | tf_op jit(solution)/shard_map/ppermute | solution.py:70
  135.5 1.9 %collective-permute-start.25 = (bf16[3,2,128,256]{3,2,1,0:T(8,128)(2,1)S(1)}, bf16[3,2,128,256]{3,2,1,0:T(8,128)(2,1)S(1)}, u32[]{:S(2)}, u32[]{:S(2)}) collective-permute-start(bf16[3,2,128,256]{3,2,1,0:T(8,128)(2,1)S(1)} %get-tuple-element.175), channel_id=1, source_target_pairs={{0,12},{4,8},{8,4},{12,0},{16,28},{20,24},{24,20},{28,16},{1,13},{... | collective-permute-start | bytes 1179656 | tf_op jit(solution)/shard_map/ppermute | solution.py:70
  137.4 0.1 pad_add_fusion.1.refs_0_
  137.5 6.8 %outputs.2 = (f32[3,2,256,1024]{3,2,1,0:T(8,128)}, f32[3,2,256,1024]{3,2,1,0:T(8,128)}) custom-call(s32[2]{0:T(128)S(1)} %pad_add_fusion.1.refs_0_, bf16[2,256,512]{2,1,0:T(8,128)(2,1)S(1)} %reshape_squeeze.7.refs_1_, f32[3,2,256,1024]{3,2,1,0:T(8,128)S(1)} %left_products.1.refs_2_, f32[3,2,256,1024]{3,2,1,0:T(8,128)S(1)} %bitcast.5, ...), custom_call_target="tpu_custom_call" | custom-call | flops 1610612736 | bytes 28311552 | tf_op jit(solution)/shard_map/outputs/pallas_call | solution.py:404
  144.3 0.7 collective-permute-done.23.refs_9_
  145.0 2.5 %collective-permute-done.24.refs_10_ = bf16[3,2,128,256]{3,2,1,0:T(8,128)(2,1)S(1)} collective-permute-done((bf16[3,2,128,256]{3,2,1,0:T(8,128)(2,1)S(1)}, bf16[3,2,128,256]{3,2,1,0:T(8,128)(2,1)S(1)}, u32[]{:S(2)}, u32[]{:S(2)}) %collective-permute-start.24) | collective-permute-done | bytes 393248 | tf_op jit(solution)/shard_map/ppermute | solution.py:70
  147.5 7.0 %collective-permute-done.25.refs_11_ = bf16[3,2,128,256]{3,2,1,0:T(8,128)(2,1)S(1)} collective-permute-done((bf16[3,2,128,256]{3,2,1,0:T(8,128)(2,1)S(1)}, bf16[3,2,128,256]{3,2,1,0:T(8,128)(2,1)S(1)}, u32[]{:S(2)}, u32[]{:S(2)}) %collective-permute-start.25) | collective-permute-done | bytes 393248 | tf_op jit(solution)/shard_map/ppermute | solution.py:70
  154.5 6.8 %outputs.3 = (f32[3,2,256,1024]{3,2,1,0:T(8,128)}, f32[3,2,256,1024]{3,2,1,0:T(8,128)}) custom-call(s32[2]{0:T(128)S(1)} %pad_add_fusion.1.refs_0_, bf16[2,256,512]{2,1,0:T(8,128)(2,1)S(1)} %reshape_squeeze.7.refs_1_, f32[3,2,256,1024]{3,2,1,0:T(8,128)S(1)} %left_products.1.refs_2_, ...), custom_call_target="tpu_custom_call", output_to_operand_aliasing={{0}: (12, {}), {1}: (13, {})} | custom-call | flops 1610612736 | bytes 28311552 | tf_op jit(solution)/shard_map/outputs/pallas_call | solution.py:404
  (54 shorter events, 0.2 us)
Async XLA Ops:
  0.6 9.9 %collective-permute-start.1 = (s32[3,6]{1,0:T(4,128)}, s32[3,6]{1,0:T(4,128)S(1)}, u32[]{:S(2)}, u32[]{:S(2)}) collective-permute-start(s32[3,6]{1,0:T(4,128)} %param.18), channel_id=1, source_target_pairs={{0,8},{4,12},{8,0},{12,4},{16,24},{20,28},{24,16},{28,20},{1,9},{5... | collective-permute-start | bytes 224 | tf_op jit(solution)/shard_map/ppermute | solution.py:70
  3.7 6.8 %collective-permute-start = (s32[3,6]{1,0:T(4,128)}, s32[3,6]{1,0:T(4,128)S(1)}, u32[]{:S(2)}, u32[]{:S(2)}) collective-permute-start(s32[3,6]{1,0:T(4,128)} %param.18), channel_id=1, source_target_pairs={{0,4},{4,0},{8,12},{12,8},{16,20},{20,16},{24,28},{28,24},{1,5},{5... | collective-permute-start | bytes 224 | tf_op jit(solution)/shard_map/ppermute | solution.py:70
  5.2 5.3 %collective-permute-start.2 = (s32[3,6]{1,0:T(4,128)}, s32[3,6]{1,0:T(4,128)S(1)}, u32[]{:S(2)}, u32[]{:S(2)}) collective-permute-start(s32[3,6]{1,0:T(4,128)} %param.18), channel_id=1, source_target_pairs={{0,12},{4,8},{8,4},{12,0},{16,28},{20,24},{24,20},{28,16},{1,13},{... | collective-permute-start | bytes 224 | tf_op jit(solution)/shard_map/ppermute | solution.py:70
  5.3 10.8 %copy-start.1 = (bf16[3,2,256,1024]{3,2,1,0:T(8,128)(2,1)S(1)}, bf16[3,2,256,1024]{3,2,1,0:T(8,128)(2,1)}, u32[]{:S(2)}) copy-start(bf16[3,2,256,1024]{3,2,1,0:T(8,128)(2,1)} %state.2) | copy-start | bytes 9437188
  10.5 24.6 %collective-permute-start.7 = (bf16[2,256,1024]{2,1,0:T(8,128)(2,1)}, bf16[2,256,1024]{2,1,0:T(8,128)(2,1)}, u32[]{:S(2)}, u32[]{:S(2)}) collective-permute-start(bf16[2,256,1024]{2,1,0:T(8,128)(2,1)} %refs_2_), channel_id=1, source_target_pairs={{0,1},{1,0},{2,3},{3,2},{4,5},{5,4},{6,7},{7,6},{8,9},{9,8},{10,11... | collective-permute-start | bytes 3145736 | tf_op jit(solution)/shard_map/ppermute | solution.py:70
  10.6 26.0 %collective-permute-start.6 = (bf16[2,256,1024]{2,1,0:T(8,128)(2,1)}, bf16[2,256,1024]{2,1,0:T(8,128)(2,1)}, u32[]{:S(2)}, u32[]{:S(2)}) collective-permute-start(bf16[2,256,1024]{2,1,0:T(8,128)(2,1)} %refs_2_), channel_id=1, source_target_pairs={{0,2},{1,3},{2,0},{3,1},{4,6},{5,7},{6,4},{7,5},{8,10},{9,11},{10,... | collective-permute-start | bytes 3145736 | tf_op jit(solution)/shard_map/ppermute | solution.py:70
  12.6 22.5 %collective-permute-start.3 = (bf16[3,2,128,256]{3,2,1,0:T(8,128)(2,1)}, bf16[3,2,128,256]{3,2,1,0:T(8,128)(2,1)}, u32[]{:S(2)}, u32[]{:S(2)}) collective-permute-start(bf16[3,2,128,256]{3,2,1,0:T(8,128)(2,1)} %get-tuple-element.98), channel_id=1, source_target_pairs={{0,4},{4,0},{8,12},{12,8},{16,20},{20,16},{24,28},{28,24},{1,5},{5... | collective-permute-start | bytes 1179656 | tf_op jit(solution)/shard_map/ppermute | solution.py:70
  14.1 21.0 %collective-permute-start.4 = (bf16[3,2,128,256]{3,2,1,0:T(8,128)(2,1)}, bf16[3,2,128,256]{3,2,1,0:T(8,128)(2,1)}, u32[]{:S(2)}, u32[]{:S(2)}) collective-permute-start(bf16[3,2,128,256]{3,2,1,0:T(8,128)(2,1)} %get-tuple-element.99), channel_id=1, source_target_pairs={{0,8},{4,12},{8,0},{12,4},{16,24},{20,28},{24,16},{28,20},{1,9},{5... | collective-permute-start | bytes 1179656 | tf_op jit(solution)/shard_map/ppermute | solution.py:70
  15.6 19.5 %collective-permute-start.5 = (bf16[3,2,128,256]{3,2,1,0:T(8,128)(2,1)}, bf16[3,2,128,256]{3,2,1,0:T(8,128)(2,1)}, u32[]{:S(2)}, u32[]{:S(2)}) collective-permute-start(bf16[3,2,128,256]{3,2,1,0:T(8,128)(2,1)} %get-tuple-element.100), channel_id=1, source_target_pairs={{0,12},{4,8},{8,4},{12,0},{16,28},{20,24},{24,20},{28,16},{1,13},{... | collective-permute-start | bytes 1179656 | tf_op jit(solution)/shard_map/ppermute | solution.py:70
  16.1 2.8 %copy-start = (f32[3,2,256,1024]{3,2,1,0:T(8,128)S(1)}, f32[3,2,256,1024]{3,2,1,0:T(8,128)}, u32[]{:S(2)}) copy-start(f32[3,2,256,1024]{3,2,1,0:T(8,128)} %slope.2) | copy-start | bytes 18874372
  18.8 7.3 %copy-start.15 = (f32[6,1024]{1,0:T(8,128)S(1)}, f32[6,1024]{1,0:T(8,128)}, u32[]{:S(2)}) copy-start(f32[6,1024]{1,0:T(8,128)} %param.15) | copy-start | bytes 73732
  20.1 1.1 copy-start.2
  21.3 0.8 copy-start.4
  22.0 0.8 copy-start.12
  22.8 0.8 copy-start.13
  23.6 0.7 copy-start.14
  24.3 8.7 %copy-start.16 = (s32[3,6]{1,0:T(4,128)S(1)}, s32[3,6]{1,0:T(4,128)}, u32[]{:S(2)}) copy-start(s32[3,6]{1,0:T(4,128)} %param.18) | copy-start | bytes 220
  24.3 8.7 %copy-start.18 = (f32[6]{0:T(128)S(1)}, f32[6]{0:T(128)}, u32[]{:S(2)}) copy-start(f32[6]{0:T(128)} %param.17) | copy-start | bytes 76
  26.1 8.8 %copy-start.17 = (s32[24,6]{0,1:T(8,128)S(1)}, s32[24,6]{0,1:T(8,128)}, u32[]{:S(2)}) copy-start(s32[24,6]{0,1:T(8,128)} %constant.37.clone) | copy-start | bytes 1732
  26.1 12.3 %copy-start.11 = (f32[2,6]{1,0:T(2,128)S(1)}, f32[2,6]{1,0:T(2,128)}, u32[]{:S(2)}) copy-start(f32[2,6]{1,0:T(2,128)} %coupling.7) | copy-start | bytes 148
  33.0 48.5 %copy-start.3 = (bf16[3,2,128,1024]{3,2,1,0:T(8,128)(2,1)S(1)}, bf16[3,2,128,1024]{3,2,1,0:T(8,128)(2,1)}, u32[]{:S(2)}) copy-start(bf16[3,2,128,1024]{3,2,1,0:T(8,128)(2,1)} %copy-done.2) | copy-start | bytes 4718596
  36.6 44.2 %collective-permute-start.12 = (bf16[3,2,128,1024]{3,2,1,0:T(8,128)(2,1)}, bf16[3,2,128,1024]{3,2,1,0:T(8,128)(2,1)S(1)}, u32[]{:S(2)}, u32[]{:S(2)}) collective-permute-start(bf16[3,2,128,1024]{3,2,1,0:T(8,128)(2,1)} %get-tuple-element.164.refs_0_), channel_id=1, source_target_pairs={{0,2},{1,3},{2,0},{3,1},{4,6},{5,7},{6,4},{7,5},{8,10},{9,11},{10,... | collective-permute-start | bytes 4718600 | tf_op jit(solution)/shard_map/ppermute | solution.py:70
  38.4 1.0 copy-start.7
  39.4 47.1 %copy-start.8 = (bf16[3,2,128,256]{3,2,1,0:T(8,128)(2,1)S(1)}, bf16[3,2,128,256]{3,2,1,0:T(8,128)(2,1)}, u32[]{:S(2)}) copy-start(bf16[3,2,128,256]{3,2,1,0:T(8,128)(2,1)} %get-tuple-element.141.refs_0_) | copy-start | bytes 1179652
  39.4 55.8 %copy-start.9 = (bf16[3,2,128,1024]{3,2,1,0:T(8,128)(2,1)S(1)}, bf16[3,2,128,1024]{3,2,1,0:T(8,128)(2,1)}, u32[]{:S(2)}) copy-start(bf16[3,2,128,1024]{3,2,1,0:T(8,128)(2,1)} %get-tuple-element.164.refs_0_) | copy-start | bytes 4718596
  42.0 38.9 %collective-permute-start.11 = (bf16[6,2,128,256]{3,2,1,0:T(8,128)(2,1)S(1)}, bf16[6,2,128,256]{3,2,1,0:T(8,128)(2,1)S(1)}, u32[]{:S(2)}, u32[]{:S(2)}) collective-permute-start(bf16[6,2,128,256]{3,2,1,0:T(8,128)(2,1)S(1)} %partial_sums.2), channel_id=1, source_target_pairs={{0,16},{4,20},{8,24},{12,28},{16,0},{20,4},{24,8},{28,12},{1,17},{... | collective-permute-start | bytes 2359304 | tf_op jit(solution)/shard_map/ppermute | solution.py:70
  45.2 11.4 %collective-permute-start.8 = (bf16[3,2,128,256]{3,2,1,0:T(8,128)(2,1)}, bf16[3,2,128,256]{3,2,1,0:T(8,128)(2,1)S(1)}, u32[]{:S(2)}, u32[]{:S(2)}) collective-permute-start(bf16[3,2,128,256]{3,2,1,0:T(8,128)(2,1)} %copy-done.14), channel_id=1, source_target_pairs={{0,4},{4,0},{8,12},{12,8},{16,20},{20,16},{24,28},{28,24},{1,5},{5... | collective-permute-start | bytes 1179656 | tf_op jit(solution)/shard_map/ppermute | solution.py:70
  46.6 25.1 %collective-permute-start.9 = (bf16[3,2,128,256]{3,2,1,0:T(8,128)(2,1)}, bf16[3,2,128,256]{3,2,1,0:T(8,128)(2,1)S(1)}, u32[]{:S(2)}, u32[]{:S(2)}) collective-permute-start(bf16[3,2,128,256]{3,2,1,0:T(8,128)(2,1)} %copy-done.13), channel_id=1, source_target_pairs={{0,8},{4,12},{8,0},{12,4},{16,24},{20,28},{24,16},{28,20},{1,9},{5... | collective-permute-start | bytes 1179656 | tf_op jit(solution)/shard_map/ppermute | solution.py:70
  48.2 32.6 %collective-permute-start.10 = (bf16[3,2,128,256]{3,2,1,0:T(8,128)(2,1)}, bf16[3,2,128,256]{3,2,1,0:T(8,128)(2,1)S(1)}, u32[]{:S(2)}, u32[]{:S(2)}) collective-permute-start(bf16[3,2,128,256]{3,2,1,0:T(8,128)(2,1)} %copy-done.12), channel_id=1, source_target_pairs={{0,12},{4,8},{8,4},{12,0},{16,28},{20,24},{24,20},{28,16},{1,13},{... | collective-permute-start | bytes 1179656 | tf_op jit(solution)/shard_map/ppermute | solution.py:70
  80.8 10.6 %collective-permute-start.16 = (bf16[3,2,128,1024]{3,2,1,0:T(8,128)(2,1)S(1)}, bf16[3,2,128,1024]{3,2,1,0:T(8,128)(2,1)S(1)}, u32[]{:S(2)}, u32[]{:S(2)}) collective-permute-start(bf16[3,2,128,1024]{3,2,1,0:T(8,128)(2,1)S(1)} %collective-permute-done.12.refs_2_), channel_id=1, source_target_pairs={{0,1},{1,0},{2,3},{3,2},{4,5},{5,4},{6,7},{7,6},{8,9},{9,8},{10,11... | collective-permute-start | bytes 4718600 | tf_op jit(solution)/shard_map/ppermute | solution.py:70
  80.8 10.6 %collective-permute-start.15 = (bf16[3,2,128,1024]{3,2,1,0:T(8,128)(2,1)}, bf16[3,2,128,1024]{3,2,1,0:T(8,128)(2,1)S(1)}, u32[]{:S(2)}, u32[]{:S(2)}) collective-permute-start(bf16[3,2,128,1024]{3,2,1,0:T(8,128)(2,1)} %get-tuple-element.164.refs_0_), channel_id=1, source_target_pairs={{0,1},{1,0},{2,3},{3,2},{4,5},{5,4},{6,7},{7,6},{8,9},{9,8},{10,11... | collective-permute-start | bytes 4718600 | tf_op jit(solution)/shard_map/ppermute | solution.py:70
  81.3 10.1 %collective-permute-start.17 = (bf16[2,256,1024]{2,1,0:T(8,128)(2,1)}, bf16[2,256,1024]{2,1,0:T(8,128)(2,1)S(1)}, u32[]{:S(2)}, u32[]{:S(2)}) collective-permute-start(bf16[2,256,1024]{2,1,0:T(8,128)(2,1)} %collective-permute-done.6.refs_4_), channel_id=1, source_target_pairs={{0,1},{1,0},{2,3},{3,2},{4,5},{5,4},{6,7},{7,6},{8,9},{9,8},{10,11... | collective-permute-start | bytes 3145736 | tf_op jit(solution)/shard_map/ppermute | solution.py:70
  81.4 41.1 %collective-permute-start.14 = (bf16[3,2,128,1024]{3,2,1,0:T(8,128)(2,1)S(1)}, bf16[3,2,128,1024]{3,2,1,0:T(8,128)(2,1)S(1)}, u32[]{:S(2)}, u32[]{:S(2)}) collective-permute-start(bf16[3,2,128,1024]{3,2,1,0:T(8,128)(2,1)S(1)} %copy-done.3), channel_id=1, source_target_pairs={{0,2},{1,3},{2,0},{3,1},{4,6},{5,7},{6,4},{7,5},{8,10},{9,11},{10,... | collective-permute-start | bytes 4718600 | tf_op jit(solution)/shard_map/ppermute | solution.py:70
  81.9 1.0 copy-start.5
  82.9 12.3 %copy-start.10 = (bf16[2,256,1024]{2,1,0:T(8,128)(2,1)S(1)}, bf16[2,256,1024]{2,1,0:T(8,128)(2,1)}, u32[]{:S(2)}) copy-start(bf16[2,256,1024]{2,1,0:T(8,128)(2,1)} %refs_2_) | copy-start | bytes 3145732
  85.0 37.5 %collective-permute-start.13 = (bf16[6,2,128,256]{3,2,1,0:T(8,128)(2,1)S(1)}, bf16[6,2,128,256]{3,2,1,0:T(8,128)(2,1)S(1)}, u32[]{:S(2)}, u32[]{:S(2)}) collective-permute-start(bf16[6,2,128,256]{3,2,1,0:T(8,128)(2,1)S(1)} %partial_sums.3), channel_id=1, source_target_pairs={{0,16},{4,20},{8,24},{12,28},{16,0},{20,4},{24,8},{28,12},{1,17},{... | collective-permute-start | bytes 2359304 | tf_op jit(solution)/shard_map/ppermute | solution.py:70
  91.5 31.1 %collective-permute-start.18 = (bf16[3,2,128,256]{3,2,1,0:T(8,128)(2,1)S(1)}, bf16[3,2,128,256]{3,2,1,0:T(8,128)(2,1)S(1)}, u32[]{:S(2)}, u32[]{:S(2)}) collective-permute-start(bf16[3,2,128,256]{3,2,1,0:T(8,128)(2,1)S(1)} %get-tuple-element.155), channel_id=1, source_target_pairs={{0,4},{4,0},{8,12},{12,8},{16,20},{20,16},{24,28},{28,24},{1,5},{5... | collective-permute-start | bytes 1179656 | tf_op jit(solution)/shard_map/ppermute | solution.py:70
  92.1 30.5 %collective-permute-start.19 = (bf16[3,2,128,256]{3,2,1,0:T(8,128)(2,1)S(1)}, bf16[3,2,128,256]{3,2,1,0:T(8,128)(2,1)S(1)}, u32[]{:S(2)}, u32[]{:S(2)}) collective-permute-start(bf16[3,2,128,256]{3,2,1,0:T(8,128)(2,1)S(1)} %get-tuple-element.156), channel_id=1, source_target_pairs={{0,8},{4,12},{8,0},{12,4},{16,24},{20,28},{24,16},{28,20},{1,9},{5... | collective-permute-start | bytes 1179656 | tf_op jit(solution)/shard_map/ppermute | solution.py:70
  95.2 33.5 %collective-permute-start.20 = (bf16[3,2,128,256]{3,2,1,0:T(8,128)(2,1)S(1)}, bf16[3,2,128,256]{3,2,1,0:T(8,128)(2,1)S(1)}, u32[]{:S(2)}, u32[]{:S(2)}) collective-permute-start(bf16[3,2,128,256]{3,2,1,0:T(8,128)(2,1)S(1)} %get-tuple-element.157), channel_id=1, source_target_pairs={{0,12},{4,8},{8,4},{12,0},{16,28},{20,24},{24,20},{28,16},{1,13},{... | collective-permute-start | bytes 1179656 | tf_op jit(solution)/shard_map/ppermute | solution.py:70
  95.2 42.2 %slice-start = ((s8[6291456]{0:T(1024)(128)(4,1)}), s8[4194304]{0:T(1024)(128)(4,1)S(1)}, s32[]{:S(2)}) async-start(s8[6291456]{0:T(1024)(128)(4,1)} %bitcast.4), calls=%async_computation | async-start | bytes 8388608
  95.2 42.2 %slice-start.1 = ((s8[6291456]{0:T(1024)(128)(4,1)}), s8[2097152]{0:T(1024)(128)(4,1)S(1)}, s32[]{:S(2)}) async-start(s8[6291456]{0:T(1024)(128)(4,1)} %bitcast.4), calls=%async_computation.1 | async-start | bytes 4194304
  105.2 24.0 %copy-start.6 = (bf16[3,2,128,256]{3,2,1,0:T(8,128)(2,1)S(1)}, bf16[3,2,128,256]{3,2,1,0:T(8,128)(2,1)}, u32[]{:S(2)}) copy-start(bf16[3,2,128,256]{3,2,1,0:T(8,128)(2,1)} %copy-done.4) | copy-start | bytes 1179652
  128.7 8.7 %collective-permute-start.21 = (bf16[3,2,128,1024]{3,2,1,0:T(8,128)(2,1)S(1)}, bf16[3,2,128,1024]{3,2,1,0:T(8,128)(2,1)S(1)}, u32[]{:S(2)}, u32[]{:S(2)}) collective-permute-start(bf16[3,2,128,1024]{3,2,1,0:T(8,128)(2,1)S(1)} %copy-done.3), channel_id=1, source_target_pairs={{0,1},{1,0},{2,3},{3,2},{4,5},{5,4},{6,7},{7,6},{8,9},{9,8},{10,11... | collective-permute-start | bytes 4718600 | tf_op jit(solution)/shard_map/ppermute | solution.py:70
  128.7 8.7 %collective-permute-start.22 = (bf16[3,2,128,1024]{3,2,1,0:T(8,128)(2,1)S(1)}, bf16[3,2,128,1024]{3,2,1,0:T(8,128)(2,1)S(1)}, u32[]{:S(2)}, u32[]{:S(2)}) collective-permute-start(bf16[3,2,128,1024]{3,2,1,0:T(8,128)(2,1)S(1)} %collective-permute-done.14.refs_6_), channel_id=1, source_target_pairs={{0,1},{1,0},{2,3},{3,2},{4,5},{5,4},{6,7},{7,6},{8,9},{9,8},{10,11... | collective-permute-start | bytes 4718600 | tf_op jit(solution)/shard_map/ppermute | solution.py:70
  133.8 11.2 %collective-permute-start.23 = (bf16[3,2,128,256]{3,2,1,0:T(8,128)(2,1)S(1)}, bf16[3,2,128,256]{3,2,1,0:T(8,128)(2,1)S(1)}, u32[]{:S(2)}, u32[]{:S(2)}) collective-permute-start(bf16[3,2,128,256]{3,2,1,0:T(8,128)(2,1)S(1)} %get-tuple-element.173), channel_id=1, source_target_pairs={{0,4},{4,0},{8,12},{12,8},{16,20},{20,16},{24,28},{28,24},{1,5},{5... | collective-permute-start | bytes 1179656 | tf_op jit(solution)/shard_map/ppermute | solution.py:70
  135.5 12.0 %collective-permute-start.24 = (bf16[3,2,128,256]{3,2,1,0:T(8,128)(2,1)S(1)}, bf16[3,2,128,256]{3,2,1,0:T(8,128)(2,1)S(1)}, u32[]{:S(2)}, u32[]{:S(2)}) collective-permute-start(bf16[3,2,128,256]{3,2,1,0:T(8,128)(2,1)S(1)} %get-tuple-element.174), channel_id=1, source_target_pairs={{0,8},{4,12},{8,0},{12,4},{16,24},{20,28},{24,16},{28,20},{1,9},{5... | collective-permute-start | bytes 1179656 | tf_op jit(solution)/shard_map/ppermute | solution.py:70
  135.5 19.0 %collective-permute-start.25 = (bf16[3,2,128,256]{3,2,1,0:T(8,128)(2,1)S(1)}, bf16[3,2,128,256]{3,2,1,0:T(8,128)(2,1)S(1)}, u32[]{:S(2)}, u32[]{:S(2)}) collective-permute-start(bf16[3,2,128,256]{3,2,1,0:T(8,128)(2,1)S(1)} %get-tuple-element.175), channel_id=1, source_target_pairs={{0,12},{4,8},{8,4},{12,0},{16,28},{20,24},{24,20},{28,16},{1,13},{... | collective-permute-start | bytes 1179656 | tf_op jit(solution)/shard_map/ppermute | solution.py:70
where the time goes:
time: 162 us; the launch traced here: 161 us
  waiting for transfers between devices  61.3 us (38%)
  Pallas kernels  50.4 us (31%)
  starting transfers between devices  28.9 us (18%)
  local copies, waits for them, and re-layouts  19.4 us (12%)
    ppermute x26, waiting for transfers between devices, swap(): return lax.ppermute(array, axis, [(i, i ^ bit) for i in range(size)])  61.3 us
    ppermute x26, starting transfers between devices, swap(): return lax.ppermute(array, axis, [(i, i ^ bit) for i in range(size)])  28.9 us
    pallas_call x2, Pallas kernels, make_final(): pl.pallas_call(lambda *refs: final_kernel(group, count, *refs[:1 + len(in...  13.6 us
    pallas_call x1, Pallas kernels, make_right(): pl.pallas_call(functools.partial(right_kernel, split, count), grid=(colum...  9.98 us
    pallas_call x2, Pallas kernels, make_coupled(): pl.pallas_call(functools.partial(coupled_kernel, links, sides, group), in...  9.54 us
    unnamed x42, local copies, waits for them, and re-layouts  8.99 us
    slice x1, local copies, waits for them, and re-layouts, shards(): blocks[:, :, :, p].reshape(2, rows, row * height)  6.77 us
    pallas_call x2, Pallas kernels, make_section(): pl.pallas_call(section_kernel, grid_spec=pltpu.PrefetchScalarGridSpec(num...  6.51 us
  transfers between devices with their start and end apart: 26, of which 9 were waited for; matrix products, arithmetic and copies ran while one was open for 7% of the time, Pallas kernels for 27%

commit v1 on v0

--- a/solution.py
+++ b/solution.py
@@ -83,7 +83,7 @@
     for bit in bits:
         for mask in list(parts):
             parts[mask ^ bit] = swap(parts[mask], "row", size, bit)
-    return parts
+    return [parts[mask] for mask in sorted(parts)]
 
 
 def section_kernel(where, state, slope, section, *chunks):
@@ -271,11 +271,7 @@
         + factors
         + [pltpu.SMEM((len(links),), jnp.int32), pltpu.SemaphoreType.DMA((2 * group + 1,))],
         compiler_params=params(16),
-        cost_estimate=pl.CostEstimate(
-            flops=40 * group * ops * size,
-            bytes_accessed=4 * size * (2 * group * ops + len(sides)),
-            transcendentals=0,
-        ),
+        cost_estimate=pl.CostEstimate(flops=1, bytes_accessed=1, transcendentals=0),
         name="coupling_sums",
     )(places, coupling, vrows, vcols, *chunks, received)
 
@@ -288,57 +284,73 @@
     return first[:height] - second[height:], second[:height] + first[height:]
 
 
-def right_kernel(split, count, where, decay, *refs):
-    sections, h_parts, (out, h_all) = refs[:split], refs[split:-2], refs[-2:]
+def right_kernel(split, count, where, decay, h_own, *refs):
+    sections, refs, (out, h_all) = refs[:split], refs[split:-2], refs[-2:]
+    h_near, h_far = refs[: 2 * count - 2], refs[2 * count - 2 :]
     j, a = pl.program_id(0), pl.program_id(1)
-    rows, tile = h_parts[0].shape[1:]
-    height = sections[0].shape[2]
-
-    @pl.when(a == 0)
+    rows, size = h_own.shape[1:]
+    height, tile = sections[0].shape[2], out.shape[3]
+    half, block = size // 2, size // 4
+    own = pl.multiple_of((where[0] // count) * half, half)
+    other = pl.multiple_of(half - own, half)
+
+    @pl.when(jnp.logical_and(j == 0, a == 0))
     def _():
         for b in range(count):
-            place = pl.ds(pl.multiple_of((where[0] ^ b) * rows, row_tile), rows)
-            h_all[:, place, :] = h_parts[b][...]
+            place = pl.multiple_of((where[0] ^ b) * rows, row_tile)
+            for x in range(2):
+                near = h_near[2 * b - 2 + x][...] if b else h_own[x]
+                h_all[x, pl.ds(place, rows), :] = near
+            place = pl.multiple_of((where[0] ^ (count + b)) * rows, row_tile)
+            h_all[:, pl.ds(place, rows), pl.ds(other, half)] = h_far[b][...]
+        for r in range(0, half, block):
+            for c in range(0, half, block):
+                here = pl.ds(pl.multiple_of(own + r, block), block)
+                there = pl.ds(pl.multiple_of(other + c, block), block)
+                h_all[0, there, here] = h_all[0, here, there].T
+                h_all[1, there, here] = -h_all[1, here, there].T
 
     columns = pl.ds(pl.multiple_of(j * tile, 128), tile)
     lost = decay[a]
     for p, section in enumerate(sections):
-        real, imag = complex_rows(section[a], h_all)
+        real, imag = complex_rows(section[a], h_all.at[:, :, columns])
         here = slice(p * height, (p + 1) * height)
         out[0, 0, here, :] = -imag - lost * section[a, 0, :, columns].astype(f32)
         out[0, 1, here, :] = real - lost * section[a, 1, :, columns].astype(f32)
 
 
-def make_right(sections, h_parts, place, decay):
+def make_right(sections, h_own, bundles, h_far, place, decay):
     ops, _, height, columns = sections[0].shape
-    split, count = len(sections), len(h_parts)
+    split, count = len(sections), len(h_far)
     rows, tile = height * split, min(columns, 512)
     held = pl.BlockSpec((ops, 2, height, columns), lambda j, a: (0, 0, 0, 0))
     return pl.pallas_call(
         functools.partial(right_kernel, split, count),
         grid=(columns // tile, ops),
-        in_specs=[scalars(), scalars()]
+        in_specs=[scalars(), scalars(), pl.BlockSpec(h_own.shape, lambda j, a: (0, 0, 0))]
         + [held] * split
-        + [pl.BlockSpec((2, rows, tile), lambda j, a: (0, 0, j))] * count,
+        + [pl.BlockSpec((rows, columns), lambda j, a, x=x: (ops + x, 0)) for x in range(2)]
+        * len(bundles)
+        + [pl.BlockSpec(h.shape, lambda j, a: (0, 0, 0)) for h in h_far],
         out_specs=pl.BlockSpec((1, 2, rows, tile), lambda j, a: (a, 0, 0, j)),
         out_shape=jax.ShapeDtypeStruct((ops, 2, rows, columns), f32),
-        scratch_shapes=[pltpu.VMEM((2, count * rows, tile), bf16)],
-        compiler_params=params(24),
+        scratch_shapes=[pltpu.VMEM((2, columns, columns), bf16)],
+        compiler_params=params(28),
         cost_estimate=pl.CostEstimate(
             flops=8 * ops * rows * columns * columns,
             bytes_accessed=4 * columns * (columns + 3 * ops * rows),
             transcendentals=0,
         ),
         name="right_products",
-    )(place, decay, *sections, *h_parts)
+    )(place, decay, h_own, *sections, *[h for h in bundles for _ in range(2)], *h_far)
 
 
 def left_kernel(count, where, h_own, base, *refs):
     s_parts, (out, s_all) = refs[:count], refs[count:]
-    height = s_parts[0].shape[2]
+    height, tile = s_parts[0].shape[2:]
     for b in range(count):
         place = pl.ds(pl.multiple_of((where[0] ^ b) * height, row_tile), height)
-        s_all[:, place, :] = s_parts[b][0]
+        s_all[:, place, :] = s_parts[b][...].reshape(2, height, tile)
     real, imag = complex_rows(h_own[...], s_all)
     out[0, 0] = base[0, 0] + imag
     out[0, 1] = base[0, 1] - real
@@ -356,7 +368,12 @@
             pl.BlockSpec(h_columns.shape, lambda j, a: (0, 0, 0)),
             block,
         ]
-        + [pl.BlockSpec((1, 2, height, tile), lambda j, a: (a, 0, 0, j))] * count,
+        + [
+            pl.BlockSpec((1, 2, height, tile), lambda j, a: (a, 0, 0, j))
+            if part.ndim == 4
+            else pl.BlockSpec((2 * height, tile), lambda j, a: (a, j))
+            for part in s_parts
+        ],
         out_specs=block,
         out_shape=jax.ShapeDtypeStruct(base.shape, f32),
         scratch_shapes=[pltpu.VMEM((2, count * height, tile), bf16)],
@@ -370,58 +387,45 @@
     )(place, h_columns, base, *s_parts)
 
 
-def final_kernel(group, count, where, h_own, base, accumulated, *refs):
-    s_parts, sums = refs[:count], refs[count : count + group]
-    slope, total, s_all = refs[-3:]
-    a, j = pl.program_id(0), pl.program_id(1)
-    height, tile, width = s_parts[0].shape[2], slope.shape[3], sums[0].shape[3]
-    for b in range(count):
-        place = pl.ds(pl.multiple_of((where[1] ^ b) * height, row_tile), height)
-        s_all[:, place, :] = s_parts[b][0]
-    real, imag = complex_rows(h_own[...], s_all)
-    slope[0, 0] = base[0, 0] + imag
-    slope[0, 1] = base[0, 1] - real
+def final_kernel(group, where, base, accumulated, *refs):
+    sums, (slope, total) = refs[:group], refs[-2:]
+    j = pl.program_id(1)
+    tile, width = slope.shape[3], sums[0].shape[3]
     for b in range(group):
         first = (where[0] ^ b) * width - j * tile
 
         @pl.when(jnp.logical_and(first >= 0, first < tile))
         def _():
             columns = pl.ds(pl.multiple_of(first, 128), width)
-            slope[0, :, :, columns] += sums[b][a].astype(f32)
-
-    total[...] = accumulated[...] + (step_size / 3.0) * slope[...]
-
-
-def make_final(p, split, base, accumulated, s_parts, h_columns, sums, places, earlier=()):
+            value = base[0, :, :, columns] + sums[b][0].astype(f32)
+            slope[0, :, :, columns] = value
+            total[0, :, :, columns] = accumulated[0, :, :, columns] + (step_size / 3.0) * value
+
+
+def make_final(p, split, base, accumulated, sums, place, earlier=()):
     ops, parts, rows, columns = base.shape
-    group, count = len(sums), len(s_parts)
-    height, tile = rows // split, min(columns, 512)
+    group = len(sums)
+    height, width, tile = rows // split, sums[0].shape[3], min(columns, 512)
     block = pl.BlockSpec((1, parts, height, tile), lambda a, j, _: (a, 0, p, j))
-    held = pl.BlockSpec(sums[0].shape, lambda a, j, _: (0, 0, 0, 0))
-    own = pl.BlockSpec((2, height, h_columns.shape[2]), lambda a, j, _: (0, p, 0))
-    part = pl.BlockSpec((1, parts, height, tile), lambda a, j, _: (a, 0, 0, j))
-    inputs = [own, block, block] + [part] * count + [held] * group
+    chunk = pl.BlockSpec((1, parts, height, width), lambda a, j, _: (a, 0, 0, 0))
     return pl.pallas_call(
-        lambda *refs: final_kernel(
-            group, count, *refs[: 1 + len(inputs)], *refs[1 + len(inputs) + len(earlier) :]
-        ),
+        functools.partial(final_kernel, group),
         grid_spec=pltpu.PrefetchScalarGridSpec(
             num_scalar_prefetch=1,
             grid=(ops, columns // tile),
-            in_specs=inputs + [anywhere()] * len(earlier),
+            in_specs=[block, block] + [chunk] * group + [anywhere()] * len(earlier),
             out_specs=[block, block],
-            scratch_shapes=[pltpu.VMEM((2, count * height, tile), bf16)],
         ),
         out_shape=[jax.ShapeDtypeStruct(base.shape, f32)] * 2,
-        input_output_aliases={1 + len(inputs) + k: k for k in range(len(earlier))},
+        input_output_aliases={3 + group + k: k for k in range(len(earlier))},
         compiler_params=params(16),
         cost_estimate=pl.CostEstimate(
-            flops=8 * ops * height * columns * count * height,
-            bytes_accessed=36 * base.size // split,
+            flops=4 * base.size // split,
+            bytes_accessed=18 * base.size // split,
             transcendentals=0,
         ),
         name="outputs",
-    )(places, h_columns, base, accumulated, *s_parts, *sums, *earlier)
+    )(place, base, accumulated, *sums, *earlier)
 
 
 def shards(
@@ -466,20 +470,18 @@
     def gather_back(done):
         return [done[0]] + [swap(done[b], "hier", hier, b) for b in range(1, group)]
 
-    def joined(near, across):
-        far = {mask ^ top: part for mask, part in tree(across, row, low).items()}
-        parts = {**near, **far}
-        return [parts[b] for b in range(row)]
-
     got, sent, received, sums, outs = [], [], [], [], []
 
+    first, first_chunks = make_section(0, split, state, prev_slope, own_place, group)
+    first, first_chunks, occupation, state, prev_slope, couple_v, hamiltonian = tie(
+        (first, first_chunks, occupation, state, prev_slope, couple_v, hamiltonian)
+    )
     half = [occupation] + [swap(occupation, "hier", hier, b) for b in range(1, group)]
-    first, first_chunks = make_section(0, split, state, prev_slope, own_place, group)
-    first, first_chunks, half, state, prev_slope, couple_v, hamiltonian = tie(
-        (first, first_chunks, half, state, prev_slope, couple_v, hamiltonian)
-    )
-
-    h_top, h_near = swap(hamiltonian, "row", row, top), tree(hamiltonian, row, low)
+
+    half_columns = lax.dynamic_slice_in_dim(
+        hamiltonian, row_at // (row // 2) * (columns // 2), columns // 2, 2
+    )
+    h_top = swap(half_columns, "row", row, top)
     second, second_chunks = make_section(1, split, state, prev_slope, own_place, group)
     chunks, sections = [first_chunks, second_chunks], [first, second]
     got.append(spread(0))
@@ -493,42 +495,38 @@
     vcols = lax.dynamic_slice_in_dim(couple_v, own * width, width, 1)
     heres = [vrows[:, p * height : (p + 1) * height] for p in range(split)]
     decay = jnp.sum(half[0].astype(f32) * damping[None, :], axis=1)
-    second, kept = tie((second, hamiltonian))
-    sections[1] = second
-    blocks = kept.reshape(2, rows, row, split, height)
-    h_columns = [blocks[:, :, :, p].reshape(2, rows, row * height) for p in range(split)]
-    got, chunks, sections, places, heres, vcols, decay, h_columns, h_top, h_near = tie(
-        (got, chunks, sections, places, heres, vcols, decay, h_columns, h_top, h_near)
+    got, chunks, sections, places, heres, vcols, decay, h_top, kept = tie(
+        (got, chunks, sections, places, heres, vcols, decay, h_top, hamiltonian)
     )
 
     sent.append(partial(0))
     received.append(swap(sent[0], "hier", hier, group))
     got.append(spread(1))
     across = swap(sections[0], "row", row, top)
-    got, received, across, sections, h_top, h_near = tie(
-        (got, received, across, sections, h_top, h_near)
+    near = jnp.concatenate([sections[0].reshape(-1, columns), kept.reshape(-1, columns)])
+    blocks = kept.reshape(2, rows, row, split, height)
+    h_columns = [blocks[:, :, :, p].reshape(2, rows, row * height) for p in range(split)]
+    got, received, across, sections, h_top, near, h_columns = tie(
+        (got, received, across, sections, h_top, near, h_columns)
     )
 
     sent.append(partial(1))
     received.append(swap(sent[1], "hier", hier, group))
     last_across = swap(sections[1], "row", row, top)
-    s_parts = joined(tree(sections[0], row, low), across)
-    h_parts = joined(h_near, h_top)
-    done, s_parts, h_parts = tie((coupled(0), s_parts, h_parts))
+    near, s_far, h_far = tree(near, row, low), tree(across, row, low), tree(h_top, row, low)
+    done, near, s_far, h_far = tie((coupled(0), near, s_far, h_far))
     sums.append(gather_back(done))
-    base = make_right(sections, h_parts, row_place, decay)
-    base = make_left(s_parts, h_columns[0], base, row_place)
+    base = make_right(sections, hamiltonian, near[1:], h_far, row_place, decay)
+    base = make_left([sections[0], *near[1:], *s_far], h_columns[0], base, row_place)
     received, last_across, sums, base, sections = tie(
         (received, last_across, sums, base, sections)
     )
 
-    s_parts = joined(tree(sections[1], row, low), last_across)
+    s_parts = tree(sections[1], row, low) + tree(last_across, row, low)
     sums.append(gather_back(coupled(1)))
-    both = jnp.concatenate([own_place, row_place])
+    base = make_left(s_parts, h_columns[1], base, row_place)
     for p in range(split):
-        outs = make_final(
-            p, split, base, accumulated, s_parts, h_columns[1], sums[p], both, outs
-        )
+        outs = make_final(p, split, base, accumulated, sums[p], own_place, outs)
     slope, total = outs
     return slope, total
 

time: 162 us -> 158 us (0.975)
  waiting for transfers between devices: 61.3 us -> 53.6 us
  Pallas kernels: 50.4 us -> 56.5 us
  local copies, waits for them, and re-layouts: 19.4 us -> 15.9 us
  other arithmetic: 0.33 us -> 3.67 us
  starting transfers between devices: 28.9 us -> 27.2 us
    ppermute x26 -> x25, waiting for transfers between devices: 61.3 us -> 53.6 us  [swap(): return lax.ppermute(array, axis, [(i, i ^ bit) for i in range(size)])]
    pallas_call x1 -> x2, Pallas kernels: 6.13 us -> 13.1 us  [make_left(): pl.pallas_call(functools.partial(left_kernel, count), grid=(columns // ti...]
    unnamed x42 -> x34, local copies, waits for them, and re-layouts: 8.99 us -> 2.85 us
    pallas_call x2, Pallas kernels: 13.6 us -> 7.91 us  [make_final(): pl.pallas_call(functools.partial(final_kernel, group), grid_spec=pltpu.Pr...]
    pallas_call x2, Pallas kernels: 4.67 us -> 6.62 us  [make_partial(): pl.pallas_call(functools.partial(partial_kernel, links, sides, group), in...]
    dynamic_slice x0 -> x1, local copies, waits for them, and re-layouts: none -> 1.87 us  [shards(): lax.dynamic_slice_in_dim(hamiltonian, row_at // (row // 2) * (columns //...]
    concatenate x1, other arithmetic: 0.07 us -> 1.9 us  [shards(): jnp.concatenate([sections[0].reshape(-1, columns), kept.reshape(-1, colum...]
    ppermute x26 -> x25, starting transfers between devices: 28.9 us -> 27.2 us  [swap(): return lax.ppermute(array, axis, [(i, i ^ bit) for i in range(size)])]
  transfers between devices with their start and end apart: 26 -> 25, of which waited for: 9 -> 6; matrix products, arithmetic and copies ran while one was open for 7% -> 11% of each run, Pallas kernels for 27% -> 30%
where the time goes in v1:
time: 158 us
  Pallas kernels  56.5 us (36%)
  waiting for transfers between devices  53.6 us (34%)
  starting transfers between devices  27.2 us (17%)
  local copies, waits for them, and re-layouts  15.9 us (10%)
  other arithmetic  3.67 us (2%)
    ppermute x25, waiting for transfers between devices, swap(): return lax.ppermute(array, axis, [(i, i ^ bit) for i in range(size)])  53.6 us
    ppermute x25, starting transfers between devices, swap(): return lax.ppermute(array, axis, [(i, i ^ bit) for i in range(size)])  27.2 us
    pallas_call x2, Pallas kernels, make_left(): pl.pallas_call(functools.partial(left_kernel, count), grid=(columns // ti...  13.1 us
    pallas_call x1, Pallas kernels, make_right(): pl.pallas_call(functools.partial(right_kernel, split, count), grid=(colum...  10.8 us
    pallas_call x2, Pallas kernels, make_coupled(): pl.pallas_call(functools.partial(coupled_kernel, links, sides, group), in...  10.5 us
    pallas_call x2, Pallas kernels, make_final(): pl.pallas_call(functools.partial(final_kernel, group), grid_spec=pltpu.Pr...  7.91 us
    pallas_call x2, Pallas kernels, make_section(): pl.pallas_call(section_kernel, grid_spec=pltpu.PrefetchScalarGridSpec(num...  7.53 us
    pallas_call x2, Pallas kernels, make_partial(): pl.pallas_call(functools.partial(partial_kernel, links, sides, group), in...  6.62 us
  transfers between devices with their start and end apart: 25, of which 6 were waited for; matrix products, arithmetic and copies ran while one was open for 11% of the time, Pallas kernels for 30%

profile of v1, /device:TPU:0, one launch (start us, length us, event | category | flops | bytes accessed | tf_op | source)
XLA Modules:
  0.0 157.8 jit_solution(16015817601668632269)
XLA Ops:
  0.7 5.2 %section.2 = (bf16[3,2,128,1024]{3,2,1,0:T(8,128)(2,1)}, bf16[3,2,128,256]{3,2,1,0:T(8,128)(2,1)}, bf16[3,2,128,256]{3,2,1,0:T(8,128)(2,1)}, bf16[3,2,128,256]{3,2,1,0:T(8,128)(2,1)}, bf16[3,2,128,256]{3,2,1,0:T(8,128)(2,1)}) custom-call(s32[1]{0:T(128)} %bitcast.where, bf16[3,2,256,1024]{3,2,1,0:T(8,128)(2,1)} %state.2, f32[3,2,256,1024]{3,2,1,0:T(8,128)} %slope.2), custom_call_target="tpu_custom_call" | custom-call | flops 1 | bytes 1 | tf_op jit(solution)/shard_map/section/pallas_call | solution.py:104
  5.9 4.0 %collective-permute-start.5 = (s32[3,6]{1,0:T(4,128)}, s32[3,6]{1,0:T(4,128)}, u32[]{:S(2)}, u32[]{:S(2)}) collective-permute-start(s32[3,6]{1,0:T(4,128)} %param.18), channel_id=1, source_target_pairs={{0,12},{4,8},{8,4},{12,0},{16,28},{20,24},{24,20},{28,16},{1,13},{... | collective-permute-start | bytes 224 | tf_op jit(solution)/shard_map/ppermute | solution.py:70
  9.9 0.5 collective-permute-start
  10.4 0.1 collective-permute-start.1
  10.5 2.9 %collective-permute-start.2 = (bf16[3,2,128,256]{3,2,1,0:T(8,128)(2,1)}, bf16[3,2,128,256]{3,2,1,0:T(8,128)(2,1)}, u32[]{:S(2)}, u32[]{:S(2)}) collective-permute-start(bf16[3,2,128,256]{3,2,1,0:T(8,128)(2,1)} %get-tuple-element.90), channel_id=1, source_target_pairs={{0,12},{4,8},{8,4},{12,0},{16,28},{20,24},{24,20},{28,16},{1,13},{... | collective-permute-start | bytes 1179656 | tf_op jit(solution)/shard_map/ppermute | solution.py:70
  13.4 1.9 %constant_dynamic-slice_fusion = bf16[2,256,512]{2,1,0:T(8,128)(2,1)} fusion(bf16[2,256,1024]{2,1,0:T(8,128)(2,1)} %h_own, s32[]{:T(128)S(6)} %select_n.29), kind=kLoop, calls=%fused_computation.8 | loop fusion | bytes 1048580 | tf_op jit(solution)/shard_map/dynamic_slice | solution.py:481
  15.2 1.5 collective-permute-start.6
  16.7 0.6 fusion
  17.3 0.8 multiply_reduce_fusion.decay
  18.1 0.2 copy.24.vrows
  18.3 0.0 collective-permute-done.5
  18.3 0.5 collective-permute-start.4
  18.9 1.6 %copy.23.vrows = f32[6,128,1]{2,1,0:T(8,128)} copy(f32[6,128,1]{1,0,2:T(8,128)} %get-tuple-element.167) | data formatting | bytes 6144 | tf_op jit(solution)/shard_map/optimization_barrier | solution.py:74
  20.5 9.0 %collective-permute-done.4 = s32[3,6]{1,0:T(4,128)} collective-permute-done((s32[3,6]{1,0:T(4,128)}, s32[3,6]{1,0:T(4,128)}, u32[]{:S(2)}, u32[]{:S(2)}) %collective-permute-start.4) | collective-permute-done | bytes 104 | tf_op jit(solution)/shard_map/ppermute | solution.py:70
  29.5 1.5 collective-permute-start.3
  31.0 2.8 %copy-done = f32[3,2,256,1024]{3,2,1,0:T(8,128)S(1)} copy-done((f32[3,2,256,1024]{3,2,1,0:T(8,128)S(1)}, f32[3,2,256,1024]{3,2,1,0:T(8,128)}, u32[]{:S(2)}) %copy-start) | copy-done | bytes 6291480
  33.8 2.3 %section.3 = (bf16[3,2,128,1024]{3,2,1,0:T(8,128)(2,1)S(1)}, bf16[3,2,128,256]{3,2,1,0:T(8,128)(2,1)S(1)}, bf16[3,2,128,256]{3,2,1,0:T(8,128)(2,1)}, bf16[3,2,12...) custom-call(s32[1]{0:T(128)} %bitcast.where, bf16[3,2,256,1024]{3,2,1,0:T(8,128)(2,1)S(1)} %copy-done.1, ...), custom_call_target="tpu_custom_call" | custom-call | flops 1 | bytes 1 | tf_op jit(solution)/shard_map/section/pallas_call | solution.py:104
  36.1 0.8 pad_add_fusion
  36.9 0.1 compare_reduce_fusion
  37.0 0.0 collective-permute-done.refs_1_
  37.1 0.0 collective-permute-done.1.refs_2_
  37.1 0.0 collective-permute-done.6.refs_4_
  37.1 1.6 %collective-permute-start.11 = (bf16[3,2,128,1024]{3,2,1,0:T(8,128)(2,1)}, bf16[3,2,128,1024]{3,2,1,0:T(8,128)(2,1)}, u32[]{:S(2)}, u32[]{:S(2)}) collective-permute-start(bf16[3,2,128,1024]{3,2,1,0:T(8,128)(2,1)} %get-tuple-element.142.refs_0_), channel_id=1, source_target_pairs={{0,2},{1,3},{2,0},{3,1},{4,6},{5,7},{6,4},{7,5},{8,10},{9,11},{10,... | collective-permute-start | bytes 4718600 | tf_op jit(solution)/shard_map/ppermute | solution.py:70
  38.7 3.7 %partial_sums.2 = bf16[6,2,128,256]{3,2,1,0:T(8,128)(2,1)} custom-call(s32[24]{0:T(128)S(1)} %select_reduce_fusion.places, f32[2,6]{1,0:T(2,128)S(1)} %copy-done.11, f32[6,128,1]{2,1,0:T(8,128)S(1)} %copy-done.3, f32[6,256]{1,0:T(8,128)S(1)} %get-tuple-element.112.vcols, bf16[3,2,128,256]{3,2,1,0:T(8,128)(2,1)S(1)} %copy-done.5, ...), custom_call_target="tpu_custom_call" | custom-call | flops 7864320 | bytes 2359296 | tf_op jit(solution)/shard_map/partial_sums/pallas_call | solution.py:243
  42.4 2.6 %collective-permute-start.10 = (bf16[6,2,128,256]{3,2,1,0:T(8,128)(2,1)}, bf16[6,2,128,256]{3,2,1,0:T(8,128)(2,1)}, u32[]{:S(2)}, u32[]{:S(2)}) collective-permute-start(bf16[6,2,128,256]{3,2,1,0:T(8,128)(2,1)} %partial_sums.2), channel_id=1, source_target_pairs={{0,16},{4,20},{8,24},{12,28},{16,0},{20,4},{24,8},{28,12},{1,17},{... | collective-permute-start | bytes 2359304 | tf_op jit(solution)/shard_map/ppermute | solution.py:70
  45.0 0.5 collective-permute-start.7
  45.6 0.5 collective-permute-start.8
  46.0 2.5 %collective-permute-start.9 = (bf16[3,2,128,256]{3,2,1,0:T(8,128)(2,1)}, bf16[3,2,128,256]{3,2,1,0:T(8,128)(2,1)}, u32[]{:S(2)}, u32[]{:S(2)}) collective-permute-start(bf16[3,2,128,256]{3,2,1,0:T(8,128)(2,1)} %get-tuple-element.109), channel_id=1, source_target_pairs={{0,12},{4,8},{8,4},{12,0},{16,28},{20,24},{24,20},{28,16},{1,13},{... | collective-permute-start | bytes 1179656 | tf_op jit(solution)/shard_map/ppermute | solution.py:70
  48.5 0.7 reshape.26
  49.3 6.6 %slice_reduce_fusion = (bf16[2,256,4,128]{3,2,1,0:T(4,128)(2,1)}, bf16[2,256,4,128]{3,2,1,0:T(4,128)(2,1)S(1)}) fusion(bf16[2,256,4,2,128]{4,3,2,1,0:T(2,128)(2,1)S(1)} %reshape.26), kind=kLoop, calls=%fused_computation.1 | loop fusion | bytes 2097152 | tf_op jit(solution)/shard_map/slice | solution.py:508
  55.9 1.2 reshape_squeeze.7.h_own
  57.1 0.2 reshape_squeeze.6.h_own
  57.3 0.0 copy-start.10
  57.4 1.9 %pad_maximum_fusion = bf16[1280,1024]{1,0:T(8,128)(2,1)S(1)} fusion(bf16[512,1024]{1,0:T(8,128)(2,1)S(1)} %bitcast.8, bf16[768,1024]{1,0:T(8,128)(2,1)} %bitcast.3), kind=kLoop, calls=%fused_computation | loop fusion | flops 5242880 | bytes 5242880 | tf_op jit(solution)/shard_map/concatenate | solution.py:506
  59.3 0.0 collective-permute-done.7.refs_1_
  59.3 12.5 %collective-permute-done.8.refs_2_ = bf16[3,2,128,256]{3,2,1,0:T(8,128)(2,1)} collective-permute-done((bf16[3,2,128,256]{3,2,1,0:T(8,128)(2,1)}, bf16[3,2,128,256]{3,2,1,0:T(8,128)(2,1)}, u32[]{:S(2)}, u32[]{:S(2)}) %collective-permute-start.8) | collective-permute-done | bytes 393248 | tf_op jit(solution)/shard_map/ppermute | solution.py:70
  71.8 8.5 %collective-permute-done.9.refs_3_ = bf16[3,2,128,256]{3,2,1,0:T(8,128)(2,1)} collective-permute-done((bf16[3,2,128,256]{3,2,1,0:T(8,128)(2,1)}, bf16[3,2,128,256]{3,2,1,0:T(8,128)(2,1)}, u32[]{:S(2)}, u32[]{:S(2)}) %collective-permute-start.9) | collective-permute-done | bytes 393248 | tf_op jit(solution)/shard_map/ppermute | solution.py:70
  80.2 0.0 collective-permute-done.11.refs_2_
  80.2 0.0 collective-permute-start.14
  80.3 0.5 collective-permute-start.15
  80.8 0.4 collective-permute-start.13
  81.1 2.9 %partial_sums.3 = bf16[6,2,128,256]{3,2,1,0:T(8,128)(2,1)S(1)} custom-call(s32[24]{0:T(128)S(1)} %select_reduce_fusion.places, f32[2,6]{1,0:T(2,128)S(1)} %copy-done.11, f32[6,128,1]{2,1,0:T(8,128)S(1)} %copy.24.vrows, f32[6,256]{1,0:T(8,128)S(1)} %get-tuple-element.112.vcols, bf16[3,2,128,256]{3,2,1,0:T(8,128)(2,1)S(1)} %copy-done.8, ...), custom_call_target="tpu_custom_call" | custom-call | flops 7864320 | bytes 2359296 | tf_op jit(solution)/shard_map/partial_sums/pallas_call | solution.py:243
  84.0 0.1 collective-permute-start.12
  84.1 5.4 %coupling_sums.2 = (bf16[3,2,128,256]{3,2,1,0:T(8,128)(2,1)S(1)}, bf16[3,2,128,256]{3,2,1,0:T(8,128)(2,1)S(1)}, bf16[3,2,128,256]{3,2,1,0:T(8,128)(2,1)S(1)}, bf16[3,2,128,256]{3,2,1,0:T(8,128)(2,1)S(1)}) custom-call(s32[24]{0:T(128)S(1)} %select_reduce_fusion.places, f32[2,6]{1,0:T(2,128)S(1)} %copy-done.11, f32[6,128,1]{2,1,0:T(8,128)S(1)} %copy-done.4, ...), custom_call_target="tpu_custom_call" | custom-call | flops 1 | bytes 1 | tf_op jit(solution)/shard_map/coupling_sums/pallas_call | solution.py:264
  89.5 0.0 collective-permute-done.15.refs_3_
  89.5 0.0 collective-permute-done.14.refs_2_.refs_3_.refs_1_
  89.5 0.8 collective-permute-start.17
  90.2 0.5 collective-permute-start.18
  90.7 2.3 %collective-permute-start.19 = (bf16[3,2,128,256]{3,2,1,0:T(8,128)(2,1)S(1)}, bf16[3,2,128,256]{3,2,1,0:T(8,128)(2,1)S(1)}, u32[]{:S(2)}, u32[]{:S(2)}) collective-permute-start(bf16[3,2,128,256]{3,2,1,0:T(8,128)(2,1)S(1)} %get-tuple-element.139), channel_id=1, source_target_pairs={{0,12},{4,8},{8,4},{12,0},{16,28},{20,24},{24,20},{28,16},{1,13},{... | collective-permute-start | bytes 1179656 | tf_op jit(solution)/shard_map/ppermute | solution.py:70
  93.0 10.8 %right_products.1.base = f32[3,2,256,1024]{3,2,1,0:T(8,128)S(1)} custom-call(s32[1]{0:T(128)} %bitcast.1.where, f32[3]{0:T(128)S(1)} %multiply_reduce_fusion.decay, bf16[2,256,1024]{2,1,0:T(8,128)(2,1)S(1)} %copy-done.2, bf16[3,2,128,1024]{3,2,1,0:T(8,128)(2,1)} %get-tuple-element.142.refs_0_, bf16[3,2,128,1024]{3,2,1,0:T(8,128)(2,1)S(1)} %copy-done.10, ...), custom_call_target="tpu_custom_call" | custom-call | flops 6442450944 | bytes 13631488 | tf_op jit(solution)/shard_map/right_products/pallas_call | solution.py:327
  103.8 7.0 %left_products.2.base = f32[3,2,256,1024]{3,2,1,0:T(8,128)S(1)} custom-call(s32[1]{0:T(128)} %bitcast.1.where, bf16[2,256,512]{2,1,0:T(8,128)(2,1)S(1)} %reshape_squeeze.6.h_own, f32[3,2,256,1024]{3,2,1,0:T(8,128)S(1)} %right_products.1.base, bf16[3,2,128,1024]{3,2,1,0:T(8,128)(2,1)} %get-tuple-element.142.refs_0_, ...), custom_call_target="tpu_custom_call" | custom-call | flops 3221225472 | bytes 18874368 | tf_op jit(solution)/shard_map/left_products/pallas_call | solution.py:363
  110.8 9.9 %collective-permute-done.12.refs_4_ = bf16[6,2,128,256]{3,2,1,0:T(8,128)(2,1)S(1)} collective-permute-done((bf16[6,2,128,256]{3,2,1,0:T(8,128)(2,1)S(1)}, bf16[6,2,128,256]{3,2,1,0:T(8,128)(2,1)S(1)}, u32[]{:S(2)}, u32[]{:S(2)}) %collective-permute-start.12) | collective-permute-done | bytes 786464 | tf_op jit(solution)/shard_map/ppermute | solution.py:70
  120.7 0.0 collective-permute-done.13.refs_2_
  120.7 0.0 collective-permute-done.17.refs_1_
  120.7 0.0 collective-permute-done.18.refs_2_
  120.7 6.8 %collective-permute-done.19.refs_3_ = bf16[3,2,128,256]{3,2,1,0:T(8,128)(2,1)S(1)} collective-permute-done((bf16[3,2,128,256]{3,2,1,0:T(8,128)(2,1)S(1)}, bf16[3,2,128,256]{3,2,1,0:T(8,128)(2,1)S(1)}, u32[]{:S(2)}, u32[]{:S(2)}) %collective-permute-start.19) | collective-permute-done | bytes 393248 | tf_op jit(solution)/shard_map/ppermute | solution.py:70
  127.4 0.5 collective-permute-start.21
  128.0 5.2 %coupling_sums.3 = (bf16[3,2,128,256]{3,2,1,0:T(8,128)(2,1)S(1)}, bf16[3,2,128,256]{3,2,1,0:T(8,128)(2,1)S(1)}, bf16[3,2,128,256]{3,2,1,0:T(8,128)(2,1)S(1)}, bf16[3,2,128,256]{3,2,1,0:T(8,128)(2,1)S(1)}) custom-call(s32[24]{0:T(128)S(1)} %select_reduce_fusion.places, f32[2,6]{1,0:T(2,128)S(1)} %copy-done.11, f32[6,128,1]{2,1,0:T(8,128)S(1)} %copy.24.vrows, ...), custom_call_target="tpu_custom_call" | custom-call | flops 1 | bytes 1 | tf_op jit(solution)/shard_map/coupling_sums/pallas_call | solution.py:264
  133.1 0.8 collective-permute-start.22
  133.9 2.8 %collective-permute-start.24 = (bf16[3,2,128,256]{3,2,1,0:T(8,128)(2,1)S(1)}, bf16[3,2,128,256]{3,2,1,0:T(8,128)(2,1)S(1)}, u32[]{:S(2)}, u32[]{:S(2)}) collective-permute-start(bf16[3,2,128,256]{3,2,1,0:T(8,128)(2,1)S(1)} %get-tuple-element.155), channel_id=1, source_target_pairs={{0,12},{4,8},{8,4},{12,0},{16,28},{20,24},{24,20},{28,16},{1,13},{... | collective-permute-start | bytes 1179656 | tf_op jit(solution)/shard_map/ppermute | solution.py:70
  136.7 6.2 %left_products.3.base = f32[3,2,256,1024]{3,2,1,0:T(8,128)S(1)} custom-call(s32[1]{0:T(128)} %bitcast.1.where, bf16[2,256,512]{2,1,0:T(8,128)(2,1)S(1)} %reshape_squeeze.7.h_own, f32[3,2,256,1024]{3,2,1,0:T(8,128)S(1)} %left_products.2.base, bf16[3,2,128,1024]{3,2,1,0:T(8,128)(2,1)S(1)} %copy-done.10, ...), custom_call_target="tpu_custom_call" | custom-call | flops 3221225472 | bytes 18874368 | tf_op jit(solution)/shard_map/left_products/pallas_call | solution.py:363
  142.9 4.0 %outputs.2 = (f32[3,2,256,1024]{3,2,1,0:T(8,128)}, f32[3,2,256,1024]{3,2,1,0:T(8,128)}) custom-call(s32[1]{0:T(128)} %bitcast.where, f32[3,2,256,1024]{3,2,1,0:T(8,128)S(1)} %left_products.3.base, f32[3,2,256,1024]{3,2,1,0:T(8,128)S(1)} %bitcast.7, bf16[3,2,128,256]{3,2,1,0:T(8,128)(2,1)S(1)} %get-tuple-element.156.refs_0_, ...), custom_call_target="tpu_custom_call" | custom-call | flops 3145728 | bytes 14155776 | tf_op jit(solution)/shard_map/outputs/pallas_call | solution.py:411
  146.9 7.0 %collective-permute-done.24.refs_3_ = bf16[3,2,128,256]{3,2,1,0:T(8,128)(2,1)S(1)} collective-permute-done((bf16[3,2,128,256]{3,2,1,0:T(8,128)(2,1)S(1)}, bf16[3,2,128,256]{3,2,1,0:T(8,128)(2,1)S(1)}, u32[]{:S(2)}, u32[]{:S(2)}) %collective-permute-start.24) | collective-permute-done | bytes 393248 | tf_op jit(solution)/shard_map/ppermute | solution.py:70
  153.8 3.9 %outputs.3 = (f32[3,2,256,1024]{3,2,1,0:T(8,128)}, f32[3,2,256,1024]{3,2,1,0:T(8,128)}) custom-call(s32[1]{0:T(128)} %bitcast.where, f32[3,2,256,1024]{3,2,1,0:T(8,128)S(1)} %left_products.3.base, f32[3,2,256,1024]{3,2,1,0:T(8,128)S(1)} %bitcast.7, ...), custom_call_target="tpu_custom_call", output_to_operand_aliasing={{0}: (7, {}), {1}: (8, {})} | custom-call | flops 3145728 | bytes 14155776 | tf_op jit(solution)/shard_map/outputs/pallas_call | solution.py:411
  (46 shorter events, 0.1 us)
Async XLA Ops:
  0.6 16.1 %copy-start.12 = (f32[6,1024]{1,0:T(8,128)S(1)}, f32[6,1024]{1,0:T(8,128)}, u32[]{:S(2)}) copy-start(f32[6,1024]{1,0:T(8,128)} %param.15) | copy-start | bytes 73732
  0.7 16.7 %copy-start.14 = (f32[6]{0:T(128)S(1)}, f32[6]{0:T(128)}, u32[]{:S(2)}) copy-start(f32[6]{0:T(128)} %param.17) | copy-start | bytes 76
  0.7 30.3 %copy-start.1 = (bf16[3,2,256,1024]{3,2,1,0:T(8,128)(2,1)S(1)}, bf16[3,2,256,1024]{3,2,1,0:T(8,128)(2,1)}, u32[]{:S(2)}) copy-start(bf16[3,2,256,1024]{3,2,1,0:T(8,128)(2,1)} %state.2) | copy-start | bytes 9437188
  5.9 12.4 %collective-permute-start.5 = (s32[3,6]{1,0:T(4,128)}, s32[3,6]{1,0:T(4,128)}, u32[]{:S(2)}, u32[]{:S(2)}) collective-permute-start(s32[3,6]{1,0:T(4,128)} %param.18), channel_id=1, source_target_pairs={{0,12},{4,8},{8,4},{12,0},{16,28},{20,24},{24,20},{28,16},{1,13},{... | collective-permute-start | bytes 224 | tf_op jit(solution)/shard_map/ppermute | solution.py:70
  9.9 27.2 %collective-permute-start = (bf16[3,2,128,256]{3,2,1,0:T(8,128)(2,1)}, bf16[3,2,128,256]{3,2,1,0:T(8,128)(2,1)}, u32[]{:S(2)}, u32[]{:S(2)}) collective-permute-start(bf16[3,2,128,256]{3,2,1,0:T(8,128)(2,1)} %get-tuple-element.88), channel_id=1, source_target_pairs={{0,4},{4,0},{8,12},{12,8},{16,20},{20,16},{24,28},{28,24},{1,5},{5... | collective-permute-start | bytes 1179656 | tf_op jit(solution)/shard_map/ppermute | solution.py:70
  10.4 26.7 %collective-permute-start.1 = (bf16[3,2,128,256]{3,2,1,0:T(8,128)(2,1)}, bf16[3,2,128,256]{3,2,1,0:T(8,128)(2,1)}, u32[]{:S(2)}, u32[]{:S(2)}) collective-permute-start(bf16[3,2,128,256]{3,2,1,0:T(8,128)(2,1)} %get-tuple-element.89), channel_id=1, source_target_pairs={{0,8},{4,12},{8,0},{12,4},{16,24},{20,28},{24,16},{28,20},{1,9},{5... | collective-permute-start | bytes 1179656 | tf_op jit(solution)/shard_map/ppermute | solution.py:70
  10.5 26.6 %collective-permute-start.2 = (bf16[3,2,128,256]{3,2,1,0:T(8,128)(2,1)}, bf16[3,2,128,256]{3,2,1,0:T(8,128)(2,1)}, u32[]{:S(2)}, u32[]{:S(2)}) collective-permute-start(bf16[3,2,128,256]{3,2,1,0:T(8,128)(2,1)} %get-tuple-element.90), channel_id=1, source_target_pairs={{0,12},{4,8},{8,4},{12,0},{16,28},{20,24},{24,20},{28,16},{1,13},{... | collective-permute-start | bytes 1179656 | tf_op jit(solution)/shard_map/ppermute | solution.py:70
  15.2 21.9 %collective-permute-start.6 = (bf16[2,256,512]{2,1,0:T(8,128)(2,1)}, bf16[2,256,512]{2,1,0:T(8,128)(2,1)}, u32[]{:S(2)}, u32[]{:S(2)}) collective-permute-start(bf16[2,256,512]{2,1,0:T(8,128)(2,1)} %constant_dynamic-slice_fusion), channel_id=1, source_target_pairs={{0,2},{1,3},{2,0},{3,1},{4,6},{5,7},{6,4},{7,5},{8,10},{9,11},{10,... | collective-permute-start | bytes 1572872 | tf_op jit(solution)/shard_map/ppermute | solution.py:70
  18.3 11.1 %collective-permute-start.4 = (s32[3,6]{1,0:T(4,128)}, s32[3,6]{1,0:T(4,128)}, u32[]{:S(2)}, u32[]{:S(2)}) collective-permute-start(s32[3,6]{1,0:T(4,128)} %param.18), channel_id=1, source_target_pairs={{0,8},{4,12},{8,0},{12,4},{16,24},{20,28},{24,16},{28,20},{1,9},{5... | collective-permute-start | bytes 224 | tf_op jit(solution)/shard_map/ppermute | solution.py:70
  18.9 19.8 %copy-start.11 = (f32[2,6]{1,0:T(2,128)S(1)}, f32[2,6]{1,0:T(2,128)}, u32[]{:S(2)}) copy-start(f32[2,6]{1,0:T(2,128)} %coupling.7) | copy-start | bytes 148
  29.5 6.6 %collective-permute-start.3 = (s32[3,6]{1,0:T(4,128)}, s32[3,6]{1,0:T(4,128)S(1)}, u32[]{:S(2)}, u32[]{:S(2)}) collective-permute-start(s32[3,6]{1,0:T(4,128)} %param.18), channel_id=1, source_target_pairs={{0,4},{4,0},{8,12},{12,8},{16,20},{20,16},{24,28},{28,24},{1,5},{5... | collective-permute-start | bytes 224 | tf_op jit(solution)/shard_map/ppermute | solution.py:70
  31.0 2.8 %copy-start = (f32[3,2,256,1024]{3,2,1,0:T(8,128)S(1)}, f32[3,2,256,1024]{3,2,1,0:T(8,128)}, u32[]{:S(2)}) copy-start(f32[3,2,256,1024]{3,2,1,0:T(8,128)} %slope.2) | copy-start | bytes 18874372
  33.8 3.2 %copy-start.13 = (s32[24,6]{0,1:T(8,128)S(1)}, s32[24,6]{0,1:T(8,128)}, u32[]{:S(2)}) copy-start(s32[24,6]{0,1:T(8,128)} %constant.52.clone) | copy-start | bytes 1732
  33.8 4.9 %copy-start.3 = (f32[6,128,1]{2,1,0:T(8,128)S(1)}, f32[6,128,1]{2,1,0:T(8,128)}, u32[]{:S(2)}) copy-start(f32[6,128,1]{2,1,0:T(8,128)} %copy.23.vrows) | copy-start | bytes 9220
  33.8 4.9 %copy-start.5 = (bf16[3,2,128,256]{3,2,1,0:T(8,128)(2,1)S(1)}, bf16[3,2,128,256]{3,2,1,0:T(8,128)(2,1)}, u32[]{:S(2)}) copy-start(bf16[3,2,128,256]{3,2,1,0:T(8,128)(2,1)} %get-tuple-element.125.refs_0_) | copy-start | bytes 1179652
  36.1 6.4 %copy-start.7 = (bf16[3,2,128,256]{3,2,1,0:T(8,128)(2,1)}, bf16[3,2,128,256]{3,2,1,0:T(8,128)(2,1)S(1)}, u32[]{:S(2)}) copy-start(bf16[3,2,128,256]{3,2,1,0:T(8,128)(2,1)S(1)} %get-tuple-element.120.refs_0_) | copy-start | bytes 1179652
  36.1 9.0 %copy-start.9 = (bf16[3,2,128,1024]{3,2,1,0:T(8,128)(2,1)}, bf16[3,2,128,1024]{3,2,1,0:T(8,128)(2,1)S(1)}, u32[]{:S(2)}) copy-start(bf16[3,2,128,1024]{3,2,1,0:T(8,128)(2,1)S(1)} %get-tuple-element.149.refs_1_.refs_0_) | copy-start | bytes 4718596
  36.1 12.5 %copy-start.2 = (bf16[2,256,1024]{2,1,0:T(8,128)(2,1)S(1)}, bf16[2,256,1024]{2,1,0:T(8,128)(2,1)}, u32[]{:S(2)}) copy-start(bf16[2,256,1024]{2,1,0:T(8,128)(2,1)} %h_own) | copy-start | bytes 3145732
  37.1 43.2 %collective-permute-start.11 = (bf16[3,2,128,1024]{3,2,1,0:T(8,128)(2,1)}, bf16[3,2,128,1024]{3,2,1,0:T(8,128)(2,1)}, u32[]{:S(2)}, u32[]{:S(2)}) collective-permute-start(bf16[3,2,128,1024]{3,2,1,0:T(8,128)(2,1)} %get-tuple-element.142.refs_0_), channel_id=1, source_target_pairs={{0,2},{1,3},{2,0},{3,1},{4,6},{5,7},{6,4},{7,5},{8,10},{9,11},{10,... | collective-permute-start | bytes 4718600 | tf_op jit(solution)/shard_map/ppermute | solution.py:70
  42.4 37.8 %collective-permute-start.10 = (bf16[6,2,128,256]{3,2,1,0:T(8,128)(2,1)}, bf16[6,2,128,256]{3,2,1,0:T(8,128)(2,1)}, u32[]{:S(2)}, u32[]{:S(2)}) collective-permute-start(bf16[6,2,128,256]{3,2,1,0:T(8,128)(2,1)} %partial_sums.2), channel_id=1, source_target_pairs={{0,16},{4,20},{8,24},{12,28},{16,0},{20,4},{24,8},{28,12},{1,17},{... | collective-permute-start | bytes 2359304 | tf_op jit(solution)/shard_map/ppermute | solution.py:70
  45.0 14.2 %collective-permute-start.7 = (bf16[3,2,128,256]{3,2,1,0:T(8,128)(2,1)}, bf16[3,2,128,256]{3,2,1,0:T(8,128)(2,1)}, u32[]{:S(2)}, u32[]{:S(2)}) collective-permute-start(bf16[3,2,128,256]{3,2,1,0:T(8,128)(2,1)} %get-tuple-element.107), channel_id=1, source_target_pairs={{0,4},{4,0},{8,12},{12,8},{16,20},{20,16},{24,28},{28,24},{1,5},{5... | collective-permute-start | bytes 1179656 | tf_op jit(solution)/shard_map/ppermute | solution.py:70
  45.6 26.2 %collective-permute-start.8 = (bf16[3,2,128,256]{3,2,1,0:T(8,128)(2,1)}, bf16[3,2,128,256]{3,2,1,0:T(8,128)(2,1)}, u32[]{:S(2)}, u32[]{:S(2)}) collective-permute-start(bf16[3,2,128,256]{3,2,1,0:T(8,128)(2,1)} %get-tuple-element.108), channel_id=1, source_target_pairs={{0,8},{4,12},{8,0},{12,4},{16,24},{20,28},{24,16},{28,20},{1,9},{5... | collective-permute-start | bytes 1179656 | tf_op jit(solution)/shard_map/ppermute | solution.py:70
  46.0 34.2 %collective-permute-start.9 = (bf16[3,2,128,256]{3,2,1,0:T(8,128)(2,1)}, bf16[3,2,128,256]{3,2,1,0:T(8,128)(2,1)}, u32[]{:S(2)}, u32[]{:S(2)}) collective-permute-start(bf16[3,2,128,256]{3,2,1,0:T(8,128)(2,1)} %get-tuple-element.109), channel_id=1, source_target_pairs={{0,12},{4,8},{8,4},{12,0},{16,28},{20,24},{24,20},{28,16},{1,13},{... | collective-permute-start | bytes 1179656 | tf_op jit(solution)/shard_map/ppermute | solution.py:70
  57.3 23.4 %copy-start.10 = (bf16[3,2,128,1024]{3,2,1,0:T(8,128)(2,1)S(1)}, bf16[3,2,128,1024]{3,2,1,0:T(8,128)(2,1)}, u32[]{:S(2)}) copy-start(bf16[3,2,128,1024]{3,2,1,0:T(8,128)(2,1)} %copy-done.9) | copy-start | bytes 4718596
  57.3 23.8 %copy-start.8 = (bf16[3,2,128,256]{3,2,1,0:T(8,128)(2,1)S(1)}, bf16[3,2,128,256]{3,2,1,0:T(8,128)(2,1)}, u32[]{:S(2)}) copy-start(bf16[3,2,128,256]{3,2,1,0:T(8,128)(2,1)} %copy-done.7) | copy-start | bytes 1179652
  57.3 26.7 %copy-start.4 = (f32[6,128,1]{2,1,0:T(8,128)S(1)}, f32[6,128,1]{2,1,0:T(8,128)}, u32[]{:S(2)}) copy-start(f32[6,128,1]{2,1,0:T(8,128)} %copy.23.vrows) | copy-start | bytes 9220
  57.4 26.7 %copy-start.6 = (bf16[3,2,128,256]{3,2,1,0:T(8,128)(2,1)S(1)}, bf16[3,2,128,256]{3,2,1,0:T(8,128)(2,1)}, u32[]{:S(2)}) copy-start(bf16[3,2,128,256]{3,2,1,0:T(8,128)(2,1)} %get-tuple-element.125.refs_0_) | copy-start | bytes 1179652
  80.2 9.2 %collective-permute-start.14 = (bf16[1280,1024]{1,0:T(8,128)(2,1)S(1)}, bf16[1280,1024]{1,0:T(8,128)(2,1)S(1)}, u32[]{:S(2)}, u32[]{:S(2)}) collective-permute-start(bf16[1280,1024]{1,0:T(8,128)(2,1)S(1)} %pad_maximum_fusion), channel_id=1, source_target_pairs={{0,1},{1,0},{2,3},{3,2},{4,5},{5,4},{6,7},{7,6},{8,9},{9,8},{10,11... | collective-permute-start | bytes 7864328 | tf_op jit(solution)/shard_map/ppermute | solution.py:70
  80.3 9.2 %collective-permute-start.15 = (bf16[3,2,128,1024]{3,2,1,0:T(8,128)(2,1)}, bf16[3,2,128,1024]{3,2,1,0:T(8,128)(2,1)S(1)}, u32[]{:S(2)}, u32[]{:S(2)}) collective-permute-start(bf16[3,2,128,1024]{3,2,1,0:T(8,128)(2,1)} %collective-permute-done.11.refs_2_), channel_id=1, source_target_pairs={{0,1},{1,0},{2,3},{3,2},{4,5},{5,4},{6,7},{7,6},{8,9},{9,8},{10,11... | collective-permute-start | bytes 4718600 | tf_op jit(solution)/shard_map/ppermute | solution.py:70
  80.8 39.9 %collective-permute-start.13 = (bf16[3,2,128,1024]{3,2,1,0:T(8,128)(2,1)S(1)}, bf16[3,2,128,1024]{3,2,1,0:T(8,128)(2,1)S(1)}, u32[]{:S(2)}, u32[]{:S(2)}) collective-permute-start(bf16[3,2,128,1024]{3,2,1,0:T(8,128)(2,1)S(1)} %copy-done.10), channel_id=1, source_target_pairs={{0,2},{1,3},{2,0},{3,1},{4,6},{5,7},{6,4},{7,5},{8,10},{9,11},{10,... | collective-permute-start | bytes 4718600 | tf_op jit(solution)/shard_map/ppermute | solution.py:70
  81.1 8.3 %collective-permute-start.16 = (bf16[2,256,512]{2,1,0:T(8,128)(2,1)}, bf16[2,256,512]{2,1,0:T(8,128)(2,1)S(1)}, u32[]{:S(2)}, u32[]{:S(2)}) collective-permute-start(bf16[2,256,512]{2,1,0:T(8,128)(2,1)} %collective-permute-done.6.refs_4_), channel_id=1, source_target_pairs={{0,1},{1,0},{2,3},{3,2},{4,5},{5,4},{6,7},{7,6},{8,9},{9,8},{10,11... | collective-permute-start | bytes 1572872 | tf_op jit(solution)/shard_map/ppermute | solution.py:70
  84.0 36.7 %collective-permute-start.12 = (bf16[6,2,128,256]{3,2,1,0:T(8,128)(2,1)S(1)}, bf16[6,2,128,256]{3,2,1,0:T(8,128)(2,1)S(1)}, u32[]{:S(2)}, u32[]{:S(2)}) collective-permute-start(bf16[6,2,128,256]{3,2,1,0:T(8,128)(2,1)S(1)} %partial_sums.3), channel_id=1, source_target_pairs={{0,16},{4,20},{8,24},{12,28},{16,0},{20,4},{24,8},{28,12},{1,17},{... | collective-permute-start | bytes 2359304 | tf_op jit(solution)/shard_map/ppermute | solution.py:70
  89.5 31.2 %collective-permute-start.17 = (bf16[3,2,128,256]{3,2,1,0:T(8,128)(2,1)S(1)}, bf16[3,2,128,256]{3,2,1,0:T(8,128)(2,1)S(1)}, u32[]{:S(2)}, u32[]{:S(2)}) collective-permute-start(bf16[3,2,128,256]{3,2,1,0:T(8,128)(2,1)S(1)} %get-tuple-element.137), channel_id=1, source_target_pairs={{0,4},{4,0},{8,12},{12,8},{16,20},{20,16},{24,28},{28,24},{1,5},{5... | collective-permute-start | bytes 1179656 | tf_op jit(solution)/shard_map/ppermute | solution.py:70
  90.2 30.4 %collective-permute-start.18 = (bf16[3,2,128,256]{3,2,1,0:T(8,128)(2,1)S(1)}, bf16[3,2,128,256]{3,2,1,0:T(8,128)(2,1)S(1)}, u32[]{:S(2)}, u32[]{:S(2)}) collective-permute-start(bf16[3,2,128,256]{3,2,1,0:T(8,128)(2,1)S(1)} %get-tuple-element.138), channel_id=1, source_target_pairs={{0,8},{4,12},{8,0},{12,4},{16,24},{20,28},{24,16},{28,20},{1,9},{5... | collective-permute-start | bytes 1179656 | tf_op jit(solution)/shard_map/ppermute | solution.py:70
  90.7 36.7 %collective-permute-start.19 = (bf16[3,2,128,256]{3,2,1,0:T(8,128)(2,1)S(1)}, bf16[3,2,128,256]{3,2,1,0:T(8,128)(2,1)S(1)}, u32[]{:S(2)}, u32[]{:S(2)}) collective-permute-start(bf16[3,2,128,256]{3,2,1,0:T(8,128)(2,1)S(1)} %get-tuple-element.139), channel_id=1, source_target_pairs={{0,12},{4,8},{8,4},{12,0},{16,28},{20,24},{24,20},{28,16},{1,13},{... | collective-permute-start | bytes 1179656 | tf_op jit(solution)/shard_map/ppermute | solution.py:70
  127.4 9.3 %collective-permute-start.20 = (bf16[3,2,128,1024]{3,2,1,0:T(8,128)(2,1)S(1)}, bf16[3,2,128,1024]{3,2,1,0:T(8,128)(2,1)S(1)}, u32[]{:S(2)}, u32[]{:S(2)}) collective-permute-start(bf16[3,2,128,1024]{3,2,1,0:T(8,128)(2,1)S(1)} %copy-done.10), channel_id=1, source_target_pairs={{0,1},{1,0},{2,3},{3,2},{4,5},{5,4},{6,7},{7,6},{8,9},{9,8},{10,11... | collective-permute-start | bytes 4718600 | tf_op jit(solution)/shard_map/ppermute | solution.py:70
  127.4 9.3 %collective-permute-start.21 = (bf16[3,2,128,1024]{3,2,1,0:T(8,128)(2,1)S(1)}, bf16[3,2,128,1024]{3,2,1,0:T(8,128)(2,1)S(1)}, u32[]{:S(2)}, u32[]{:S(2)}) collective-permute-start(bf16[3,2,128,1024]{3,2,1,0:T(8,128)(2,1)S(1)} %collective-permute-done.13.refs_2_), channel_id=1, source_target_pairs={{0,1},{1,0},{2,3},{3,2},{4,5},{5,4},{6,7},{7,6},{8,9},{9,8},{10,11... | collective-permute-start | bytes 4718600 | tf_op jit(solution)/shard_map/ppermute | solution.py:70
  128.0 14.9 %slice-start = ((s8[6291456]{0:T(1024)(128)(4,1)}), s8[4194304]{0:T(1024)(128)(4,1)S(1)}, s32[]{:S(2)}) async-start(s8[6291456]{0:T(1024)(128)(4,1)} %bitcast.6), calls=%async_computation | async-start | bytes 8388608
  133.1 13.7 %collective-permute-start.22 = (bf16[3,2,128,256]{3,2,1,0:T(8,128)(2,1)S(1)}, bf16[3,2,128,256]{3,2,1,0:T(8,128)(2,1)S(1)}, u32[]{:S(2)}, u32[]{:S(2)}) collective-permute-start(bf16[3,2,128,256]{3,2,1,0:T(8,128)(2,1)S(1)} %get-tuple-element.153), channel_id=1, source_target_pairs={{0,4},{4,0},{8,12},{12,8},{16,20},{20,16},{24,28},{28,24},{1,5},{5... | collective-permute-start | bytes 1179656 | tf_op jit(solution)/shard_map/ppermute | solution.py:70
  133.9 13.0 %collective-permute-start.23 = (bf16[3,2,128,256]{3,2,1,0:T(8,128)(2,1)S(1)}, bf16[3,2,128,256]{3,2,1,0:T(8,128)(2,1)S(1)}, u32[]{:S(2)}, u32[]{:S(2)}) collective-permute-start(bf16[3,2,128,256]{3,2,1,0:T(8,128)(2,1)S(1)} %get-tuple-element.154), channel_id=1, source_target_pairs={{0,8},{4,12},{8,0},{12,4},{16,24},{20,28},{24,16},{28,20},{1,9},{5... | collective-permute-start | bytes 1179656 | tf_op jit(solution)/shard_map/ppermute | solution.py:70
  133.9 9.0 %slice-start.1 = ((s8[6291456]{0:T(1024)(128)(4,1)}), s8[2097152]{0:T(1024)(128)(4,1)S(1)}, s32[]{:S(2)}) async-start(s8[6291456]{0:T(1024)(128)(4,1)} %bitcast.6), calls=%async_computation.1 | async-start | bytes 4194304
  133.9 19.9 %collective-permute-start.24 = (bf16[3,2,128,256]{3,2,1,0:T(8,128)(2,1)S(1)}, bf16[3,2,128,256]{3,2,1,0:T(8,128)(2,1)S(1)}, u32[]{:S(2)}, u32[]{:S(2)}) collective-permute-start(bf16[3,2,128,256]{3,2,1,0:T(8,128)(2,1)S(1)} %get-tuple-element.155), channel_id=1, source_target_pairs={{0,12},{4,8},{8,4},{12,0},{16,28},{20,24},{24,20},{28,16},{1,13},{... | collective-permute-start | bytes 1179656 | tf_op jit(solution)/shard_map/ppermute | solution.py:70

commit v2 on v1

--- a/solution.py
+++ b/solution.py
@@ -86,36 +86,47 @@
     return [parts[mask] for mask in sorted(parts)]
 
 
-def section_kernel(where, state, slope, section, *chunks):
+def section_kernel(group, where, _, state, slope, *refs):
+    extra, section, chunks = refs[: -group - 1], refs[-group - 1], refs[-group:]
     value = (state[...].astype(f32) + (0.5 * step_size) * slope[...]).astype(bf16)
     section[...] = value
     width = chunks[0].shape[-1]
     for b, chunk in enumerate(chunks):
         columns = pl.ds(pl.multiple_of((where[0] ^ b) * width, 128), width)
         chunk[...] = section[:, :, :, columns]
-
-
-def make_section(p, split, state, prev_slope, place, group):
+    if extra:
+        source, target = extra
+
+        @pl.when(pl.program_id(0) == 0)
+        def _():
+            target[...] = source[...]
+
+
+def make_section(p, split, state, prev_slope, place, half_at, group, hamiltonian=None):
     ops, parts, rows, columns = state.shape
     height, width = rows // split, columns // group
-    block = pl.BlockSpec((1, parts, height, columns), lambda a, _: (a, 0, p, 0))
-    out = pl.BlockSpec((1, parts, height, columns), lambda a, _: (a, 0, 0, 0))
-    chunk = pl.BlockSpec((1, parts, height, width), lambda a, _: (a, 0, 0, 0))
-    section, *chunks = pl.pallas_call(
-        section_kernel,
+    block = pl.BlockSpec((1, parts, height, columns), lambda a, *_: (a, 0, p, 0))
+    out = pl.BlockSpec((1, parts, height, columns), lambda a, *_: (a, 0, 0, 0))
+    chunk = pl.BlockSpec((1, parts, height, width), lambda a, *_: (a, 0, 0, 0))
+    half = (2, rows, columns // 2)
+    extra = [] if hamiltonian is None else [hamiltonian]
+    return pl.pallas_call(
+        functools.partial(section_kernel, group),
         grid_spec=pltpu.PrefetchScalarGridSpec(
-            num_scalar_prefetch=1,
+            num_scalar_prefetch=2,
             grid=(ops,),
-            in_specs=[block, block],
-            out_specs=[out] + [chunk] * group,
-        ),
-        out_shape=[jax.ShapeDtypeStruct((ops, parts, height, columns), bf16)]
+            in_specs=[block, block] + [pl.BlockSpec(half, lambda a, _, h: (0, 0, h[0])) for _ in extra],
+            out_specs=[pl.BlockSpec(half, lambda a, *_: (0, 0, 0)) for _ in extra]
+            + [out]
+            + [chunk] * group,
+        ),
+        out_shape=[jax.ShapeDtypeStruct(half, bf16) for _ in extra]
+        + [jax.ShapeDtypeStruct((ops, parts, height, columns), bf16)]
         + [jax.ShapeDtypeStruct((ops, parts, height, width), bf16)] * group,
-        compiler_params=params(60 if p == 0 else 16),
+        compiler_params=params(54 if p == 0 else 16),
         cost_estimate=pl.CostEstimate(flops=1, bytes_accessed=1, transcendentals=0),
         name="section",
-    )(place, state, prev_slope)
-    return section, chunks
+    )(place, half_at, state, prev_slope, *extra)
 
 
 def fill_factors(vrows, vcols, coupling, factors):
@@ -149,21 +160,15 @@
 
 
 def partial_kernel(links, sides, group, places, coupling, vrows, vcols, *refs):
-    chunks, out, held, factors, sems = refs[:group], *refs[group:]
+    chunks, out, held, factors = refs[:group], *refs[group:]
     modes = vrows.shape[0]
     height, width = held.shape[2:]
     ops = chunks[0].shape[0]
     empty = group * ops
-    loads = [
-        pltpu.make_async_copy(chunk, held.at[pl.ds(b * ops, ops)], sems.at[b])
-        for b, chunk in enumerate(chunks)
-    ]
-    for load in loads:
-        load.start()
     fill_factors(vrows, vcols, coupling, factors)
+    for b, chunk in enumerate(chunks):
+        held[b * ops : (b + 1) * ops] = chunk[...]
     held[empty] = jnp.zeros(held.shape[1:], bf16)
-    for load in loads:
-        load.wait()
     for u, c in enumerate(sides):
 
         @pl.when(places[c] < empty)
@@ -183,28 +188,20 @@
 
 def coupled_kernel(links, sides, group, places, coupling, vrows, vcols, *refs):
     chunks, received, outs = refs[:group], refs[group], refs[group + 1 : 2 * group + 1]
-    held, done, factors, spots, sems = refs[2 * group + 1 :]
+    held, done, factors, spots = refs[2 * group + 1 :]
     modes = vrows.shape[0]
     height, width = held.shape[2:]
     ops = chunks[0].shape[0]
     empty = group * ops
-    loads = [
-        pltpu.make_async_copy(chunk, held.at[pl.ds(b * ops, ops)], sems.at[b])
-        for b, chunk in enumerate(chunks)
-    ]
-    loads.append(
-        pltpu.make_async_copy(received, held.at[pl.ds(empty + 1, len(sides))], sems.at[group])
-    )
-    for load in loads:
-        load.start()
     fill_factors(vrows, vcols, coupling, factors)
+    for b, chunk in enumerate(chunks):
+        held[b * ops : (b + 1) * ops] = chunk[...]
     held[empty] = jnp.zeros(held.shape[1:], bf16)
+    held[empty + 1 :] = received[...]
     for c in range(len(links)):
         spots[c] = places[c]
     for u, c in enumerate(sides):
         spots[c] = jnp.where(places[c] == empty, empty + 1 + u, places[c])
-    for load in loads:
-        load.wait()
     for c in range(len(links)):
 
         @pl.when(places[c] < empty)
@@ -221,14 +218,8 @@
                 done[places[c], 0, rows, :] = real.astype(bf16)
                 done[places[c], 1, rows, :] = imag.astype(bf16)
 
-    stores = [
-        pltpu.make_async_copy(done.at[pl.ds(b * ops, ops)], out, sems.at[group + 1 + b])
-        for b, out in enumerate(outs)
-    ]
-    for store in stores:
-        store.start()
-    for store in stores:
-        store.wait()
+    for b, out in enumerate(outs):
+        out[...] = done[b * ops : (b + 1) * ops]
 
 
 def coupling_scratch(entries, height, width, modes):
@@ -242,10 +233,10 @@
     size = height * width
     return pl.pallas_call(
         functools.partial(partial_kernel, links, sides, group),
-        in_specs=[scalars(), scalars()] + [whole()] * 2 + [anywhere()] * group,
+        in_specs=[scalars(), scalars()] + [whole()] * (2 + group),
         out_specs=whole(),
         out_shape=jax.ShapeDtypeStruct((len(sides), 2, height, width), bf16),
-        scratch_shapes=held + factors + [pltpu.SemaphoreType.DMA((group,))],
+        scratch_shapes=held + factors,
         compiler_params=params(12),
         cost_estimate=pl.CostEstimate(
             flops=40 * len(sides) * size,
@@ -263,13 +254,13 @@
     size = height * width
     return pl.pallas_call(
         functools.partial(coupled_kernel, links, sides, group),
-        in_specs=[scalars(), scalars()] + [whole()] * 2 + [anywhere()] * (1 + group),
-        out_specs=[anywhere()] * group,
+        in_specs=[scalars(), scalars()] + [whole()] * (3 + group),
+        out_specs=[whole()] * group,
         out_shape=[jax.ShapeDtypeStruct(chunks[0].shape, bf16)] * group,
         scratch_shapes=held
         + [pltpu.VMEM((group * ops, 2, height, width), bf16)]
         + factors
-        + [pltpu.SMEM((len(links),), jnp.int32), pltpu.SemaphoreType.DMA((2 * group + 1,))],
+        + [pltpu.SMEM((len(links),), jnp.int32)],
         compiler_params=params(16),
         cost_estimate=pl.CostEstimate(flops=1, bytes_accessed=1, transcendentals=0),
         name="coupling_sums",
@@ -472,17 +463,19 @@
 
     got, sent, received, sums, outs = [], [], [], [], []
 
-    first, first_chunks = make_section(0, split, state, prev_slope, own_place, group)
-    first, first_chunks, occupation, state, prev_slope, couple_v, hamiltonian = tie(
-        (first, first_chunks, occupation, state, prev_slope, couple_v, hamiltonian)
+    half = [occupation] + [swap(occupation, "hier", hier, b) for b in range(1, group)]
+    half_at = (row_at // (row // 2)).reshape(1).astype(jnp.int32)
+    half_columns, first, *first_chunks = make_section(
+        0, split, state, prev_slope, own_place, half_at, group, hamiltonian
     )
-    half = [occupation] + [swap(occupation, "hier", hier, b) for b in range(1, group)]
-
-    half_columns = lax.dynamic_slice_in_dim(
-        hamiltonian, row_at // (row // 2) * (columns // 2), columns // 2, 2
+    half_columns, first, first_chunks, half, state, prev_slope, couple_v, hamiltonian = tie(
+        (half_columns, first, first_chunks, half, state, prev_slope, couple_v, hamiltonian)
     )
+
     h_top = swap(half_columns, "row", row, top)
-    second, second_chunks = make_section(1, split, state, prev_slope, own_place, group)
+    second, *second_chunks = make_section(
+        1, split, state, prev_slope, own_place, half_at, group
+    )
     chunks, sections = [first_chunks, second_chunks], [first, second]
     got.append(spread(0))
 
@@ -518,12 +511,11 @@
     sums.append(gather_back(done))
     base = make_right(sections, hamiltonian, near[1:], h_far, row_place, decay)
     base = make_left([sections[0], *near[1:], *s_far], h_columns[0], base, row_place)
-    received, last_across, sums, base, sections = tie(
-        (received, last_across, sums, base, sections)
-    )
-
-    s_parts = tree(sections[1], row, low) + tree(last_across, row, low)
-    sums.append(gather_back(coupled(1)))
+    received, last_across, base = tie((received, last_across, base))
+
+    done, sums, last_across, last_own = tie((coupled(1), sums, last_across, sections[1]))
+    sums.append(gather_back(done))
+    s_parts = tree(last_own, row, low) + tree(last_across, row, low)
     base = make_left(s_parts, h_columns[1], base, row_place)
     for p in range(split):
         outs = make_final(p, split, base, accumulated, sums[p], own_place, outs)

time: 158 us -> 149 us (0.943)
  waiting for transfers between devices: 53.6 us -> 42.2 us
  local copies, waits for them, and re-layouts: 15.9 us -> 22.7 us
  Pallas kernels: 56.5 us -> 52.8 us
  other arithmetic: 3.67 us -> 1.87 us
    ppermute x25, waiting for transfers between devices: 53.6 us -> 42.2 us  [swap(): return lax.ppermute(array, axis, [(i, i ^ bit) for i in range(size)])]
    unnamed x34 -> x48, local copies, waits for them, and re-layouts: 2.85 us -> 5.96 us
    another operation x2, local copies, waits for them, and re-layouts: 1.44 us -> 4.1 us  [shards(): blocks[:, :, :, p].reshape(2, rows, row * height)]
    pallas_call x2, Pallas kernels: 10.5 us -> 8.44 us  [make_coupled(): pl.pallas_call(functools.partial(coupled_kernel, links, sides, group), in...]
    slice x1, local copies, waits for them, and re-layouts: 6.6 us -> 8.67 us  [shards(): blocks[:, :, :, p].reshape(2, rows, row * height)]
    dynamic_slice x1 -> x0, local copies, waits for them, and re-layouts: 1.87 us -> none  [shards(): lax.dynamic_slice_in_dim(hamiltonian, row_at // (row // 2) * (columns //...]
    concatenate x1, other arithmetic: 1.9 us -> 0.24 us  [shards(): jnp.concatenate([sections[0].reshape(-1, columns), kept.reshape(-1, colum...]
  transfers between devices with their start and end apart: 25 -> 25, of which waited for: 6 -> 8; matrix products, arithmetic and copies ran while one was open for 11% -> 13% of each run, Pallas kernels for 30% -> 33%
where the time goes in v2:
time: 149 us; the launch traced here: 148 us
  Pallas kernels  52.8 us (35%)
  waiting for transfers between devices  42.2 us (28%)
  starting transfers between devices  28 us (19%)
  local copies, waits for them, and re-layouts  22.7 us (15%)
  other arithmetic  1.87 us (1%)
    ppermute x25, waiting for transfers between devices, swap(): return lax.ppermute(array, axis, [(i, i ^ bit) for i in range(size)])  42.2 us
    ppermute x25, starting transfers between devices, swap(): return lax.ppermute(array, axis, [(i, i ^ bit) for i in range(size)])  28 us
    pallas_call x2, Pallas kernels, make_left(): pl.pallas_call(functools.partial(left_kernel, count), grid=(columns // ti...  13 us
    pallas_call x1, Pallas kernels, make_right(): pl.pallas_call(functools.partial(right_kernel, split, count), grid=(colum...  10.4 us
    slice x1, local copies, waits for them, and re-layouts, shards(): blocks[:, :, :, p].reshape(2, rows, row * height)  8.67 us
    pallas_call x2, Pallas kernels, make_coupled(): pl.pallas_call(functools.partial(coupled_kernel, links, sides, group), in...  8.44 us
    pallas_call x2, Pallas kernels, make_final(): pl.pallas_call(functools.partial(final_kernel, group), grid_spec=pltpu.Pr...  7.92 us
    pallas_call x2, Pallas kernels, make_section(): pl.pallas_call(functools.partial(section_kernel, group), grid_spec=pltpu....  7.69 us
  transfers between devices with their start and end apart: 25, of which 8 were waited for; matrix products, arithmetic and copies ran while one was open for 13% of the time, Pallas kernels for 33%

profile of v2, /device:TPU:0, one launch (start us, length us, event | category | flops | bytes accessed | tf_op | source)
XLA Modules:
  0.0 148.5 jit_solution(1146807072039476130)
XLA Ops:
  0.6 3.1 %collective-permute-start.1 = (s32[3,6]{1,0:T(4,128)}, s32[3,6]{1,0:T(4,128)S(1)}, u32[]{:S(2)}, u32[]{:S(2)}) collective-permute-start(s32[3,6]{1,0:T(4,128)} %param.18), channel_id=1, source_target_pairs={{0,8},{4,12},{8,0},{12,4},{16,24},{20,28},{24,16},{28,20},{1,9},{5... | collective-permute-start | bytes 224 | tf_op jit(solution)/shard_map/ppermute | solution.py:70
  3.7 1.5 %collective-permute-start = (s32[3,6]{1,0:T(4,128)}, s32[3,6]{1,0:T(4,128)S(1)}, u32[]{:S(2)}, u32[]{:S(2)}) collective-permute-start(s32[3,6]{1,0:T(4,128)} %param.18), channel_id=1, source_target_pairs={{0,4},{4,0},{8,12},{12,8},{16,20},{20,16},{24,28},{28,24},{1,5},{5... | collective-permute-start | bytes 224 | tf_op jit(solution)/shard_map/ppermute | solution.py:70
  5.2 0.1 collective-permute-start.2
  5.3 6.4 %section.2 = (bf16[2,256,512]{2,1,0:T(8,128)(2,1)}, bf16[3,2,128,1024]{3,2,1,0:T(8,128)(2,1)}, bf16[3,2,128,256]{3,2,1,0:T(8,128)(2,1)}, bf16[3,2,128,256]{3,2,1...) custom-call(s32[1]{0:T(128)} %bitcast.where, s32[1]{0:T(128)} %bitcast.2._, ...), custom_call_target="tpu_custom_call" | custom-call | flops 1 | bytes 1 | tf_op jit(solution)/shard_map/section/pallas_call | solution.py:113
  11.7 0.0 collective-permute-done.1
  11.7 0.0 collective-permute-done.2
  11.7 0.5 copy-done.18
  12.3 0.0 copy-done.19
  12.3 0.0 copy-done.20
  12.3 1.9 %collective-permute-start.6 = (bf16[2,256,512]{2,1,0:T(8,128)(2,1)}, bf16[2,256,512]{2,1,0:T(8,128)(2,1)}, u32[]{:S(2)}, u32[]{:S(2)}) collective-permute-start(bf16[2,256,512]{2,1,0:T(8,128)(2,1)} %get-tuple-element.115), channel_id=1, source_target_pairs={{0,2},{1,3},{2,0},{3,1},{4,6},{5,7},{6,4},{7,5},{8,10},{9,11},{10,... | collective-permute-start | bytes 1572872 | tf_op jit(solution)/shard_map/ppermute | solution.py:70
  14.2 0.6 fusion
  14.8 1.5 %collective-permute-start.3 = (bf16[3,2,128,256]{3,2,1,0:T(8,128)(2,1)}, bf16[3,2,128,256]{3,2,1,0:T(8,128)(2,1)}, u32[]{:S(2)}, u32[]{:S(2)}) collective-permute-start(bf16[3,2,128,256]{3,2,1,0:T(8,128)(2,1)} %get-tuple-element.99), channel_id=1, source_target_pairs={{0,4},{4,0},{8,12},{12,8},{16,20},{20,16},{24,28},{28,24},{1,5},{5... | collective-permute-start | bytes 1179656 | tf_op jit(solution)/shard_map/ppermute | solution.py:70
  16.3 1.6 %collective-permute-start.4 = (bf16[3,2,128,256]{3,2,1,0:T(8,128)(2,1)}, bf16[3,2,128,256]{3,2,1,0:T(8,128)(2,1)}, u32[]{:S(2)}, u32[]{:S(2)}) collective-permute-start(bf16[3,2,128,256]{3,2,1,0:T(8,128)(2,1)} %get-tuple-element.100), channel_id=1, source_target_pairs={{0,8},{4,12},{8,0},{12,4},{16,24},{20,28},{24,16},{28,20},{1,9},{5... | collective-permute-start | bytes 1179656 | tf_op jit(solution)/shard_map/ppermute | solution.py:70
  17.9 0.4 collective-permute-start.5
  18.3 0.1 multiply_reduce_fusion.decay
  18.4 0.0 copy-start.12
  18.4 1.3 section.3
  19.7 0.8 copy-done.6
  20.5 1.1 copy-done.10
  21.7 0.8 copy-done.13
  22.5 0.8 copy-done.14
  23.3 0.8 copy-done.15
  24.1 0.9 copy.24.vrows
  25.0 0.9 copy.23.vrows
  25.9 0.7 pad_add_fusion
  26.6 0.8 compare_reduce_fusion
  27.4 0.0 collective-permute-done.3.refs_1_
  27.4 1.2 collective-permute-done.4.refs_2_
  28.7 5.8 %collective-permute-done.5.refs_3_ = bf16[3,2,128,256]{3,2,1,0:T(8,128)(2,1)} collective-permute-done((bf16[3,2,128,256]{3,2,1,0:T(8,128)(2,1)}, bf16[3,2,128,256]{3,2,1,0:T(8,128)(2,1)}, u32[]{:S(2)}, u32[]{:S(2)}) %collective-permute-start.5) | collective-permute-done | bytes 393248 | tf_op jit(solution)/shard_map/ppermute | solution.py:70
  34.5 0.4 collective-permute-start.11
  34.9 1.0 copy-done.8
  35.9 3.1 %partial_sums.2 = bf16[6,2,128,256]{3,2,1,0:T(8,128)(2,1)} custom-call(s32[24]{0:T(128)S(1)} %select_reduce_fusion.places, f32[2,6]{1,0:T(2,128)S(1)} %copy-done.12, f32[6,128,1]{2,1,0:T(8,128)S(1)} %copy.23.vrows, f32[6,256]{1,0:T(8,128)S(1)} %get-tuple-element.127.vcols, bf16[3,2,128,256]{3,2,1,0:T(8,128)(2,1)S(1)} %copy-done.8, ...), custom_call_target="tpu_custom_call" | custom-call | flops 7864320 | bytes 2359296 | tf_op jit(solution)/shard_map/partial_sums/pallas_call | solution.py:234
  39.0 3.1 %collective-permute-start.10 = (bf16[6,2,128,256]{3,2,1,0:T(8,128)(2,1)}, bf16[6,2,128,256]{3,2,1,0:T(8,128)(2,1)}, u32[]{:S(2)}, u32[]{:S(2)}) collective-permute-start(bf16[6,2,128,256]{3,2,1,0:T(8,128)(2,1)} %partial_sums.2), channel_id=1, source_target_pairs={{0,16},{4,20},{8,24},{12,28},{16,0},{20,4},{24,8},{28,12},{1,17},{... | collective-permute-start | bytes 2359304 | tf_op jit(solution)/shard_map/ppermute | solution.py:70
  42.0 1.5 %collective-permute-start.7 = (bf16[3,2,128,256]{3,2,1,0:T(8,128)(2,1)}, bf16[3,2,128,256]{3,2,1,0:T(8,128)(2,1)}, u32[]{:S(2)}, u32[]{:S(2)}) collective-permute-start(bf16[3,2,128,256]{3,2,1,0:T(8,128)(2,1)} %copy-done.15), channel_id=1, source_target_pairs={{0,4},{4,0},{8,12},{12,8},{16,20},{20,16},{24,28},{28,24},{1,5},{5... | collective-permute-start | bytes 1179656 | tf_op jit(solution)/shard_map/ppermute | solution.py:70
  43.5 1.6 %collective-permute-start.8 = (bf16[3,2,128,256]{3,2,1,0:T(8,128)(2,1)}, bf16[3,2,128,256]{3,2,1,0:T(8,128)(2,1)}, u32[]{:S(2)}, u32[]{:S(2)}) collective-permute-start(bf16[3,2,128,256]{3,2,1,0:T(8,128)(2,1)} %copy-done.14), channel_id=1, source_target_pairs={{0,8},{4,12},{8,0},{12,4},{16,24},{20,28},{24,16},{28,20},{1,9},{5... | collective-permute-start | bytes 1179656 | tf_op jit(solution)/shard_map/ppermute | solution.py:70
  45.1 0.4 collective-permute-start.9
  45.5 1.5 %reshape.30 = bf16[2,256,4,2,128]{4,3,2,1,0:T(2,128)(2,1)} reshape(bf16[2,256,1024]{2,1,0:T(8,128)(2,1)S(1)} %copy-done.2) | data formatting | bytes 2097152 | tf_op jit(solution)/shard_map/reshape | solution.py:500
  47.1 8.7 %slice_reduce_fusion = (bf16[2,256,4,128]{3,2,1,0:T(4,128)(2,1)}, bf16[2,256,4,128]{3,2,1,0:T(4,128)(2,1)}) fusion(bf16[2,256,4,2,128]{4,3,2,1,0:T(2,128)(2,1)} %reshape.30), kind=kLoop, calls=%fused_computation.1 | loop fusion | bytes 2097152 | tf_op jit(solution)/shard_map/slice | solution.py:501
  55.8 2.0 %reshape_squeeze.7.h_own = bf16[2,256,512]{2,1,0:T(8,128)(2,1)} reshape(bf16[2,256,4,128]{3,2,1,0:T(4,128)(2,1)} %get-tuple-element.182) | data formatting | bytes 1048576 | tf_op jit(solution)/shard_map/reshape;squeeze | solution.py:501
  57.8 2.0 %reshape_squeeze.6.h_own = bf16[2,256,512]{2,1,0:T(8,128)(2,1)} reshape(bf16[2,256,4,128]{3,2,1,0:T(4,128)(2,1)} %get-tuple-element.183) | data formatting | bytes 1048576 | tf_op jit(solution)/shard_map/reshape;squeeze | solution.py:501
  59.9 0.2 pad_maximum_fusion
  60.1 8.7 %collective-permute-done.8.refs_2_ = bf16[3,2,128,256]{3,2,1,0:T(8,128)(2,1)} collective-permute-done((bf16[3,2,128,256]{3,2,1,0:T(8,128)(2,1)}, bf16[3,2,128,256]{3,2,1,0:T(8,128)(2,1)}, u32[]{:S(2)}, u32[]{:S(2)}) %collective-permute-start.8) | collective-permute-done | bytes 393248 | tf_op jit(solution)/shard_map/ppermute | solution.py:70
  68.8 6.9 %collective-permute-done.9.refs_3_ = bf16[3,2,128,256]{3,2,1,0:T(8,128)(2,1)} collective-permute-done((bf16[3,2,128,256]{3,2,1,0:T(8,128)(2,1)}, bf16[3,2,128,256]{3,2,1,0:T(8,128)(2,1)}, u32[]{:S(2)}, u32[]{:S(2)}) %collective-permute-start.9) | collective-permute-done | bytes 393248 | tf_op jit(solution)/shard_map/ppermute | solution.py:70
  75.7 0.5 collective-permute-start.15
  76.2 1.5 %collective-permute-start.13 = (bf16[3,2,128,1024]{3,2,1,0:T(8,128)(2,1)S(1)}, bf16[3,2,128,1024]{3,2,1,0:T(8,128)(2,1)S(1)}, u32[]{:S(2)}, u32[]{:S(2)}) collective-permute-start(bf16[3,2,128,1024]{3,2,1,0:T(8,128)(2,1)S(1)} %copy-done.11), channel_id=1, source_target_pairs={{0,2},{1,3},{2,0},{3,1},{4,6},{5,7},{6,4},{7,5},{8,10},{9,11},{10,... | collective-permute-start | bytes 4718600 | tf_op jit(solution)/shard_map/ppermute | solution.py:70
  77.7 2.2 %partial_sums.3 = bf16[6,2,128,256]{3,2,1,0:T(8,128)(2,1)S(1)} custom-call(s32[24]{0:T(128)S(1)} %select_reduce_fusion.places, f32[2,6]{1,0:T(2,128)S(1)} %copy-done.12, f32[6,128,1]{2,1,0:T(8,128)S(1)} %copy.24.vrows, f32[6,256]{1,0:T(8,128)S(1)} %get-tuple-element.127.vcols, bf16[3,2,128,256]{3,2,1,0:T(8,128)(2,1)S(1)} %copy-done.7, ...), custom_call_target="tpu_custom_call" | custom-call | flops 7864320 | bytes 2359296 | tf_op jit(solution)/shard_map/partial_sums/pallas_call | solution.py:234
  79.9 1.5 collective-permute-start.12
  81.4 4.4 %coupling_sums.2 = (bf16[3,2,128,256]{3,2,1,0:T(8,128)(2,1)S(1)}, bf16[3,2,128,256]{3,2,1,0:T(8,128)(2,1)S(1)}, bf16[3,2,128,256]{3,2,1,0:T(8,128)(2,1)S(1)}, bf16[3,2,128,256]{3,2,1,0:T(8,128)(2,1)S(1)}) custom-call(s32[24]{0:T(128)S(1)} %select_reduce_fusion.places, f32[2,6]{1,0:T(2,128)S(1)} %copy-done.12, f32[6,128,1]{2,1,0:T(8,128)S(1)} %copy.23.vrows, ...), custom_call_target="tpu_custom_call" | custom-call | flops 1 | bytes 1 | tf_op jit(solution)/shard_map/coupling_sums/pallas_call | solution.py:255
  85.8 0.6 collective-permute-start.17
  86.4 2.9 %collective-permute-start.18 = (bf16[3,2,128,256]{3,2,1,0:T(8,128)(2,1)S(1)}, bf16[3,2,128,256]{3,2,1,0:T(8,128)(2,1)S(1)}, u32[]{:S(2)}, u32[]{:S(2)}) collective-permute-start(bf16[3,2,128,256]{3,2,1,0:T(8,128)(2,1)S(1)} %get-tuple-element.167), channel_id=1, source_target_pairs={{0,8},{4,12},{8,0},{12,4},{16,24},{20,28},{24,16},{28,20},{1,9},{5... | collective-permute-start | bytes 1179656 | tf_op jit(solution)/shard_map/ppermute | solution.py:70
  89.3 0.1 collective-permute-start.19
  89.4 10.4 %right_products.1.base = f32[3,2,256,1024]{3,2,1,0:T(8,128)S(1)} custom-call(s32[1]{0:T(128)} %bitcast.1.where, f32[3]{0:T(128)S(1)} %multiply_reduce_fusion.decay, bf16[2,256,1024]{2,1,0:T(8,128)(2,1)S(1)} %copy-done.2, bf16[3,2,128,1024]{3,2,1,0:T(8,128)(2,1)S(1)} %copy-done.3, bf16[3,2,128,1024]{3,2,1,0:T(8,128)(2,1)S(1)} %copy-done.11, ...), custom_call_target="tpu_custom_call" | custom-call | flops 6442450944 | bytes 13631488 | tf_op jit(solution)/shard_map/right_products/pallas_call | solution.py:318
  99.8 6.9 %left_products.2.base = f32[3,2,256,1024]{3,2,1,0:T(8,128)S(1)} custom-call(s32[1]{0:T(128)} %bitcast.1.where, bf16[2,256,512]{2,1,0:T(8,128)(2,1)S(1)} %copy-done.5, f32[3,2,256,1024]{3,2,1,0:T(8,128)S(1)} %right_products.1.base, bf16[3,2,128,1024]{3,2,1,0:T(8,128)(2,1)S(1)} %copy-done.3, ...), custom_call_target="tpu_custom_call" | custom-call | flops 3221225472 | bytes 18874368 | tf_op jit(solution)/shard_map/left_products/pallas_call | solution.py:354
  106.7 11.1 %collective-permute-done.12.refs_4_ = bf16[6,2,128,256]{3,2,1,0:T(8,128)(2,1)S(1)} collective-permute-done((bf16[6,2,128,256]{3,2,1,0:T(8,128)(2,1)S(1)}, bf16[6,2,128,256]{3,2,1,0:T(8,128)(2,1)S(1)}, u32[]{:S(2)}, u32[]{:S(2)}) %collective-permute-start.12) | collective-permute-done | bytes 786464 | tf_op jit(solution)/shard_map/ppermute | solution.py:70
  117.8 4.1 %coupling_sums.3 = (bf16[3,2,128,256]{3,2,1,0:T(8,128)(2,1)S(1)}, bf16[3,2,128,256]{3,2,1,0:T(8,128)(2,1)S(1)}, bf16[3,2,128,256]{3,2,1,0:T(8,128)(2,1)S(1)}, bf16[3,2,128,256]{3,2,1,0:T(8,128)(2,1)S(1)}) custom-call(s32[24]{0:T(128)S(1)} %select_reduce_fusion.places, f32[2,6]{1,0:T(2,128)S(1)} %copy-done.12, f32[6,128,1]{2,1,0:T(8,128)S(1)} %copy.24.vrows, ...), custom_call_target="tpu_custom_call" | custom-call | flops 1 | bytes 1 | tf_op jit(solution)/shard_map/coupling_sums/pallas_call | solution.py:255
  121.9 1.5 collective-permute-done.19.refs_3_
  123.4 0.5 collective-permute-start.21
  123.9 1.2 collective-permute-start.22
  125.1 2.3 %collective-permute-start.24 = (bf16[3,2,128,256]{3,2,1,0:T(8,128)(2,1)S(1)}, bf16[3,2,128,256]{3,2,1,0:T(8,128)(2,1)S(1)}, u32[]{:S(2)}, u32[]{:S(2)}) collective-permute-start(bf16[3,2,128,256]{3,2,1,0:T(8,128)(2,1)S(1)} %get-tuple-element.175), channel_id=1, source_target_pairs={{0,12},{4,8},{8,4},{12,0},{16,28},{20,24},{24,20},{28,16},{1,13},{... | collective-permute-start | bytes 1179656 | tf_op jit(solution)/shard_map/ppermute | solution.py:70
  127.4 1.7 %collective-permute-done.21.refs_3_ = bf16[3,2,128,1024]{3,2,1,0:T(8,128)(2,1)S(1)} collective-permute-done((bf16[3,2,128,1024]{3,2,1,0:T(8,128)(2,1)S(1)}, bf16[3,2,128,1024]{3,2,1,0:T(8,128)(2,1)S(1)}, u32[]{:S(2)}, u32[]{:S(2)}) %collective-permute-start.21) | collective-permute-done | bytes 1572896 | tf_op jit(solution)/shard_map/ppermute | solution.py:70
  129.0 6.1 %left_products.3.base = f32[3,2,256,1024]{3,2,1,0:T(8,128)S(1)} custom-call(s32[1]{0:T(128)} %bitcast.1.where, bf16[2,256,512]{2,1,0:T(8,128)(2,1)S(1)} %copy-done.4, f32[3,2,256,1024]{3,2,1,0:T(8,128)S(1)} %left_products.2.base, bf16[3,2,128,1024]{3,2,1,0:T(8,128)(2,1)S(1)} %copy-done.11, bf16[3,2,128,1024]{3,2,1,0:T(8,128)(2,1)S(1)} %collective-permute-done.20.refs_1_, ...), custom_call_target="tpu_custom_call" | custom-call | flops 3221225472 | bytes 18874368 | tf_op jit(solution)/shard_map/left_products/pallas_call | solution.py:354
  135.2 4.0 %outputs.2 = (f32[3,2,256,1024]{3,2,1,0:T(8,128)}, f32[3,2,256,1024]{3,2,1,0:T(8,128)}) custom-call(s32[1]{0:T(128)} %bitcast.where, f32[3,2,256,1024]{3,2,1,0:T(8,128)S(1)} %left_products.3.base, f32[3,2,256,1024]{3,2,1,0:T(8,128)S(1)} %bitcast.8, bf16[3,2,128,256]{3,2,1,0:T(8,128)(2,1)S(1)} %get-tuple-element.176.refs_0_, ...), custom_call_target="tpu_custom_call" | custom-call | flops 3145728 | bytes 14155776 | tf_op jit(solution)/shard_map/outputs/pallas_call | solution.py:402
  139.2 5.4 %collective-permute-done.24.refs_3_ = bf16[3,2,128,256]{3,2,1,0:T(8,128)(2,1)S(1)} collective-permute-done((bf16[3,2,128,256]{3,2,1,0:T(8,128)(2,1)S(1)}, bf16[3,2,128,256]{3,2,1,0:T(8,128)(2,1)S(1)}, u32[]{:S(2)}, u32[]{:S(2)}) %collective-permute-start.24) | collective-permute-done | bytes 393248 | tf_op jit(solution)/shard_map/ppermute | solution.py:70
  144.5 3.9 %outputs.3 = (f32[3,2,256,1024]{3,2,1,0:T(8,128)}, f32[3,2,256,1024]{3,2,1,0:T(8,128)}) custom-call(s32[1]{0:T(128)} %bitcast.where, f32[3,2,256,1024]{3,2,1,0:T(8,128)S(1)} %left_products.3.base, f32[3,2,256,1024]{3,2,1,0:T(8,128)S(1)} %bitcast.8, ...), custom_call_target="tpu_custom_call", output_to_operand_aliasing={{0}: (7, {}), {1}: (8, {})} | custom-call | flops 3145728 | bytes 14155776 | tf_op jit(solution)/shard_map/outputs/pallas_call | solution.py:402
  (59 shorter events, 0.1 us)
Async XLA Ops:
  0.6 11.1 %collective-permute-start.1 = (s32[3,6]{1,0:T(4,128)}, s32[3,6]{1,0:T(4,128)S(1)}, u32[]{:S(2)}, u32[]{:S(2)}) collective-permute-start(s32[3,6]{1,0:T(4,128)} %param.18), channel_id=1, source_target_pairs={{0,8},{4,12},{8,0},{12,4},{16,24},{20,28},{24,16},{28,20},{1,9},{5... | collective-permute-start | bytes 224 | tf_op jit(solution)/shard_map/ppermute | solution.py:70
  3.7 8.0 %collective-permute-start = (s32[3,6]{1,0:T(4,128)}, s32[3,6]{1,0:T(4,128)S(1)}, u32[]{:S(2)}, u32[]{:S(2)}) collective-permute-start(s32[3,6]{1,0:T(4,128)} %param.18), channel_id=1, source_target_pairs={{0,4},{4,0},{8,12},{12,8},{16,20},{20,16},{24,28},{28,24},{1,5},{5... | collective-permute-start | bytes 224 | tf_op jit(solution)/shard_map/ppermute | solution.py:70
  5.2 6.5 %collective-permute-start.2 = (s32[3,6]{1,0:T(4,128)}, s32[3,6]{1,0:T(4,128)S(1)}, u32[]{:S(2)}, u32[]{:S(2)}) collective-permute-start(s32[3,6]{1,0:T(4,128)} %param.18), channel_id=1, source_target_pairs={{0,12},{4,8},{8,4},{12,0},{16,28},{20,24},{24,20},{28,16},{1,13},{... | collective-permute-start | bytes 224 | tf_op jit(solution)/shard_map/ppermute | solution.py:70
  5.3 8.9 %copy-start.16 = (f32[6,1024]{1,0:T(8,128)S(1)}, f32[6,1024]{1,0:T(8,128)}, u32[]{:S(2)}) copy-start(f32[6,1024]{1,0:T(8,128)} %param.15) | copy-start | bytes 73732
  5.3 13.0 %copy-start.17 = (s32[3,6]{1,0:T(4,128)S(1)}, s32[3,6]{1,0:T(4,128)}, u32[]{:S(2)}) copy-start(s32[3,6]{1,0:T(4,128)} %param.18) | copy-start | bytes 220
  5.3 13.0 %copy-start.21 = (f32[6]{0:T(128)S(1)}, f32[6]{0:T(128)}, u32[]{:S(2)}) copy-start(f32[6]{0:T(128)} %param.17) | copy-start | bytes 76
  5.3 13.2 %copy-start = (f32[3,2,256,1024]{3,2,1,0:T(8,128)S(1)}, f32[3,2,256,1024]{3,2,1,0:T(8,128)}, u32[]{:S(2)}) copy-start(f32[3,2,256,1024]{3,2,1,0:T(8,128)} %slope.2) | copy-start | bytes 18874372
  5.3 13.2 %copy-start.1 = (bf16[3,2,256,1024]{3,2,1,0:T(8,128)(2,1)S(1)}, bf16[3,2,256,1024]{3,2,1,0:T(8,128)(2,1)}, u32[]{:S(2)}) copy-start(bf16[3,2,256,1024]{3,2,1,0:T(8,128)(2,1)} %state.2) | copy-start | bytes 9437188
  11.7 0.6 copy-start.18
  11.7 0.6 copy-start.19
  11.7 0.6 copy-start.20
  12.3 22.2 %collective-permute-start.6 = (bf16[2,256,512]{2,1,0:T(8,128)(2,1)}, bf16[2,256,512]{2,1,0:T(8,128)(2,1)}, u32[]{:S(2)}, u32[]{:S(2)}) collective-permute-start(bf16[2,256,512]{2,1,0:T(8,128)(2,1)} %get-tuple-element.115), channel_id=1, source_target_pairs={{0,2},{1,3},{2,0},{3,1},{4,6},{5,7},{6,4},{7,5},{8,10},{9,11},{10,... | collective-permute-start | bytes 1572872 | tf_op jit(solution)/shard_map/ppermute | solution.py:70
  14.8 12.6 %collective-permute-start.3 = (bf16[3,2,128,256]{3,2,1,0:T(8,128)(2,1)}, bf16[3,2,128,256]{3,2,1,0:T(8,128)(2,1)}, u32[]{:S(2)}, u32[]{:S(2)}) collective-permute-start(bf16[3,2,128,256]{3,2,1,0:T(8,128)(2,1)} %get-tuple-element.99), channel_id=1, source_target_pairs={{0,4},{4,0},{8,12},{12,8},{16,20},{20,16},{24,28},{28,24},{1,5},{5... | collective-permute-start | bytes 1179656 | tf_op jit(solution)/shard_map/ppermute | solution.py:70
  16.3 12.4 %collective-permute-start.4 = (bf16[3,2,128,256]{3,2,1,0:T(8,128)(2,1)}, bf16[3,2,128,256]{3,2,1,0:T(8,128)(2,1)}, u32[]{:S(2)}, u32[]{:S(2)}) collective-permute-start(bf16[3,2,128,256]{3,2,1,0:T(8,128)(2,1)} %get-tuple-element.100), channel_id=1, source_target_pairs={{0,8},{4,12},{8,0},{12,4},{16,24},{20,28},{24,16},{28,20},{1,9},{5... | collective-permute-start | bytes 1179656 | tf_op jit(solution)/shard_map/ppermute | solution.py:70
  17.9 16.6 %collective-permute-start.5 = (bf16[3,2,128,256]{3,2,1,0:T(8,128)(2,1)}, bf16[3,2,128,256]{3,2,1,0:T(8,128)(2,1)}, u32[]{:S(2)}, u32[]{:S(2)}) collective-permute-start(bf16[3,2,128,256]{3,2,1,0:T(8,128)(2,1)} %get-tuple-element.101), channel_id=1, source_target_pairs={{0,12},{4,8},{8,4},{12,0},{16,28},{20,24},{24,20},{28,16},{1,13},{... | collective-permute-start | bytes 1179656 | tf_op jit(solution)/shard_map/ppermute | solution.py:70
  18.4 16.5 %copy-start.12 = (f32[2,6]{1,0:T(2,128)S(1)}, f32[2,6]{1,0:T(2,128)}, u32[]{:S(2)}) copy-start(f32[2,6]{1,0:T(2,128)} %coupling.7) | copy-start | bytes 148
  19.7 0.8 copy-start.6
  20.5 1.1 copy-start.10
  21.7 0.8 copy-start.13
  22.5 0.8 copy-start.14
  23.3 0.8 copy-start.15
  24.1 21.5 %copy-start.2 = (bf16[2,256,1024]{2,1,0:T(8,128)(2,1)S(1)}, bf16[2,256,1024]{2,1,0:T(8,128)(2,1)}, u32[]{:S(2)}) copy-start(bf16[2,256,1024]{2,1,0:T(8,128)(2,1)} %h_own) | copy-start | bytes 3145732
  34.5 41.2 %collective-permute-start.11 = (bf16[3,2,128,1024]{3,2,1,0:T(8,128)(2,1)}, bf16[3,2,128,1024]{3,2,1,0:T(8,128)(2,1)}, u32[]{:S(2)}, u32[]{:S(2)}) collective-permute-start(bf16[3,2,128,1024]{3,2,1,0:T(8,128)(2,1)} %get-tuple-element.142.refs_0_), channel_id=1, source_target_pairs={{0,2},{1,3},{2,0},{3,1},{4,6},{5,7},{6,4},{7,5},{8,10},{9,11},{10,... | collective-permute-start | bytes 4718600 | tf_op jit(solution)/shard_map/ppermute | solution.py:70
  34.9 1.0 copy-start.8
  39.0 36.7 %collective-permute-start.10 = (bf16[6,2,128,256]{3,2,1,0:T(8,128)(2,1)}, bf16[6,2,128,256]{3,2,1,0:T(8,128)(2,1)}, u32[]{:S(2)}, u32[]{:S(2)}) collective-permute-start(bf16[6,2,128,256]{3,2,1,0:T(8,128)(2,1)} %partial_sums.2), channel_id=1, source_target_pairs={{0,16},{4,20},{8,24},{12,28},{16,0},{20,4},{24,8},{28,12},{1,17},{... | collective-permute-start | bytes 2359304 | tf_op jit(solution)/shard_map/ppermute | solution.py:70
  42.0 18.1 %collective-permute-start.7 = (bf16[3,2,128,256]{3,2,1,0:T(8,128)(2,1)}, bf16[3,2,128,256]{3,2,1,0:T(8,128)(2,1)}, u32[]{:S(2)}, u32[]{:S(2)}) collective-permute-start(bf16[3,2,128,256]{3,2,1,0:T(8,128)(2,1)} %copy-done.15), channel_id=1, source_target_pairs={{0,4},{4,0},{8,12},{12,8},{16,20},{20,16},{24,28},{28,24},{1,5},{5... | collective-permute-start | bytes 1179656 | tf_op jit(solution)/shard_map/ppermute | solution.py:70
  43.5 25.2 %collective-permute-start.8 = (bf16[3,2,128,256]{3,2,1,0:T(8,128)(2,1)}, bf16[3,2,128,256]{3,2,1,0:T(8,128)(2,1)}, u32[]{:S(2)}, u32[]{:S(2)}) collective-permute-start(bf16[3,2,128,256]{3,2,1,0:T(8,128)(2,1)} %copy-done.14), channel_id=1, source_target_pairs={{0,8},{4,12},{8,0},{12,4},{16,24},{20,28},{24,16},{28,20},{1,9},{5... | collective-permute-start | bytes 1179656 | tf_op jit(solution)/shard_map/ppermute | solution.py:70
  45.1 30.6 %collective-permute-start.9 = (bf16[3,2,128,256]{3,2,1,0:T(8,128)(2,1)}, bf16[3,2,128,256]{3,2,1,0:T(8,128)(2,1)}, u32[]{:S(2)}, u32[]{:S(2)}) collective-permute-start(bf16[3,2,128,256]{3,2,1,0:T(8,128)(2,1)} %copy-done.13), channel_id=1, source_target_pairs={{0,12},{4,8},{8,4},{12,0},{16,28},{20,24},{24,20},{28,16},{1,13},{... | collective-permute-start | bytes 1179656 | tf_op jit(solution)/shard_map/ppermute | solution.py:70
  47.1 12.8 %copy-start.3 = (bf16[3,2,128,1024]{3,2,1,0:T(8,128)(2,1)S(1)}, bf16[3,2,128,1024]{3,2,1,0:T(8,128)(2,1)}, u32[]{:S(2)}) copy-start(bf16[3,2,128,1024]{3,2,1,0:T(8,128)(2,1)} %get-tuple-element.142.refs_0_) | copy-start | bytes 4718596
  59.9 16.3 %copy-start.11 = (bf16[3,2,128,1024]{3,2,1,0:T(8,128)(2,1)S(1)}, bf16[3,2,128,1024]{3,2,1,0:T(8,128)(2,1)}, u32[]{:S(2)}) copy-start(bf16[3,2,128,1024]{3,2,1,0:T(8,128)(2,1)} %copy-done.10) | copy-start | bytes 4718596
  59.9 17.9 %copy-start.7 = (bf16[3,2,128,256]{3,2,1,0:T(8,128)(2,1)S(1)}, bf16[3,2,128,256]{3,2,1,0:T(8,128)(2,1)}, u32[]{:S(2)}) copy-start(bf16[3,2,128,256]{3,2,1,0:T(8,128)(2,1)} %copy-done.6) | copy-start | bytes 1179652
  59.9 21.5 %copy-start.9 = (bf16[3,2,128,256]{3,2,1,0:T(8,128)(2,1)S(1)}, bf16[3,2,128,256]{3,2,1,0:T(8,128)(2,1)}, u32[]{:S(2)}) copy-start(bf16[3,2,128,256]{3,2,1,0:T(8,128)(2,1)} %get-tuple-element.143.refs_0_) | copy-start | bytes 1179652
  75.7 10.1 %collective-permute-start.14 = (bf16[1280,1024]{1,0:T(8,128)(2,1)S(1)}, bf16[1280,1024]{1,0:T(8,128)(2,1)S(1)}, u32[]{:S(2)}, u32[]{:S(2)}) collective-permute-start(bf16[1280,1024]{1,0:T(8,128)(2,1)S(1)} %pad_maximum_fusion), channel_id=1, source_target_pairs={{0,1},{1,0},{2,3},{3,2},{4,5},{5,4},{6,7},{7,6},{8,9},{9,8},{10,11... | collective-permute-start | bytes 7864328 | tf_op jit(solution)/shard_map/ppermute | solution.py:70
  75.7 10.1 %collective-permute-start.15 = (bf16[3,2,128,1024]{3,2,1,0:T(8,128)(2,1)}, bf16[3,2,128,1024]{3,2,1,0:T(8,128)(2,1)S(1)}, u32[]{:S(2)}, u32[]{:S(2)}) collective-permute-start(bf16[3,2,128,1024]{3,2,1,0:T(8,128)(2,1)} %collective-permute-done.11.refs_2_), channel_id=1, source_target_pairs={{0,1},{1,0},{2,3},{3,2},{4,5},{5,4},{6,7},{7,6},{8,9},{9,8},{10,11... | collective-permute-start | bytes 4718600 | tf_op jit(solution)/shard_map/ppermute | solution.py:70
  76.2 41.6 %collective-permute-start.13 = (bf16[3,2,128,1024]{3,2,1,0:T(8,128)(2,1)S(1)}, bf16[3,2,128,1024]{3,2,1,0:T(8,128)(2,1)S(1)}, u32[]{:S(2)}, u32[]{:S(2)}) collective-permute-start(bf16[3,2,128,1024]{3,2,1,0:T(8,128)(2,1)S(1)} %copy-done.11), channel_id=1, source_target_pairs={{0,2},{1,3},{2,0},{3,1},{4,6},{5,7},{6,4},{7,5},{8,10},{9,11},{10,... | collective-permute-start | bytes 4718600 | tf_op jit(solution)/shard_map/ppermute | solution.py:70
  77.7 8.1 %collective-permute-start.16 = (bf16[2,256,512]{2,1,0:T(8,128)(2,1)}, bf16[2,256,512]{2,1,0:T(8,128)(2,1)S(1)}, u32[]{:S(2)}, u32[]{:S(2)}) collective-permute-start(bf16[2,256,512]{2,1,0:T(8,128)(2,1)} %collective-permute-done.6.refs_4_), channel_id=1, source_target_pairs={{0,1},{1,0},{2,3},{3,2},{4,5},{5,4},{6,7},{7,6},{8,9},{9,8},{10,11... | collective-permute-start | bytes 1572872 | tf_op jit(solution)/shard_map/ppermute | solution.py:70
  79.9 37.9 %collective-permute-start.12 = (bf16[6,2,128,256]{3,2,1,0:T(8,128)(2,1)S(1)}, bf16[6,2,128,256]{3,2,1,0:T(8,128)(2,1)S(1)}, u32[]{:S(2)}, u32[]{:S(2)}) collective-permute-start(bf16[6,2,128,256]{3,2,1,0:T(8,128)(2,1)S(1)} %partial_sums.3), channel_id=1, source_target_pairs={{0,16},{4,20},{8,24},{12,28},{16,0},{20,4},{24,8},{28,12},{1,17},{... | collective-permute-start | bytes 2359304 | tf_op jit(solution)/shard_map/ppermute | solution.py:70
  85.8 36.1 %collective-permute-start.17 = (bf16[3,2,128,256]{3,2,1,0:T(8,128)(2,1)S(1)}, bf16[3,2,128,256]{3,2,1,0:T(8,128)(2,1)S(1)}, u32[]{:S(2)}, u32[]{:S(2)}) collective-permute-start(bf16[3,2,128,256]{3,2,1,0:T(8,128)(2,1)S(1)} %get-tuple-element.166), channel_id=1, source_target_pairs={{0,4},{4,0},{8,12},{12,8},{16,20},{20,16},{24,28},{28,24},{1,5},{5... | collective-permute-start | bytes 1179656 | tf_op jit(solution)/shard_map/ppermute | solution.py:70
  86.4 35.5 %collective-permute-start.18 = (bf16[3,2,128,256]{3,2,1,0:T(8,128)(2,1)S(1)}, bf16[3,2,128,256]{3,2,1,0:T(8,128)(2,1)S(1)}, u32[]{:S(2)}, u32[]{:S(2)}) collective-permute-start(bf16[3,2,128,256]{3,2,1,0:T(8,128)(2,1)S(1)} %get-tuple-element.167), channel_id=1, source_target_pairs={{0,8},{4,12},{8,0},{12,4},{16,24},{20,28},{24,16},{28,20},{1,9},{5... | collective-permute-start | bytes 1179656 | tf_op jit(solution)/shard_map/ppermute | solution.py:70
  89.3 34.1 %collective-permute-start.19 = (bf16[3,2,128,256]{3,2,1,0:T(8,128)(2,1)S(1)}, bf16[3,2,128,256]{3,2,1,0:T(8,128)(2,1)S(1)}, u32[]{:S(2)}, u32[]{:S(2)}) collective-permute-start(bf16[3,2,128,256]{3,2,1,0:T(8,128)(2,1)S(1)} %get-tuple-element.168), channel_id=1, source_target_pairs={{0,12},{4,8},{8,4},{12,0},{16,28},{20,24},{24,20},{28,16},{1,13},{... | collective-permute-start | bytes 1179656 | tf_op jit(solution)/shard_map/ppermute | solution.py:70
  89.4 10.4 %copy-start.5 = (bf16[2,256,512]{2,1,0:T(8,128)(2,1)S(1)}, bf16[2,256,512]{2,1,0:T(8,128)(2,1)}, u32[]{:S(2)}) copy-start(bf16[2,256,512]{2,1,0:T(8,128)(2,1)} %reshape_squeeze.6.h_own) | copy-start | bytes 1572868
  99.8 29.3 %copy-start.4 = (bf16[2,256,512]{2,1,0:T(8,128)(2,1)S(1)}, bf16[2,256,512]{2,1,0:T(8,128)(2,1)}, u32[]{:S(2)}) copy-start(bf16[2,256,512]{2,1,0:T(8,128)(2,1)} %reshape_squeeze.7.h_own) | copy-start | bytes 1572868
  117.8 17.4 %slice-start = ((s8[6291456]{0:T(1024)(128)(4,1)}), s8[4194304]{0:T(1024)(128)(4,1)S(1)}, s32[]{:S(2)}) async-start(s8[6291456]{0:T(1024)(128)(4,1)} %bitcast.7), calls=%async_computation | async-start | bytes 8388608
  123.4 11.8 %slice-start.1 = ((s8[6291456]{0:T(1024)(128)(4,1)}), s8[2097152]{0:T(1024)(128)(4,1)S(1)}, s32[]{:S(2)}) async-start(s8[6291456]{0:T(1024)(128)(4,1)} %bitcast.7), calls=%async_computation.1 | async-start | bytes 4194304
  123.4 4.0 %collective-permute-start.20 = (bf16[3,2,128,1024]{3,2,1,0:T(8,128)(2,1)S(1)}, bf16[3,2,128,1024]{3,2,1,0:T(8,128)(2,1)S(1)}, u32[]{:S(2)}, u32[]{:S(2)}) collective-permute-start(bf16[3,2,128,1024]{3,2,1,0:T(8,128)(2,1)S(1)} %copy-done.11), channel_id=1, source_target_pairs={{0,1},{1,0},{2,3},{3,2},{4,5},{5,4},{6,7},{7,6},{8,9},{9,8},{10,11... | collective-permute-start | bytes 4718600 | tf_op jit(solution)/shard_map/ppermute | solution.py:70
  123.4 5.7 %collective-permute-start.21 = (bf16[3,2,128,1024]{3,2,1,0:T(8,128)(2,1)S(1)}, bf16[3,2,128,1024]{3,2,1,0:T(8,128)(2,1)S(1)}, u32[]{:S(2)}, u32[]{:S(2)}) collective-permute-start(bf16[3,2,128,1024]{3,2,1,0:T(8,128)(2,1)S(1)} %collective-permute-done.13.refs_2_), channel_id=1, source_target_pairs={{0,1},{1,0},{2,3},{3,2},{4,5},{5,4},{6,7},{7,6},{8,9},{9,8},{10,11... | collective-permute-start | bytes 4718600 | tf_op jit(solution)/shard_map/ppermute | solution.py:70
  123.9 15.3 %collective-permute-start.22 = (bf16[3,2,128,256]{3,2,1,0:T(8,128)(2,1)S(1)}, bf16[3,2,128,256]{3,2,1,0:T(8,128)(2,1)S(1)}, u32[]{:S(2)}, u32[]{:S(2)}) collective-permute-start(bf16[3,2,128,256]{3,2,1,0:T(8,128)(2,1)S(1)} %get-tuple-element.173), channel_id=1, source_target_pairs={{0,4},{4,0},{8,12},{12,8},{16,20},{20,16},{24,28},{28,24},{1,5},{5... | collective-permute-start | bytes 1179656 | tf_op jit(solution)/shard_map/ppermute | solution.py:70
  125.1 14.1 %collective-permute-start.23 = (bf16[3,2,128,256]{3,2,1,0:T(8,128)(2,1)S(1)}, bf16[3,2,128,256]{3,2,1,0:T(8,128)(2,1)S(1)}, u32[]{:S(2)}, u32[]{:S(2)}) collective-permute-start(bf16[3,2,128,256]{3,2,1,0:T(8,128)(2,1)S(1)} %get-tuple-element.174), channel_id=1, source_target_pairs={{0,8},{4,12},{8,0},{12,4},{16,24},{20,28},{24,16},{28,20},{1,9},{5... | collective-permute-start | bytes 1179656 | tf_op jit(solution)/shard_map/ppermute | solution.py:70
  125.1 19.5 %collective-permute-start.24 = (bf16[3,2,128,256]{3,2,1,0:T(8,128)(2,1)S(1)}, bf16[3,2,128,256]{3,2,1,0:T(8,128)(2,1)S(1)}, u32[]{:S(2)}, u32[]{:S(2)}) collective-permute-start(bf16[3,2,128,256]{3,2,1,0:T(8,128)(2,1)S(1)} %get-tuple-element.175), channel_id=1, source_target_pairs={{0,12},{4,8},{8,4},{12,0},{16,28},{20,24},{24,20},{28,16},{1,13},{... | collective-permute-start | bytes 1179656 | tf_op jit(solution)/shard_map/ppermute | solution.py:70

commit v3 on v2

--- a/solution.py
+++ b/solution.py
@@ -105,22 +105,22 @@
 def make_section(p, split, state, prev_slope, place, half_at, group, hamiltonian=None):
     ops, parts, rows, columns = state.shape
     height, width = rows // split, columns // group
-    block = pl.BlockSpec((1, parts, height, columns), lambda a, *_: (a, 0, p, 0))
-    out = pl.BlockSpec((1, parts, height, columns), lambda a, *_: (a, 0, 0, 0))
-    chunk = pl.BlockSpec((1, parts, height, width), lambda a, *_: (a, 0, 0, 0))
-    half = (2, rows, columns // 2)
+    block = pl.BlockSpec((1, 1, height, columns), lambda a, x, *_: (a, x, p, 0))
+    out = pl.BlockSpec((1, 1, height, columns), lambda a, x, *_: (a, x, 0, 0))
+    chunk = pl.BlockSpec((1, 1, height, width), lambda a, x, *_: (a, x, 0, 0))
+    half = (1, rows, columns // 2)
     extra = [] if hamiltonian is None else [hamiltonian]
     return pl.pallas_call(
         functools.partial(section_kernel, group),
         grid_spec=pltpu.PrefetchScalarGridSpec(
             num_scalar_prefetch=2,
-            grid=(ops,),
-            in_specs=[block, block] + [pl.BlockSpec(half, lambda a, _, h: (0, 0, h[0])) for _ in extra],
-            out_specs=[pl.BlockSpec(half, lambda a, *_: (0, 0, 0)) for _ in extra]
+            grid=(ops, parts),
+            in_specs=[block, block] + [pl.BlockSpec(half, lambda a, x, _, h: (jnp.where(a == 0, x, parts - 1), 0, h[0])) for _ in extra],
+            out_specs=[pl.BlockSpec(half, lambda a, x, *_: (jnp.where(a == 0, x, parts - 1), 0, 0)) for _ in extra]
             + [out]
             + [chunk] * group,
         ),
-        out_shape=[jax.ShapeDtypeStruct(half, bf16) for _ in extra]
+        out_shape=[jax.ShapeDtypeStruct((parts, *half[1:]), bf16) for _ in extra]
         + [jax.ShapeDtypeStruct((ops, parts, height, columns), bf16)]
         + [jax.ShapeDtypeStruct((ops, parts, height, width), bf16)] * group,
         compiler_params=params(54 if p == 0 else 16),
@@ -160,15 +160,18 @@
 
 
 def partial_kernel(links, sides, group, places, coupling, vrows, vcols, *refs):
-    chunks, out, held, factors = refs[:group], *refs[group:]
+    chunks, out, held, factors, sem = refs[:group], *refs[group:]
     modes = vrows.shape[0]
     height, width = held.shape[2:]
     ops = chunks[0].shape[0]
     empty = group * ops
+    load = pltpu.make_async_copy(chunks[0], held.at[pl.ds(0, ops)], sem)
+    load.start()
     fill_factors(vrows, vcols, coupling, factors)
-    for b, chunk in enumerate(chunks):
-        held[b * ops : (b + 1) * ops] = chunk[...]
+    for b in range(1, group):
+        held[b * ops : (b + 1) * ops] = chunks[b][...]
     held[empty] = jnp.zeros(held.shape[1:], bf16)
+    load.wait()
     for u, c in enumerate(sides):
 
         @pl.when(places[c] < empty)
@@ -177,7 +180,7 @@
 
         @pl.when(places[c] == empty)
         def _():
-            @pl.loop(0, height // row_tile)
+            @pl.loop(0, height // row_tile, unroll=2)
             def _(i):
                 rows = pl.ds(pl.multiple_of(i * row_tile, row_tile), row_tile)
                 zero = jnp.zeros((row_tile, width), f32)
@@ -188,16 +191,19 @@
 
 def coupled_kernel(links, sides, group, places, coupling, vrows, vcols, *refs):
     chunks, received, outs = refs[:group], refs[group], refs[group + 1 : 2 * group + 1]
-    held, done, factors, spots = refs[2 * group + 1 :]
+    held, done, factors, spots, sem = refs[2 * group + 1 :]
     modes = vrows.shape[0]
     height, width = held.shape[2:]
     ops = chunks[0].shape[0]
     empty = group * ops
+    load = pltpu.make_async_copy(chunks[0], held.at[pl.ds(0, ops)], sem)
+    load.start()
     fill_factors(vrows, vcols, coupling, factors)
-    for b, chunk in enumerate(chunks):
-        held[b * ops : (b + 1) * ops] = chunk[...]
+    for b in range(1, group):
+        held[b * ops : (b + 1) * ops] = chunks[b][...]
     held[empty] = jnp.zeros(held.shape[1:], bf16)
     held[empty + 1 :] = received[...]
+    load.wait()
     for c in range(len(links)):
         spots[c] = places[c]
     for u, c in enumerate(sides):
@@ -206,7 +212,7 @@
 
         @pl.when(places[c] < empty)
         def _():
-            @pl.loop(0, height // row_tile)
+            @pl.loop(0, height // row_tile, unroll=2)
             def _(i):
                 rows = pl.ds(pl.multiple_of(i * row_tile, row_tile), row_tile)
                 if c in sides:
@@ -233,10 +239,10 @@
     size = height * width
     return pl.pallas_call(
         functools.partial(partial_kernel, links, sides, group),
-        in_specs=[scalars(), scalars()] + [whole()] * (2 + group),
+        in_specs=[scalars(), scalars(), whole(), whole(), anywhere()] + [whole()] * (group - 1),
         out_specs=whole(),
         out_shape=jax.ShapeDtypeStruct((len(sides), 2, height, width), bf16),
-        scratch_shapes=held + factors,
+        scratch_shapes=held + factors + [pltpu.SemaphoreType.DMA],
         compiler_params=params(12),
         cost_estimate=pl.CostEstimate(
             flops=40 * len(sides) * size,
@@ -254,13 +260,13 @@
     size = height * width
     return pl.pallas_call(
         functools.partial(coupled_kernel, links, sides, group),
-        in_specs=[scalars(), scalars()] + [whole()] * (3 + group),
+        in_specs=[scalars(), scalars(), whole(), whole(), anywhere()] + [whole()] * group,
         out_specs=[whole()] * group,
         out_shape=[jax.ShapeDtypeStruct(chunks[0].shape, bf16)] * group,
         scratch_shapes=held
         + [pltpu.VMEM((group * ops, 2, height, width), bf16)]
         + factors
-        + [pltpu.SMEM((len(links),), jnp.int32)],
+        + [pltpu.SMEM((len(links),), jnp.int32), pltpu.SemaphoreType.DMA],
         compiler_params=params(16),
         cost_estimate=pl.CostEstimate(flops=1, bytes_accessed=1, transcendentals=0),
         name="coupling_sums",

time: 149 us -> 150 us (level)
  transfers between devices with their start and end apart: 25 -> 25, of which waited for: 8 -> 8; matrix products, arithmetic and copies ran while one was open for 13% -> 12% of each run, Pallas kernels for 33% -> 33%
where the time goes in v3:
time: 150 us; the launch traced here: 149 us
  Pallas kernels  52.6 us (35%)
  waiting for transfers between devices  42.3 us (28%)
  starting transfers between devices  28.7 us (19%)
  local copies, waits for them, and re-layouts  22.7 us (15%)
  other arithmetic  1.87 us (1%)
    ppermute x25, waiting for transfers between devices, swap(): return lax.ppermute(array, axis, [(i, i ^ bit) for i in range(size)])  42.3 us
    ppermute x25, starting transfers between devices, swap(): return lax.ppermute(array, axis, [(i, i ^ bit) for i in range(size)])  28.7 us
    pallas_call x2, Pallas kernels, make_left(): pl.pallas_call(functools.partial(left_kernel, count), grid=(columns // ti...  13 us
    pallas_call x1, Pallas kernels, make_right(): pl.pallas_call(functools.partial(right_kernel, split, count), grid=(colum...  10.4 us
    slice x1, local copies, waits for them, and re-layouts, shards(): blocks[:, :, :, p].reshape(2, rows, row * height)  8.67 us
    pallas_call x2, Pallas kernels, make_coupled(): pl.pallas_call(functools.partial(coupled_kernel, links, sides, group), in...  8.14 us
    pallas_call x2, Pallas kernels, make_section(): pl.pallas_call(functools.partial(section_kernel, group), grid_spec=pltpu....  7.98 us
    pallas_call x2, Pallas kernels, make_final(): pl.pallas_call(functools.partial(final_kernel, group), grid_spec=pltpu.Pr...  7.92 us
  transfers between devices with their start and end apart: 25, of which 8 were waited for; matrix products, arithmetic and copies ran while one was open for 12% of the time, Pallas kernels for 33%

profile of v3, /device:TPU:0, one launch (start us, length us, event | category | flops | bytes accessed | tf_op | source)
XLA Modules:
  0.0 149.2 jit_solution(15769896685610502657)
XLA Ops:
  0.6 3.1 %collective-permute-start.1 = (s32[3,6]{1,0:T(4,128)}, s32[3,6]{1,0:T(4,128)S(1)}, u32[]{:S(2)}, u32[]{:S(2)}) collective-permute-start(s32[3,6]{1,0:T(4,128)} %param.18), channel_id=1, source_target_pairs={{0,8},{4,12},{8,0},{12,4},{16,24},{20,28},{24,16},{28,20},{1,9},{5... | collective-permute-start | bytes 224 | tf_op jit(solution)/shard_map/ppermute | solution.py:70
  3.7 1.5 collective-permute-start
  5.2 0.1 collective-permute-start.2
  5.3 7.0 %section.2 = (bf16[2,256,512]{2,1,0:T(8,128)(2,1)}, bf16[3,2,128,1024]{3,2,1,0:T(8,128)(2,1)}, bf16[3,2,128,256]{3,2,1,0:T(8,128)(2,1)}, bf16[3,2,128,256]{3,2,1...) custom-call(s32[1]{0:T(128)} %bitcast.where, s32[1]{0:T(128)} %bitcast.2._, ...), custom_call_target="tpu_custom_call" | custom-call | flops 1 | bytes 1 | tf_op jit(solution)/shard_map/section/pallas_call | solution.py:113
  12.3 0.0 collective-permute-done.1
  12.4 0.5 copy-done.18
  12.9 0.0 copy-done.19
  12.9 0.0 copy-done.20
  13.0 1.9 %collective-permute-start.6 = (bf16[2,256,512]{2,1,0:T(8,128)(2,1)}, bf16[2,256,512]{2,1,0:T(8,128)(2,1)}, u32[]{:S(2)}, u32[]{:S(2)}) collective-permute-start(bf16[2,256,512]{2,1,0:T(8,128)(2,1)} %get-tuple-element.115), channel_id=1, source_target_pairs={{0,2},{1,3},{2,0},{3,1},{4,6},{5,7},{6,4},{7,5},{8,10},{9,11},{10,... | collective-permute-start | bytes 1572872 | tf_op jit(solution)/shard_map/ppermute | solution.py:70
  14.8 0.6 fusion
  15.5 1.5 %collective-permute-start.3 = (bf16[3,2,128,256]{3,2,1,0:T(8,128)(2,1)}, bf16[3,2,128,256]{3,2,1,0:T(8,128)(2,1)}, u32[]{:S(2)}, u32[]{:S(2)}) collective-permute-start(bf16[3,2,128,256]{3,2,1,0:T(8,128)(2,1)} %get-tuple-element.99), channel_id=1, source_target_pairs={{0,4},{4,0},{8,12},{12,8},{16,20},{20,16},{24,28},{28,24},{1,5},{5... | collective-permute-start | bytes 1179656 | tf_op jit(solution)/shard_map/ppermute | solution.py:70
  16.9 1.6 %collective-permute-start.4 = (bf16[3,2,128,256]{3,2,1,0:T(8,128)(2,1)}, bf16[3,2,128,256]{3,2,1,0:T(8,128)(2,1)}, u32[]{:S(2)}, u32[]{:S(2)}) collective-permute-start(bf16[3,2,128,256]{3,2,1,0:T(8,128)(2,1)} %get-tuple-element.100), channel_id=1, source_target_pairs={{0,8},{4,12},{8,0},{12,4},{16,24},{20,28},{24,16},{28,20},{1,9},{5... | collective-permute-start | bytes 1179656 | tf_op jit(solution)/shard_map/ppermute | solution.py:70
  18.5 0.4 collective-permute-start.5
  18.9 0.1 multiply_reduce_fusion.decay
  19.1 0.0 copy-start.12
  19.1 0.9 section.3
  20.0 0.8 copy-done.6
  20.8 1.1 copy-done.10
  22.0 0.8 copy-done.13
  22.8 0.8 copy-done.14
  23.6 0.8 copy-done.15
  24.4 0.9 copy.24.vrows
  25.3 0.9 copy.23.vrows
  26.2 0.7 pad_add_fusion
  26.9 0.8 compare_reduce_fusion
  27.7 0.0 collective-permute-done.3.refs_1_
  27.7 1.6 %collective-permute-done.4.refs_2_ = bf16[3,2,128,256]{3,2,1,0:T(8,128)(2,1)} collective-permute-done((bf16[3,2,128,256]{3,2,1,0:T(8,128)(2,1)}, bf16[3,2,128,256]{3,2,1,0:T(8,128)(2,1)}, u32[]{:S(2)}, u32[]{:S(2)}) %collective-permute-start.4) | collective-permute-done | bytes 393248 | tf_op jit(solution)/shard_map/ppermute | solution.py:70
  29.3 5.8 %collective-permute-done.5.refs_3_ = bf16[3,2,128,256]{3,2,1,0:T(8,128)(2,1)} collective-permute-done((bf16[3,2,128,256]{3,2,1,0:T(8,128)(2,1)}, bf16[3,2,128,256]{3,2,1,0:T(8,128)(2,1)}, u32[]{:S(2)}, u32[]{:S(2)}) %collective-permute-start.5) | collective-permute-done | bytes 393248 | tf_op jit(solution)/shard_map/ppermute | solution.py:70
  35.1 0.0 collective-permute-done.6.refs_4_
  35.1 0.4 collective-permute-start.11
  35.5 1.0 copy-done.8
  36.5 3.0 %partial_sums.2 = bf16[6,2,128,256]{3,2,1,0:T(8,128)(2,1)} custom-call(s32[24]{0:T(128)S(1)} %select_reduce_fusion.places, f32[2,6]{1,0:T(2,128)S(1)} %copy-done.12, f32[6,128,1]{2,1,0:T(8,128)S(1)} %copy.23.vrows, f32[6,256]{1,0:T(8,128)S(1)} %get-tuple-element.127.vcols, bf16[3,2,128,256]{3,2,1,0:T(8,128)(2,1)S(1)} %copy-done.8, ...), custom_call_target="tpu_custom_call" | custom-call | flops 7864320 | bytes 2359296 | tf_op jit(solution)/shard_map/partial_sums/pallas_call | solution.py:240
  39.5 3.4 %collective-permute-start.10 = (bf16[6,2,128,256]{3,2,1,0:T(8,128)(2,1)}, bf16[6,2,128,256]{3,2,1,0:T(8,128)(2,1)}, u32[]{:S(2)}, u32[]{:S(2)}) collective-permute-start(bf16[6,2,128,256]{3,2,1,0:T(8,128)(2,1)} %partial_sums.2), channel_id=1, source_target_pairs={{0,16},{4,20},{8,24},{12,28},{16,0},{20,4},{24,8},{28,12},{1,17},{... | collective-permute-start | bytes 2359304 | tf_op jit(solution)/shard_map/ppermute | solution.py:70
  43.0 1.5 %collective-permute-start.7 = (bf16[3,2,128,256]{3,2,1,0:T(8,128)(2,1)}, bf16[3,2,128,256]{3,2,1,0:T(8,128)(2,1)}, u32[]{:S(2)}, u32[]{:S(2)}) collective-permute-start(bf16[3,2,128,256]{3,2,1,0:T(8,128)(2,1)} %copy-done.15), channel_id=1, source_target_pairs={{0,4},{4,0},{8,12},{12,8},{16,20},{20,16},{24,28},{28,24},{1,5},{5... | collective-permute-start | bytes 1179656 | tf_op jit(solution)/shard_map/ppermute | solution.py:70
  44.5 1.6 %collective-permute-start.8 = (bf16[3,2,128,256]{3,2,1,0:T(8,128)(2,1)}, bf16[3,2,128,256]{3,2,1,0:T(8,128)(2,1)}, u32[]{:S(2)}, u32[]{:S(2)}) collective-permute-start(bf16[3,2,128,256]{3,2,1,0:T(8,128)(2,1)} %copy-done.14), channel_id=1, source_target_pairs={{0,8},{4,12},{8,0},{12,4},{16,24},{20,28},{24,16},{28,20},{1,9},{5... | collective-permute-start | bytes 1179656 | tf_op jit(solution)/shard_map/ppermute | solution.py:70
  46.0 0.4 collective-permute-start.9
  46.5 1.5 %reshape.30 = bf16[2,256,4,2,128]{4,3,2,1,0:T(2,128)(2,1)} reshape(bf16[2,256,1024]{2,1,0:T(8,128)(2,1)S(1)} %copy-done.2) | data formatting | bytes 2097152 | tf_op jit(solution)/shard_map/reshape | solution.py:506
  48.0 8.7 %slice_reduce_fusion = (bf16[2,256,4,128]{3,2,1,0:T(4,128)(2,1)}, bf16[2,256,4,128]{3,2,1,0:T(4,128)(2,1)}) fusion(bf16[2,256,4,2,128]{4,3,2,1,0:T(2,128)(2,1)} %reshape.30), kind=kLoop, calls=%fused_computation.1 | loop fusion | bytes 2097152 | tf_op jit(solution)/shard_map/slice | solution.py:507
  56.7 2.0 %reshape_squeeze.7.h_own = bf16[2,256,512]{2,1,0:T(8,128)(2,1)} reshape(bf16[2,256,4,128]{3,2,1,0:T(4,128)(2,1)} %get-tuple-element.182) | data formatting | bytes 1048576 | tf_op jit(solution)/shard_map/reshape;squeeze | solution.py:507
  58.7 2.0 %reshape_squeeze.6.h_own = bf16[2,256,512]{2,1,0:T(8,128)(2,1)} reshape(bf16[2,256,4,128]{3,2,1,0:T(4,128)(2,1)} %get-tuple-element.183) | data formatting | bytes 1048576 | tf_op jit(solution)/shard_map/reshape;squeeze | solution.py:507
  60.8 0.2 pad_maximum_fusion
  61.1 8.7 %collective-permute-done.8.refs_2_ = bf16[3,2,128,256]{3,2,1,0:T(8,128)(2,1)} collective-permute-done((bf16[3,2,128,256]{3,2,1,0:T(8,128)(2,1)}, bf16[3,2,128,256]{3,2,1,0:T(8,128)(2,1)}, u32[]{:S(2)}, u32[]{:S(2)}) %collective-permute-start.8) | collective-permute-done | bytes 393248 | tf_op jit(solution)/shard_map/ppermute | solution.py:70
  69.7 6.9 %collective-permute-done.9.refs_3_ = bf16[3,2,128,256]{3,2,1,0:T(8,128)(2,1)} collective-permute-done((bf16[3,2,128,256]{3,2,1,0:T(8,128)(2,1)}, bf16[3,2,128,256]{3,2,1,0:T(8,128)(2,1)}, u32[]{:S(2)}, u32[]{:S(2)}) %collective-permute-start.9) | collective-permute-done | bytes 393248 | tf_op jit(solution)/shard_map/ppermute | solution.py:70
  76.6 0.5 collective-permute-start.15
  77.1 1.5 %collective-permute-start.13 = (bf16[3,2,128,1024]{3,2,1,0:T(8,128)(2,1)S(1)}, bf16[3,2,128,1024]{3,2,1,0:T(8,128)(2,1)S(1)}, u32[]{:S(2)}, u32[]{:S(2)}) collective-permute-start(bf16[3,2,128,1024]{3,2,1,0:T(8,128)(2,1)S(1)} %copy-done.11), channel_id=1, source_target_pairs={{0,2},{1,3},{2,0},{3,1},{4,6},{5,7},{6,4},{7,5},{8,10},{9,11},{10,... | collective-permute-start | bytes 4718600 | tf_op jit(solution)/shard_map/ppermute | solution.py:70
  78.7 2.1 %partial_sums.3 = bf16[6,2,128,256]{3,2,1,0:T(8,128)(2,1)S(1)} custom-call(s32[24]{0:T(128)S(1)} %select_reduce_fusion.places, f32[2,6]{1,0:T(2,128)S(1)} %copy-done.12, f32[6,128,1]{2,1,0:T(8,128)S(1)} %copy.24.vrows, f32[6,256]{1,0:T(8,128)S(1)} %get-tuple-element.127.vcols, bf16[3,2,128,256]{3,2,1,0:T(8,128)(2,1)S(1)} %copy-done.7, ...), custom_call_target="tpu_custom_call" | custom-call | flops 7864320 | bytes 2359296 | tf_op jit(solution)/shard_map/partial_sums/pallas_call | solution.py:240
  80.8 1.8 %collective-permute-start.12 = (bf16[6,2,128,256]{3,2,1,0:T(8,128)(2,1)S(1)}, bf16[6,2,128,256]{3,2,1,0:T(8,128)(2,1)S(1)}, u32[]{:S(2)}, u32[]{:S(2)}) collective-permute-start(bf16[6,2,128,256]{3,2,1,0:T(8,128)(2,1)S(1)} %partial_sums.3), channel_id=1, source_target_pairs={{0,16},{4,20},{8,24},{12,28},{16,0},{20,4},{24,8},{28,12},{1,17},{... | collective-permute-start | bytes 2359304 | tf_op jit(solution)/shard_map/ppermute | solution.py:70
  82.6 4.2 %coupling_sums.2 = (bf16[3,2,128,256]{3,2,1,0:T(8,128)(2,1)S(1)}, bf16[3,2,128,256]{3,2,1,0:T(8,128)(2,1)S(1)}, bf16[3,2,128,256]{3,2,1,0:T(8,128)(2,1)S(1)}, bf16[3,2,128,256]{3,2,1,0:T(8,128)(2,1)S(1)}) custom-call(s32[24]{0:T(128)S(1)} %select_reduce_fusion.places, f32[2,6]{1,0:T(2,128)S(1)} %copy-done.12, f32[6,128,1]{2,1,0:T(8,128)S(1)} %copy.23.vrows, ...), custom_call_target="tpu_custom_call" | custom-call | flops 1 | bytes 1 | tf_op jit(solution)/shard_map/coupling_sums/pallas_call | solution.py:261
  86.8 0.6 collective-permute-start.17
  87.4 2.9 %collective-permute-start.18 = (bf16[3,2,128,256]{3,2,1,0:T(8,128)(2,1)S(1)}, bf16[3,2,128,256]{3,2,1,0:T(8,128)(2,1)S(1)}, u32[]{:S(2)}, u32[]{:S(2)}) collective-permute-start(bf16[3,2,128,256]{3,2,1,0:T(8,128)(2,1)S(1)} %get-tuple-element.167), channel_id=1, source_target_pairs={{0,8},{4,12},{8,0},{12,4},{16,24},{20,28},{24,16},{28,20},{1,9},{5... | collective-permute-start | bytes 1179656 | tf_op jit(solution)/shard_map/ppermute | solution.py:70
  90.4 0.0 collective-permute-start.19
  90.4 10.4 %right_products.1.base = f32[3,2,256,1024]{3,2,1,0:T(8,128)S(1)} custom-call(s32[1]{0:T(128)} %bitcast.1.where, f32[3]{0:T(128)S(1)} %multiply_reduce_fusion.decay, bf16[2,256,1024]{2,1,0:T(8,128)(2,1)S(1)} %copy-done.2, bf16[3,2,128,1024]{3,2,1,0:T(8,128)(2,1)S(1)} %copy-done.3, bf16[3,2,128,1024]{3,2,1,0:T(8,128)(2,1)S(1)} %copy-done.11, ...), custom_call_target="tpu_custom_call" | custom-call | flops 6442450944 | bytes 13631488 | tf_op jit(solution)/shard_map/right_products/pallas_call | solution.py:324
  100.8 6.9 %left_products.2.base = f32[3,2,256,1024]{3,2,1,0:T(8,128)S(1)} custom-call(s32[1]{0:T(128)} %bitcast.1.where, bf16[2,256,512]{2,1,0:T(8,128)(2,1)S(1)} %copy-done.5, f32[3,2,256,1024]{3,2,1,0:T(8,128)S(1)} %right_products.1.base, bf16[3,2,128,1024]{3,2,1,0:T(8,128)(2,1)S(1)} %copy-done.3, ...), custom_call_target="tpu_custom_call" | custom-call | flops 3221225472 | bytes 18874368 | tf_op jit(solution)/shard_map/left_products/pallas_call | solution.py:360
  107.7 10.9 %collective-permute-done.12.refs_4_ = bf16[6,2,128,256]{3,2,1,0:T(8,128)(2,1)S(1)} collective-permute-done((bf16[6,2,128,256]{3,2,1,0:T(8,128)(2,1)S(1)}, bf16[6,2,128,256]{3,2,1,0:T(8,128)(2,1)S(1)}, u32[]{:S(2)}, u32[]{:S(2)}) %collective-permute-start.12) | collective-permute-done | bytes 786464 | tf_op jit(solution)/shard_map/ppermute | solution.py:70
  118.6 3.9 %coupling_sums.3 = (bf16[3,2,128,256]{3,2,1,0:T(8,128)(2,1)S(1)}, bf16[3,2,128,256]{3,2,1,0:T(8,128)(2,1)S(1)}, bf16[3,2,128,256]{3,2,1,0:T(8,128)(2,1)S(1)}, bf16[3,2,128,256]{3,2,1,0:T(8,128)(2,1)S(1)}) custom-call(s32[24]{0:T(128)S(1)} %select_reduce_fusion.places, f32[2,6]{1,0:T(2,128)S(1)} %copy-done.12, f32[6,128,1]{2,1,0:T(8,128)S(1)} %copy.24.vrows, ...), custom_call_target="tpu_custom_call" | custom-call | flops 1 | bytes 1 | tf_op jit(solution)/shard_map/coupling_sums/pallas_call | solution.py:261
  122.6 1.5 collective-permute-done.19.refs_3_
  124.1 0.5 collective-permute-start.21
  124.6 1.6 %collective-permute-start.22 = (bf16[3,2,128,256]{3,2,1,0:T(8,128)(2,1)S(1)}, bf16[3,2,128,256]{3,2,1,0:T(8,128)(2,1)S(1)}, u32[]{:S(2)}, u32[]{:S(2)}) collective-permute-start(bf16[3,2,128,256]{3,2,1,0:T(8,128)(2,1)S(1)} %get-tuple-element.173), channel_id=1, source_target_pairs={{0,4},{4,0},{8,12},{12,8},{16,20},{20,16},{24,28},{28,24},{1,5},{5... | collective-permute-start | bytes 1179656 | tf_op jit(solution)/shard_map/ppermute | solution.py:70
  126.2 1.9 %collective-permute-start.24 = (bf16[3,2,128,256]{3,2,1,0:T(8,128)(2,1)S(1)}, bf16[3,2,128,256]{3,2,1,0:T(8,128)(2,1)S(1)}, u32[]{:S(2)}, u32[]{:S(2)}) collective-permute-start(bf16[3,2,128,256]{3,2,1,0:T(8,128)(2,1)S(1)} %get-tuple-element.175), channel_id=1, source_target_pairs={{0,12},{4,8},{8,4},{12,0},{16,28},{20,24},{24,20},{28,16},{1,13},{... | collective-permute-start | bytes 1179656 | tf_op jit(solution)/shard_map/ppermute | solution.py:70
  128.1 1.7 %collective-permute-done.21.refs_3_ = bf16[3,2,128,1024]{3,2,1,0:T(8,128)(2,1)S(1)} collective-permute-done((bf16[3,2,128,1024]{3,2,1,0:T(8,128)(2,1)S(1)}, bf16[3,2,128,1024]{3,2,1,0:T(8,128)(2,1)S(1)}, u32[]{:S(2)}, u32[]{:S(2)}) %collective-permute-start.21) | collective-permute-done | bytes 1572896 | tf_op jit(solution)/shard_map/ppermute | solution.py:70
  129.7 6.1 %left_products.3.base = f32[3,2,256,1024]{3,2,1,0:T(8,128)S(1)} custom-call(s32[1]{0:T(128)} %bitcast.1.where, bf16[2,256,512]{2,1,0:T(8,128)(2,1)S(1)} %copy-done.4, f32[3,2,256,1024]{3,2,1,0:T(8,128)S(1)} %left_products.2.base, bf16[3,2,128,1024]{3,2,1,0:T(8,128)(2,1)S(1)} %copy-done.11, bf16[3,2,128,1024]{3,2,1,0:T(8,128)(2,1)S(1)} %collective-permute-done.20.refs_1_, ...), custom_call_target="tpu_custom_call" | custom-call | flops 3221225472 | bytes 18874368 | tf_op jit(solution)/shard_map/left_products/pallas_call | solution.py:360
  135.9 4.0 %outputs.2 = (f32[3,2,256,1024]{3,2,1,0:T(8,128)}, f32[3,2,256,1024]{3,2,1,0:T(8,128)}) custom-call(s32[1]{0:T(128)} %bitcast.where, f32[3,2,256,1024]{3,2,1,0:T(8,128)S(1)} %left_products.3.base, f32[3,2,256,1024]{3,2,1,0:T(8,128)S(1)} %bitcast.8, bf16[3,2,128,256]{3,2,1,0:T(8,128)(2,1)S(1)} %get-tuple-element.176.refs_0_, ...), custom_call_target="tpu_custom_call" | custom-call | flops 3145728 | bytes 14155776 | tf_op jit(solution)/shard_map/outputs/pallas_call | solution.py:408
  139.9 5.4 %collective-permute-done.24.refs_3_ = bf16[3,2,128,256]{3,2,1,0:T(8,128)(2,1)S(1)} collective-permute-done((bf16[3,2,128,256]{3,2,1,0:T(8,128)(2,1)S(1)}, bf16[3,2,128,256]{3,2,1,0:T(8,128)(2,1)S(1)}, u32[]{:S(2)}, u32[]{:S(2)}) %collective-permute-start.24) | collective-permute-done | bytes 393248 | tf_op jit(solution)/shard_map/ppermute | solution.py:70
  145.2 3.9 %outputs.3 = (f32[3,2,256,1024]{3,2,1,0:T(8,128)}, f32[3,2,256,1024]{3,2,1,0:T(8,128)}) custom-call(s32[1]{0:T(128)} %bitcast.where, f32[3,2,256,1024]{3,2,1,0:T(8,128)S(1)} %left_products.3.base, f32[3,2,256,1024]{3,2,1,0:T(8,128)S(1)} %bitcast.8, ...), custom_call_target="tpu_custom_call", output_to_operand_aliasing={{0}: (7, {}), {1}: (8, {})} | custom-call | flops 3145728 | bytes 14155776 | tf_op jit(solution)/shard_map/outputs/pallas_call | solution.py:408
  (59 shorter events, 0.1 us)
Async XLA Ops:
  0.6 11.7 %collective-permute-start.1 = (s32[3,6]{1,0:T(4,128)}, s32[3,6]{1,0:T(4,128)S(1)}, u32[]{:S(2)}, u32[]{:S(2)}) collective-permute-start(s32[3,6]{1,0:T(4,128)} %param.18), channel_id=1, source_target_pairs={{0,8},{4,12},{8,0},{12,4},{16,24},{20,28},{24,16},{28,20},{1,9},{5... | collective-permute-start | bytes 224 | tf_op jit(solution)/shard_map/ppermute | solution.py:70
  3.7 8.6 %collective-permute-start = (s32[3,6]{1,0:T(4,128)}, s32[3,6]{1,0:T(4,128)S(1)}, u32[]{:S(2)}, u32[]{:S(2)}) collective-permute-start(s32[3,6]{1,0:T(4,128)} %param.18), channel_id=1, source_target_pairs={{0,4},{4,0},{8,12},{12,8},{16,20},{20,16},{24,28},{28,24},{1,5},{5... | collective-permute-start | bytes 224 | tf_op jit(solution)/shard_map/ppermute | solution.py:70
  5.2 7.2 %collective-permute-start.2 = (s32[3,6]{1,0:T(4,128)}, s32[3,6]{1,0:T(4,128)S(1)}, u32[]{:S(2)}, u32[]{:S(2)}) collective-permute-start(s32[3,6]{1,0:T(4,128)} %param.18), channel_id=1, source_target_pairs={{0,12},{4,8},{8,4},{12,0},{16,28},{20,24},{24,20},{28,16},{1,13},{... | collective-permute-start | bytes 224 | tf_op jit(solution)/shard_map/ppermute | solution.py:70
  5.3 9.6 %copy-start.16 = (f32[6,1024]{1,0:T(8,128)S(1)}, f32[6,1024]{1,0:T(8,128)}, u32[]{:S(2)}) copy-start(f32[6,1024]{1,0:T(8,128)} %param.15) | copy-start | bytes 73732
  5.3 13.7 %copy-start.17 = (s32[3,6]{1,0:T(4,128)S(1)}, s32[3,6]{1,0:T(4,128)}, u32[]{:S(2)}) copy-start(s32[3,6]{1,0:T(4,128)} %param.18) | copy-start | bytes 220
  5.3 13.7 %copy-start.21 = (f32[6]{0:T(128)S(1)}, f32[6]{0:T(128)}, u32[]{:S(2)}) copy-start(f32[6]{0:T(128)} %param.17) | copy-start | bytes 76
  5.3 13.8 %copy-start = (f32[3,2,256,1024]{3,2,1,0:T(8,128)S(1)}, f32[3,2,256,1024]{3,2,1,0:T(8,128)}, u32[]{:S(2)}) copy-start(f32[3,2,256,1024]{3,2,1,0:T(8,128)} %slope.2) | copy-start | bytes 18874372
  5.3 13.8 %copy-start.1 = (bf16[3,2,256,1024]{3,2,1,0:T(8,128)(2,1)S(1)}, bf16[3,2,256,1024]{3,2,1,0:T(8,128)(2,1)}, u32[]{:S(2)}) copy-start(bf16[3,2,256,1024]{3,2,1,0:T(8,128)(2,1)} %state.2) | copy-start | bytes 9437188
  12.3 0.6 copy-start.18
  12.4 0.6 copy-start.19
  12.4 0.6 copy-start.20
  13.0 22.2 %collective-permute-start.6 = (bf16[2,256,512]{2,1,0:T(8,128)(2,1)}, bf16[2,256,512]{2,1,0:T(8,128)(2,1)}, u32[]{:S(2)}, u32[]{:S(2)}) collective-permute-start(bf16[2,256,512]{2,1,0:T(8,128)(2,1)} %get-tuple-element.115), channel_id=1, source_target_pairs={{0,2},{1,3},{2,0},{3,1},{4,6},{5,7},{6,4},{7,5},{8,10},{9,11},{10,... | collective-permute-start | bytes 1572872 | tf_op jit(solution)/shard_map/ppermute | solution.py:70
  15.5 12.3 %collective-permute-start.3 = (bf16[3,2,128,256]{3,2,1,0:T(8,128)(2,1)}, bf16[3,2,128,256]{3,2,1,0:T(8,128)(2,1)}, u32[]{:S(2)}, u32[]{:S(2)}) collective-permute-start(bf16[3,2,128,256]{3,2,1,0:T(8,128)(2,1)} %get-tuple-element.99), channel_id=1, source_target_pairs={{0,4},{4,0},{8,12},{12,8},{16,20},{20,16},{24,28},{28,24},{1,5},{5... | collective-permute-start | bytes 1179656 | tf_op jit(solution)/shard_map/ppermute | solution.py:70
  16.9 12.4 %collective-permute-start.4 = (bf16[3,2,128,256]{3,2,1,0:T(8,128)(2,1)}, bf16[3,2,128,256]{3,2,1,0:T(8,128)(2,1)}, u32[]{:S(2)}, u32[]{:S(2)}) collective-permute-start(bf16[3,2,128,256]{3,2,1,0:T(8,128)(2,1)} %get-tuple-element.100), channel_id=1, source_target_pairs={{0,8},{4,12},{8,0},{12,4},{16,24},{20,28},{24,16},{28,20},{1,9},{5... | collective-permute-start | bytes 1179656 | tf_op jit(solution)/shard_map/ppermute | solution.py:70
  18.5 16.6 %collective-permute-start.5 = (bf16[3,2,128,256]{3,2,1,0:T(8,128)(2,1)}, bf16[3,2,128,256]{3,2,1,0:T(8,128)(2,1)}, u32[]{:S(2)}, u32[]{:S(2)}) collective-permute-start(bf16[3,2,128,256]{3,2,1,0:T(8,128)(2,1)} %get-tuple-element.101), channel_id=1, source_target_pairs={{0,12},{4,8},{8,4},{12,0},{16,28},{20,24},{24,20},{28,16},{1,13},{... | collective-permute-start | bytes 1179656 | tf_op jit(solution)/shard_map/ppermute | solution.py:70
  19.1 16.5 %copy-start.12 = (f32[2,6]{1,0:T(2,128)S(1)}, f32[2,6]{1,0:T(2,128)}, u32[]{:S(2)}) copy-start(f32[2,6]{1,0:T(2,128)} %coupling.7) | copy-start | bytes 148
  20.0 0.8 copy-start.6
  20.8 1.1 copy-start.10
  22.0 0.8 copy-start.13
  22.8 0.8 copy-start.14
  23.6 0.8 copy-start.15
  24.4 22.1 %copy-start.2 = (bf16[2,256,1024]{2,1,0:T(8,128)(2,1)S(1)}, bf16[2,256,1024]{2,1,0:T(8,128)(2,1)}, u32[]{:S(2)}) copy-start(bf16[2,256,1024]{2,1,0:T(8,128)(2,1)} %h_own) | copy-start | bytes 3145732
  35.1 41.5 %collective-permute-start.11 = (bf16[3,2,128,1024]{3,2,1,0:T(8,128)(2,1)}, bf16[3,2,128,1024]{3,2,1,0:T(8,128)(2,1)}, u32[]{:S(2)}, u32[]{:S(2)}) collective-permute-start(bf16[3,2,128,1024]{3,2,1,0:T(8,128)(2,1)} %get-tuple-element.142.refs_0_), channel_id=1, source_target_pairs={{0,2},{1,3},{2,0},{3,1},{4,6},{5,7},{6,4},{7,5},{8,10},{9,11},{10,... | collective-permute-start | bytes 4718600 | tf_op jit(solution)/shard_map/ppermute | solution.py:70
  35.5 1.0 copy-start.8
  39.5 37.1 %collective-permute-start.10 = (bf16[6,2,128,256]{3,2,1,0:T(8,128)(2,1)}, bf16[6,2,128,256]{3,2,1,0:T(8,128)(2,1)}, u32[]{:S(2)}, u32[]{:S(2)}) collective-permute-start(bf16[6,2,128,256]{3,2,1,0:T(8,128)(2,1)} %partial_sums.2), channel_id=1, source_target_pairs={{0,16},{4,20},{8,24},{12,28},{16,0},{20,4},{24,8},{28,12},{1,17},{... | collective-permute-start | bytes 2359304 | tf_op jit(solution)/shard_map/ppermute | solution.py:70
  43.0 18.1 %collective-permute-start.7 = (bf16[3,2,128,256]{3,2,1,0:T(8,128)(2,1)}, bf16[3,2,128,256]{3,2,1,0:T(8,128)(2,1)}, u32[]{:S(2)}, u32[]{:S(2)}) collective-permute-start(bf16[3,2,128,256]{3,2,1,0:T(8,128)(2,1)} %copy-done.15), channel_id=1, source_target_pairs={{0,4},{4,0},{8,12},{12,8},{16,20},{20,16},{24,28},{28,24},{1,5},{5... | collective-permute-start | bytes 1179656 | tf_op jit(solution)/shard_map/ppermute | solution.py:70
  44.5 25.2 %collective-permute-start.8 = (bf16[3,2,128,256]{3,2,1,0:T(8,128)(2,1)}, bf16[3,2,128,256]{3,2,1,0:T(8,128)(2,1)}, u32[]{:S(2)}, u32[]{:S(2)}) collective-permute-start(bf16[3,2,128,256]{3,2,1,0:T(8,128)(2,1)} %copy-done.14), channel_id=1, source_target_pairs={{0,8},{4,12},{8,0},{12,4},{16,24},{20,28},{24,16},{28,20},{1,9},{5... | collective-permute-start | bytes 1179656 | tf_op jit(solution)/shard_map/ppermute | solution.py:70
  46.0 30.6 %collective-permute-start.9 = (bf16[3,2,128,256]{3,2,1,0:T(8,128)(2,1)}, bf16[3,2,128,256]{3,2,1,0:T(8,128)(2,1)}, u32[]{:S(2)}, u32[]{:S(2)}) collective-permute-start(bf16[3,2,128,256]{3,2,1,0:T(8,128)(2,1)} %copy-done.13), channel_id=1, source_target_pairs={{0,12},{4,8},{8,4},{12,0},{16,28},{20,24},{24,20},{28,16},{1,13},{... | collective-permute-start | bytes 1179656 | tf_op jit(solution)/shard_map/ppermute | solution.py:70
  48.0 12.8 %copy-start.3 = (bf16[3,2,128,1024]{3,2,1,0:T(8,128)(2,1)S(1)}, bf16[3,2,128,1024]{3,2,1,0:T(8,128)(2,1)}, u32[]{:S(2)}) copy-start(bf16[3,2,128,1024]{3,2,1,0:T(8,128)(2,1)} %get-tuple-element.142.refs_0_) | copy-start | bytes 4718596
  60.8 16.3 %copy-start.11 = (bf16[3,2,128,1024]{3,2,1,0:T(8,128)(2,1)S(1)}, bf16[3,2,128,1024]{3,2,1,0:T(8,128)(2,1)}, u32[]{:S(2)}) copy-start(bf16[3,2,128,1024]{3,2,1,0:T(8,128)(2,1)} %copy-done.10) | copy-start | bytes 4718596
  60.8 17.9 %copy-start.7 = (bf16[3,2,128,256]{3,2,1,0:T(8,128)(2,1)S(1)}, bf16[3,2,128,256]{3,2,1,0:T(8,128)(2,1)}, u32[]{:S(2)}) copy-start(bf16[3,2,128,256]{3,2,1,0:T(8,128)(2,1)} %copy-done.6) | copy-start | bytes 1179652
  60.8 21.8 %copy-start.9 = (bf16[3,2,128,256]{3,2,1,0:T(8,128)(2,1)S(1)}, bf16[3,2,128,256]{3,2,1,0:T(8,128)(2,1)}, u32[]{:S(2)}) copy-start(bf16[3,2,128,256]{3,2,1,0:T(8,128)(2,1)} %get-tuple-element.143.refs_0_) | copy-start | bytes 1179652
  76.6 10.2 %collective-permute-start.14 = (bf16[1280,1024]{1,0:T(8,128)(2,1)S(1)}, bf16[1280,1024]{1,0:T(8,128)(2,1)S(1)}, u32[]{:S(2)}, u32[]{:S(2)}) collective-permute-start(bf16[1280,1024]{1,0:T(8,128)(2,1)S(1)} %pad_maximum_fusion), channel_id=1, source_target_pairs={{0,1},{1,0},{2,3},{3,2},{4,5},{5,4},{6,7},{7,6},{8,9},{9,8},{10,11... | collective-permute-start | bytes 7864328 | tf_op jit(solution)/shard_map/ppermute | solution.py:70
  76.6 10.2 %collective-permute-start.15 = (bf16[3,2,128,1024]{3,2,1,0:T(8,128)(2,1)}, bf16[3,2,128,1024]{3,2,1,0:T(8,128)(2,1)S(1)}, u32[]{:S(2)}, u32[]{:S(2)}) collective-permute-start(bf16[3,2,128,1024]{3,2,1,0:T(8,128)(2,1)} %collective-permute-done.11.refs_2_), channel_id=1, source_target_pairs={{0,1},{1,0},{2,3},{3,2},{4,5},{5,4},{6,7},{7,6},{8,9},{9,8},{10,11... | collective-permute-start | bytes 4718600 | tf_op jit(solution)/shard_map/ppermute | solution.py:70
  77.1 41.5 %collective-permute-start.13 = (bf16[3,2,128,1024]{3,2,1,0:T(8,128)(2,1)S(1)}, bf16[3,2,128,1024]{3,2,1,0:T(8,128)(2,1)S(1)}, u32[]{:S(2)}, u32[]{:S(2)}) collective-permute-start(bf16[3,2,128,1024]{3,2,1,0:T(8,128)(2,1)S(1)} %copy-done.11), channel_id=1, source_target_pairs={{0,2},{1,3},{2,0},{3,1},{4,6},{5,7},{6,4},{7,5},{8,10},{9,11},{10,... | collective-permute-start | bytes 4718600 | tf_op jit(solution)/shard_map/ppermute | solution.py:70
  78.6 8.2 %collective-permute-start.16 = (bf16[2,256,512]{2,1,0:T(8,128)(2,1)}, bf16[2,256,512]{2,1,0:T(8,128)(2,1)S(1)}, u32[]{:S(2)}, u32[]{:S(2)}) collective-permute-start(bf16[2,256,512]{2,1,0:T(8,128)(2,1)} %collective-permute-done.6.refs_4_), channel_id=1, source_target_pairs={{0,1},{1,0},{2,3},{3,2},{4,5},{5,4},{6,7},{7,6},{8,9},{9,8},{10,11... | collective-permute-start | bytes 1572872 | tf_op jit(solution)/shard_map/ppermute | solution.py:70
  80.8 37.9 %collective-permute-start.12 = (bf16[6,2,128,256]{3,2,1,0:T(8,128)(2,1)S(1)}, bf16[6,2,128,256]{3,2,1,0:T(8,128)(2,1)S(1)}, u32[]{:S(2)}, u32[]{:S(2)}) collective-permute-start(bf16[6,2,128,256]{3,2,1,0:T(8,128)(2,1)S(1)} %partial_sums.3), channel_id=1, source_target_pairs={{0,16},{4,20},{8,24},{12,28},{16,0},{20,4},{24,8},{28,12},{1,17},{... | collective-permute-start | bytes 2359304 | tf_op jit(solution)/shard_map/ppermute | solution.py:70
  86.8 35.7 %collective-permute-start.17 = (bf16[3,2,128,256]{3,2,1,0:T(8,128)(2,1)S(1)}, bf16[3,2,128,256]{3,2,1,0:T(8,128)(2,1)S(1)}, u32[]{:S(2)}, u32[]{:S(2)}) collective-permute-start(bf16[3,2,128,256]{3,2,1,0:T(8,128)(2,1)S(1)} %get-tuple-element.166), channel_id=1, source_target_pairs={{0,4},{4,0},{8,12},{12,8},{16,20},{20,16},{24,28},{28,24},{1,5},{5... | collective-permute-start | bytes 1179656 | tf_op jit(solution)/shard_map/ppermute | solution.py:70
  87.4 35.2 %collective-permute-start.18 = (bf16[3,2,128,256]{3,2,1,0:T(8,128)(2,1)S(1)}, bf16[3,2,128,256]{3,2,1,0:T(8,128)(2,1)S(1)}, u32[]{:S(2)}, u32[]{:S(2)}) collective-permute-start(bf16[3,2,128,256]{3,2,1,0:T(8,128)(2,1)S(1)} %get-tuple-element.167), channel_id=1, source_target_pairs={{0,8},{4,12},{8,0},{12,4},{16,24},{20,28},{24,16},{28,20},{1,9},{5... | collective-permute-start | bytes 1179656 | tf_op jit(solution)/shard_map/ppermute | solution.py:70
  90.4 33.7 %collective-permute-start.19 = (bf16[3,2,128,256]{3,2,1,0:T(8,128)(2,1)S(1)}, bf16[3,2,128,256]{3,2,1,0:T(8,128)(2,1)S(1)}, u32[]{:S(2)}, u32[]{:S(2)}) collective-permute-start(bf16[3,2,128,256]{3,2,1,0:T(8,128)(2,1)S(1)} %get-tuple-element.168), channel_id=1, source_target_pairs={{0,12},{4,8},{8,4},{12,0},{16,28},{20,24},{24,20},{28,16},{1,13},{... | collective-permute-start | bytes 1179656 | tf_op jit(solution)/shard_map/ppermute | solution.py:70
  90.4 10.4 %copy-start.5 = (bf16[2,256,512]{2,1,0:T(8,128)(2,1)S(1)}, bf16[2,256,512]{2,1,0:T(8,128)(2,1)}, u32[]{:S(2)}) copy-start(bf16[2,256,512]{2,1,0:T(8,128)(2,1)} %reshape_squeeze.6.h_own) | copy-start | bytes 1572868
  100.8 28.9 %copy-start.4 = (bf16[2,256,512]{2,1,0:T(8,128)(2,1)S(1)}, bf16[2,256,512]{2,1,0:T(8,128)(2,1)}, u32[]{:S(2)}) copy-start(bf16[2,256,512]{2,1,0:T(8,128)(2,1)} %reshape_squeeze.7.h_own) | copy-start | bytes 1572868
  118.6 17.2 %slice-start = ((s8[6291456]{0:T(1024)(128)(4,1)}), s8[4194304]{0:T(1024)(128)(4,1)S(1)}, s32[]{:S(2)}) async-start(s8[6291456]{0:T(1024)(128)(4,1)} %bitcast.7), calls=%async_computation | async-start | bytes 8388608
  124.1 11.8 %slice-start.1 = ((s8[6291456]{0:T(1024)(128)(4,1)}), s8[2097152]{0:T(1024)(128)(4,1)S(1)}, s32[]{:S(2)}) async-start(s8[6291456]{0:T(1024)(128)(4,1)} %bitcast.7), calls=%async_computation.1 | async-start | bytes 4194304
  124.1 4.0 %collective-permute-start.20 = (bf16[3,2,128,1024]{3,2,1,0:T(8,128)(2,1)S(1)}, bf16[3,2,128,1024]{3,2,1,0:T(8,128)(2,1)S(1)}, u32[]{:S(2)}, u32[]{:S(2)}) collective-permute-start(bf16[3,2,128,1024]{3,2,1,0:T(8,128)(2,1)S(1)} %copy-done.11), channel_id=1, source_target_pairs={{0,1},{1,0},{2,3},{3,2},{4,5},{5,4},{6,7},{7,6},{8,9},{9,8},{10,11... | collective-permute-start | bytes 4718600 | tf_op jit(solution)/shard_map/ppermute | solution.py:70
  124.1 5.7 %collective-permute-start.21 = (bf16[3,2,128,1024]{3,2,1,0:T(8,128)(2,1)S(1)}, bf16[3,2,128,1024]{3,2,1,0:T(8,128)(2,1)S(1)}, u32[]{:S(2)}, u32[]{:S(2)}) collective-permute-start(bf16[3,2,128,1024]{3,2,1,0:T(8,128)(2,1)S(1)} %collective-permute-done.13.refs_2_), channel_id=1, source_target_pairs={{0,1},{1,0},{2,3},{3,2},{4,5},{5,4},{6,7},{7,6},{8,9},{9,8},{10,11... | collective-permute-start | bytes 4718600 | tf_op jit(solution)/shard_map/ppermute | solution.py:70
  124.6 15.3 %collective-permute-start.22 = (bf16[3,2,128,256]{3,2,1,0:T(8,128)(2,1)S(1)}, bf16[3,2,128,256]{3,2,1,0:T(8,128)(2,1)S(1)}, u32[]{:S(2)}, u32[]{:S(2)}) collective-permute-start(bf16[3,2,128,256]{3,2,1,0:T(8,128)(2,1)S(1)} %get-tuple-element.173), channel_id=1, source_target_pairs={{0,4},{4,0},{8,12},{12,8},{16,20},{20,16},{24,28},{28,24},{1,5},{5... | collective-permute-start | bytes 1179656 | tf_op jit(solution)/shard_map/ppermute | solution.py:70
  126.1 13.7 %collective-permute-start.23 = (bf16[3,2,128,256]{3,2,1,0:T(8,128)(2,1)S(1)}, bf16[3,2,128,256]{3,2,1,0:T(8,128)(2,1)S(1)}, u32[]{:S(2)}, u32[]{:S(2)}) collective-permute-start(bf16[3,2,128,256]{3,2,1,0:T(8,128)(2,1)S(1)} %get-tuple-element.174), channel_id=1, source_target_pairs={{0,8},{4,12},{8,0},{12,4},{16,24},{20,28},{24,16},{28,20},{1,9},{5... | collective-permute-start | bytes 1179656 | tf_op jit(solution)/shard_map/ppermute | solution.py:70
  126.2 19.1 %collective-permute-start.24 = (bf16[3,2,128,256]{3,2,1,0:T(8,128)(2,1)S(1)}, bf16[3,2,128,256]{3,2,1,0:T(8,128)(2,1)S(1)}, u32[]{:S(2)}, u32[]{:S(2)}) collective-permute-start(bf16[3,2,128,256]{3,2,1,0:T(8,128)(2,1)S(1)} %get-tuple-element.175), channel_id=1, source_target_pairs={{0,12},{4,8},{8,4},{12,0},{16,28},{20,24},{24,20},{28,16},{1,13},{... | collective-permute-start | bytes 1179656 | tf_op jit(solution)/shard_map/ppermute | solution.py:70

commit v4 on v3

--- a/solution.py
+++ b/solution.py
@@ -105,25 +105,25 @@
 def make_section(p, split, state, prev_slope, place, half_at, group, hamiltonian=None):
     ops, parts, rows, columns = state.shape
     height, width = rows // split, columns // group
-    block = pl.BlockSpec((1, 1, height, columns), lambda a, x, *_: (a, x, p, 0))
-    out = pl.BlockSpec((1, 1, height, columns), lambda a, x, *_: (a, x, 0, 0))
-    chunk = pl.BlockSpec((1, 1, height, width), lambda a, x, *_: (a, x, 0, 0))
-    half = (1, rows, columns // 2)
+    block = pl.BlockSpec((1, parts, height, columns), lambda a, *_: (a, 0, p, 0))
+    out = pl.BlockSpec((1, parts, height, columns), lambda a, *_: (a, 0, 0, 0))
+    chunk = pl.BlockSpec((1, parts, height, width), lambda a, *_: (a, 0, 0, 0))
+    half = (2, rows, columns // 2)
     extra = [] if hamiltonian is None else [hamiltonian]
     return pl.pallas_call(
         functools.partial(section_kernel, group),
         grid_spec=pltpu.PrefetchScalarGridSpec(
             num_scalar_prefetch=2,
-            grid=(ops, parts),
-            in_specs=[block, block] + [pl.BlockSpec(half, lambda a, x, _, h: (jnp.where(a == 0, x, parts - 1), 0, h[0])) for _ in extra],
-            out_specs=[pl.BlockSpec(half, lambda a, x, *_: (jnp.where(a == 0, x, parts - 1), 0, 0)) for _ in extra]
+            grid=(ops,),
+            in_specs=[block, block] + [pl.BlockSpec(half, lambda a, _, h: (0, 0, h[0])) for _ in extra],
+            out_specs=[pl.BlockSpec(half, lambda a, *_: (0, 0, 0)) for _ in extra]
             + [out]
             + [chunk] * group,
         ),
-        out_shape=[jax.ShapeDtypeStruct((parts, *half[1:]), bf16) for _ in extra]
+        out_shape=[jax.ShapeDtypeStruct(half, bf16) for _ in extra]
         + [jax.ShapeDtypeStruct((ops, parts, height, columns), bf16)]
         + [jax.ShapeDtypeStruct((ops, parts, height, width), bf16)] * group,
-        compiler_params=params(54 if p == 0 else 16),
+        compiler_params=params(60 if p == 0 else 16),
         cost_estimate=pl.CostEstimate(flops=1, bytes_accessed=1, transcendentals=0),
         name="section",
     )(place, half_at, state, prev_slope, *extra)
@@ -456,13 +456,13 @@
     top, low = bits[0], bits[1:]
 
     def spread(p):
-        return [chunks[p][0]] + [swap(chunks[p][b], "hier", hier, b) for b in range(1, group)]
+        return [swap(chunks[p][b], "hier", hier, b) for b in range(1, group)]
 
     def partial(p):
-        return make_partial(got[p], places, coupling, heres[p], vcols, links, sides)
+        return make_partial([owns[p], *got[p]], places, coupling, heres[p], vcols, links, sides)
 
     def coupled(p):
-        return make_coupled(got[p], received[p], places, coupling, heres[p], vcols, links, sides)
+        return make_coupled([owns[p], *got[p]], received[p], places, coupling, heres[p], vcols, links, sides)
 
     def gather_back(done):
         return [done[0]] + [swap(done[b], "hier", hier, b) for b in range(1, group)]
@@ -474,6 +474,7 @@
     half_columns, first, *first_chunks = make_section(
         0, split, state, prev_slope, own_place, half_at, group, hamiltonian
     )
+    owns = [first_chunks[0]]
     half_columns, first, first_chunks, half, state, prev_slope, couple_v, hamiltonian = tie(
         (half_columns, first, first_chunks, half, state, prev_slope, couple_v, hamiltonian)
     )
@@ -482,6 +483,7 @@
     second, *second_chunks = make_section(
         1, split, state, prev_slope, own_place, half_at, group
     )
+    owns.append(second_chunks[0])
     chunks, sections = [first_chunks, second_chunks], [first, second]
     got.append(spread(0))
 

time: 150 us -> 148 us (0.987)
  local copies, waits for them, and re-layouts: 22.7 us -> 25.5 us
  waiting for transfers between devices: 42.3 us -> 39.9 us
    unnamed x48, local copies, waits for them, and re-layouts: 5.96 us -> 8.73 us
    ppermute x25, waiting for transfers between devices: 42.3 us -> 39.9 us  [swap(): return lax.ppermute(array, axis, [(i, i ^ bit) for i in range(size)])]
  transfers between devices with their start and end apart: 25 -> 25, of which waited for: 8 -> 7; matrix products, arithmetic and copies ran while one was open for 12% -> 13% of each run, Pallas kernels for 33% -> 32%
where the time goes in v4:
time: 148 us
  Pallas kernels  51.9 us (35%)
  waiting for transfers between devices  39.9 us (27%)
  starting transfers between devices  27.6 us (19%)
  local copies, waits for them, and re-layouts  25.5 us (17%)
  other arithmetic  1.87 us (1%)
    ppermute x25, waiting for transfers between devices, swap(): return lax.ppermute(array, axis, [(i, i ^ bit) for i in range(size)])  39.9 us
    ppermute x25, starting transfers between devices, swap(): return lax.ppermute(array, axis, [(i, i ^ bit) for i in range(size)])  27.6 us
    pallas_call x2, Pallas kernels, make_left(): pl.pallas_call(functools.partial(left_kernel, count), grid=(columns // ti...  13 us
    pallas_call x1, Pallas kernels, make_right(): pl.pallas_call(functools.partial(right_kernel, split, count), grid=(colum...  10.4 us
    unnamed x48, local copies, waits for them, and re-layouts  8.73 us
    slice x1, local copies, waits for them, and re-layouts, shards(): blocks[:, :, :, p].reshape(2, rows, row * height)  8.67 us
    pallas_call x2, Pallas kernels, make_coupled(): pl.pallas_call(functools.partial(coupled_kernel, links, sides, group), in...  7.96 us
    pallas_call x2, Pallas kernels, make_final(): pl.pallas_call(functools.partial(final_kernel, group), grid_spec=pltpu.Pr...  7.92 us
  transfers between devices with their start and end apart: 25, of which 7 were waited for; matrix products, arithmetic and copies ran while one was open for 13% of the time, Pallas kernels for 32%

profile of v4, /device:TPU:0, one launch (start us, length us, event | category | flops | bytes accessed | tf_op | source)
XLA Modules:
  0.0 147.6 jit_solution(17755512876715389635)
XLA Ops:
  0.6 3.1 %collective-permute-start.1 = (s32[3,6]{1,0:T(4,128)}, s32[3,6]{1,0:T(4,128)S(1)}, u32[]{:S(2)}, u32[]{:S(2)}) collective-permute-start(s32[3,6]{1,0:T(4,128)} %param.18), channel_id=1, source_target_pairs={{0,8},{4,12},{8,0},{12,4},{16,24},{20,28},{24,16},{28,20},{1,9},{5... | collective-permute-start | bytes 224 | tf_op jit(solution)/shard_map/ppermute | solution.py:70
  3.7 1.5 %collective-permute-start = (s32[3,6]{1,0:T(4,128)}, s32[3,6]{1,0:T(4,128)S(1)}, u32[]{:S(2)}, u32[]{:S(2)}) collective-permute-start(s32[3,6]{1,0:T(4,128)} %param.18), channel_id=1, source_target_pairs={{0,4},{4,0},{8,12},{12,8},{16,20},{20,16},{24,28},{28,24},{1,5},{5... | collective-permute-start | bytes 224 | tf_op jit(solution)/shard_map/ppermute | solution.py:70
  5.2 0.1 collective-permute-start.2
  5.3 5.7 %section.2 = (bf16[2,256,512]{2,1,0:T(8,128)(2,1)}, bf16[3,2,128,1024]{3,2,1,0:T(8,128)(2,1)}, bf16[3,2,128,256]{3,2,1,0:T(8,128)(2,1)}, bf16[3,2,128,256]{3,2,1...) custom-call(s32[1]{0:T(128)} %bitcast.where, s32[1]{0:T(128)} %bitcast.2._, ...), custom_call_target="tpu_custom_call" | custom-call | flops 1 | bytes 1 | tf_op jit(solution)/shard_map/section/pallas_call | solution.py:113
  11.0 0.0 collective-permute-done
  11.0 0.5 copy-done.18
  11.5 0.0 copy-done.19
  11.6 0.0 copy-done.20
  11.6 1.9 %collective-permute-start.6 = (bf16[2,256,512]{2,1,0:T(8,128)(2,1)}, bf16[2,256,512]{2,1,0:T(8,128)(2,1)}, u32[]{:S(2)}, u32[]{:S(2)}) collective-permute-start(bf16[2,256,512]{2,1,0:T(8,128)(2,1)} %get-tuple-element.109), channel_id=1, source_target_pairs={{0,2},{1,3},{2,0},{3,1},{4,6},{5,7},{6,4},{7,5},{8,10},{9,11},{10,... | collective-permute-start | bytes 1572872 | tf_op jit(solution)/shard_map/ppermute | solution.py:70
  13.5 0.6 fusion
  14.1 1.5 %collective-permute-start.3 = (bf16[3,2,128,256]{3,2,1,0:T(8,128)(2,1)}, bf16[3,2,128,256]{3,2,1,0:T(8,128)(2,1)}, u32[]{:S(2)}, u32[]{:S(2)}) collective-permute-start(bf16[3,2,128,256]{3,2,1,0:T(8,128)(2,1)} %get-tuple-element.93), channel_id=1, source_target_pairs={{0,4},{4,0},{8,12},{12,8},{16,20},{20,16},{24,28},{28,24},{1,5},{5... | collective-permute-start | bytes 1179656 | tf_op jit(solution)/shard_map/ppermute | solution.py:70
  15.6 1.6 %collective-permute-start.4 = (bf16[3,2,128,256]{3,2,1,0:T(8,128)(2,1)}, bf16[3,2,128,256]{3,2,1,0:T(8,128)(2,1)}, u32[]{:S(2)}, u32[]{:S(2)}) collective-permute-start(bf16[3,2,128,256]{3,2,1,0:T(8,128)(2,1)} %get-tuple-element.94), channel_id=1, source_target_pairs={{0,8},{4,12},{8,0},{12,4},{16,24},{20,28},{24,16},{28,20},{1,9},{5... | collective-permute-start | bytes 1179656 | tf_op jit(solution)/shard_map/ppermute | solution.py:70
  17.1 0.4 collective-permute-start.5
  17.6 0.1 multiply_reduce_fusion.decay
  17.7 0.0 copy-start
  17.7 2.8 %copy-done = f32[3,2,256,1024]{3,2,1,0:T(8,128)S(1)} copy-done((f32[3,2,256,1024]{3,2,1,0:T(8,128)S(1)}, f32[3,2,256,1024]{3,2,1,0:T(8,128)}, u32[]{:S(2)}) %copy-start) | copy-done | bytes 6291480
  20.5 1.3 section.3
  21.8 0.8 copy-done.6
  22.5 1.1 copy-done.10
  23.7 0.8 copy-done.13
  24.5 0.8 copy-done.14
  25.3 0.8 copy-done.15
  26.1 0.9 copy.24.vrows
  27.0 0.9 copy.23.vrows
  27.9 0.7 pad_add_fusion
  28.6 0.8 compare_reduce_fusion
  29.5 4.3 %collective-permute-done.5.refs_3_ = bf16[3,2,128,256]{3,2,1,0:T(8,128)(2,1)} collective-permute-done((bf16[3,2,128,256]{3,2,1,0:T(8,128)(2,1)}, bf16[3,2,128,256]{3,2,1,0:T(8,128)(2,1)}, u32[]{:S(2)}, u32[]{:S(2)}) %collective-permute-start.5) | collective-permute-done | bytes 393248 | tf_op jit(solution)/shard_map/ppermute | solution.py:70
  33.7 0.4 collective-permute-start.11
  34.2 1.0 copy-done.8
  35.1 3.3 %partial_sums.2 = bf16[6,2,128,256]{3,2,1,0:T(8,128)(2,1)} custom-call(s32[24]{0:T(128)S(1)} %select_reduce_fusion.places, f32[2,6]{1,0:T(2,128)S(1)} %copy-done.12, f32[6,128,1]{2,1,0:T(8,128)S(1)} %copy.23.vrows, f32[6,256]{1,0:T(8,128)S(1)} %get-tuple-element.119.vcols, bf16[3,2,128,256]{3,2,1,0:T(8,128)(2,1)S(1)} %copy-done.8, ...), custom_call_target="tpu_custom_call" | custom-call | flops 7864320 | bytes 2359296 | tf_op jit(solution)/shard_map/partial_sums/pallas_call | solution.py:240
  38.4 2.9 %collective-permute-start.10 = (bf16[6,2,128,256]{3,2,1,0:T(8,128)(2,1)}, bf16[6,2,128,256]{3,2,1,0:T(8,128)(2,1)}, u32[]{:S(2)}, u32[]{:S(2)}) collective-permute-start(bf16[6,2,128,256]{3,2,1,0:T(8,128)(2,1)} %partial_sums.2), channel_id=1, source_target_pairs={{0,16},{4,20},{8,24},{12,28},{16,0},{20,4},{24,8},{28,12},{1,17},{... | collective-permute-start | bytes 2359304 | tf_op jit(solution)/shard_map/ppermute | solution.py:70
  41.3 1.5 %collective-permute-start.7 = (bf16[3,2,128,256]{3,2,1,0:T(8,128)(2,1)}, bf16[3,2,128,256]{3,2,1,0:T(8,128)(2,1)}, u32[]{:S(2)}, u32[]{:S(2)}) collective-permute-start(bf16[3,2,128,256]{3,2,1,0:T(8,128)(2,1)} %copy-done.15), channel_id=1, source_target_pairs={{0,4},{4,0},{8,12},{12,8},{16,20},{20,16},{24,28},{28,24},{1,5},{5... | collective-permute-start | bytes 1179656 | tf_op jit(solution)/shard_map/ppermute | solution.py:70
  42.8 1.6 %collective-permute-start.8 = (bf16[3,2,128,256]{3,2,1,0:T(8,128)(2,1)}, bf16[3,2,128,256]{3,2,1,0:T(8,128)(2,1)}, u32[]{:S(2)}, u32[]{:S(2)}) collective-permute-start(bf16[3,2,128,256]{3,2,1,0:T(8,128)(2,1)} %copy-done.14), channel_id=1, source_target_pairs={{0,8},{4,12},{8,0},{12,4},{16,24},{20,28},{24,16},{28,20},{1,9},{5... | collective-permute-start | bytes 1179656 | tf_op jit(solution)/shard_map/ppermute | solution.py:70
  44.4 0.4 collective-permute-start.9
  44.8 1.5 %reshape.30 = bf16[2,256,4,2,128]{4,3,2,1,0:T(2,128)(2,1)} reshape(bf16[2,256,1024]{2,1,0:T(8,128)(2,1)S(1)} %copy-done.2) | data formatting | bytes 2097152 | tf_op jit(solution)/shard_map/reshape | solution.py:508
  46.3 8.7 %slice_reduce_fusion = (bf16[2,256,4,128]{3,2,1,0:T(4,128)(2,1)}, bf16[2,256,4,128]{3,2,1,0:T(4,128)(2,1)}) fusion(bf16[2,256,4,2,128]{4,3,2,1,0:T(2,128)(2,1)} %reshape.30), kind=kLoop, calls=%fused_computation.1 | loop fusion | bytes 2097152 | tf_op jit(solution)/shard_map/slice | solution.py:509
  55.0 2.0 %reshape_squeeze.7.h_own = bf16[2,256,512]{2,1,0:T(8,128)(2,1)} reshape(bf16[2,256,4,128]{3,2,1,0:T(4,128)(2,1)} %get-tuple-element.172) | data formatting | bytes 1048576 | tf_op jit(solution)/shard_map/reshape;squeeze | solution.py:509
  57.1 2.0 %reshape_squeeze.6.h_own = bf16[2,256,512]{2,1,0:T(8,128)(2,1)} reshape(bf16[2,256,4,128]{3,2,1,0:T(4,128)(2,1)} %get-tuple-element.173) | data formatting | bytes 1048576 | tf_op jit(solution)/shard_map/reshape;squeeze | solution.py:509
  59.1 0.2 pad_maximum_fusion
  59.4 8.7 %collective-permute-done.8.refs_2_ = bf16[3,2,128,256]{3,2,1,0:T(8,128)(2,1)} collective-permute-done((bf16[3,2,128,256]{3,2,1,0:T(8,128)(2,1)}, bf16[3,2,128,256]{3,2,1,0:T(8,128)(2,1)}, u32[]{:S(2)}, u32[]{:S(2)}) %collective-permute-start.8) | collective-permute-done | bytes 393248 | tf_op jit(solution)/shard_map/ppermute | solution.py:70
  68.0 6.9 %collective-permute-done.9.refs_3_ = bf16[3,2,128,256]{3,2,1,0:T(8,128)(2,1)} collective-permute-done((bf16[3,2,128,256]{3,2,1,0:T(8,128)(2,1)}, bf16[3,2,128,256]{3,2,1,0:T(8,128)(2,1)}, u32[]{:S(2)}, u32[]{:S(2)}) %collective-permute-start.9) | collective-permute-done | bytes 393248 | tf_op jit(solution)/shard_map/ppermute | solution.py:70
  74.9 0.0 collective-permute-done.10.refs_4_
  74.9 0.0 collective-permute-done.11.refs_2_
  75.0 0.5 collective-permute-start.15
  75.5 1.5 %collective-permute-start.13 = (bf16[3,2,128,1024]{3,2,1,0:T(8,128)(2,1)S(1)}, bf16[3,2,128,1024]{3,2,1,0:T(8,128)(2,1)S(1)}, u32[]{:S(2)}, u32[]{:S(2)}) collective-permute-start(bf16[3,2,128,1024]{3,2,1,0:T(8,128)(2,1)S(1)} %copy-done.11), channel_id=1, source_target_pairs={{0,2},{1,3},{2,0},{3,1},{4,6},{5,7},{6,4},{7,5},{8,10},{9,11},{10,... | collective-permute-start | bytes 4718600 | tf_op jit(solution)/shard_map/ppermute | solution.py:70
  77.0 2.4 %partial_sums.3 = bf16[6,2,128,256]{3,2,1,0:T(8,128)(2,1)S(1)} custom-call(s32[24]{0:T(128)S(1)} %select_reduce_fusion.places, f32[2,6]{1,0:T(2,128)S(1)} %copy-done.12, f32[6,128,1]{2,1,0:T(8,128)S(1)} %copy.24.vrows, f32[6,256]{1,0:T(8,128)S(1)} %get-tuple-element.119.vcols, bf16[3,2,128,256]{3,2,1,0:T(8,128)(2,1)S(1)} %copy-done.7, ...), custom_call_target="tpu_custom_call" | custom-call | flops 7864320 | bytes 2359296 | tf_op jit(solution)/shard_map/partial_sums/pallas_call | solution.py:240
  79.4 1.2 collective-permute-start.12
  80.6 4.1 %coupling_sums.2 = (bf16[3,2,128,256]{3,2,1,0:T(8,128)(2,1)S(1)}, bf16[3,2,128,256]{3,2,1,0:T(8,128)(2,1)S(1)}, bf16[3,2,128,256]{3,2,1,0:T(8,128)(2,1)S(1)}, bf16[3,2,128,256]{3,2,1,0:T(8,128)(2,1)S(1)}) custom-call(s32[24]{0:T(128)S(1)} %select_reduce_fusion.places, f32[2,6]{1,0:T(2,128)S(1)} %copy-done.12, f32[6,128,1]{2,1,0:T(8,128)S(1)} %copy.23.vrows, ...), custom_call_target="tpu_custom_call" | custom-call | flops 1 | bytes 1 | tf_op jit(solution)/shard_map/coupling_sums/pallas_call | solution.py:261
  84.8 0.6 collective-permute-start.17
  85.4 3.0 %collective-permute-start.18 = (bf16[3,2,128,256]{3,2,1,0:T(8,128)(2,1)S(1)}, bf16[3,2,128,256]{3,2,1,0:T(8,128)(2,1)S(1)}, u32[]{:S(2)}, u32[]{:S(2)}) collective-permute-start(bf16[3,2,128,256]{3,2,1,0:T(8,128)(2,1)S(1)} %get-tuple-element.157), channel_id=1, source_target_pairs={{0,8},{4,12},{8,0},{12,4},{16,24},{20,28},{24,16},{28,20},{1,9},{5... | collective-permute-start | bytes 1179656 | tf_op jit(solution)/shard_map/ppermute | solution.py:70
  88.3 0.0 collective-permute-start.19
  88.3 10.4 %right_products.1.base = f32[3,2,256,1024]{3,2,1,0:T(8,128)S(1)} custom-call(s32[1]{0:T(128)} %bitcast.1.where, f32[3]{0:T(128)S(1)} %multiply_reduce_fusion.decay, bf16[2,256,1024]{2,1,0:T(8,128)(2,1)S(1)} %copy-done.2, bf16[3,2,128,1024]{3,2,1,0:T(8,128)(2,1)S(1)} %copy-done.3, bf16[3,2,128,1024]{3,2,1,0:T(8,128)(2,1)S(1)} %copy-done.11, ...), custom_call_target="tpu_custom_call" | custom-call | flops 6442450944 | bytes 13631488 | tf_op jit(solution)/shard_map/right_products/pallas_call | solution.py:324
  98.7 6.9 %left_products.2.base = f32[3,2,256,1024]{3,2,1,0:T(8,128)S(1)} custom-call(s32[1]{0:T(128)} %bitcast.1.where, bf16[2,256,512]{2,1,0:T(8,128)(2,1)S(1)} %copy-done.5, f32[3,2,256,1024]{3,2,1,0:T(8,128)S(1)} %right_products.1.base, bf16[3,2,128,1024]{3,2,1,0:T(8,128)(2,1)S(1)} %copy-done.3, ...), custom_call_target="tpu_custom_call" | custom-call | flops 3221225472 | bytes 18874368 | tf_op jit(solution)/shard_map/left_products/pallas_call | solution.py:360
  105.7 11.6 %collective-permute-done.12.refs_4_ = bf16[6,2,128,256]{3,2,1,0:T(8,128)(2,1)S(1)} collective-permute-done((bf16[6,2,128,256]{3,2,1,0:T(8,128)(2,1)S(1)}, bf16[6,2,128,256]{3,2,1,0:T(8,128)(2,1)S(1)}, u32[]{:S(2)}, u32[]{:S(2)}) %collective-permute-start.12) | collective-permute-done | bytes 786464 | tf_op jit(solution)/shard_map/ppermute | solution.py:70
  117.3 3.8 %coupling_sums.3 = (bf16[3,2,128,256]{3,2,1,0:T(8,128)(2,1)S(1)}, bf16[3,2,128,256]{3,2,1,0:T(8,128)(2,1)S(1)}, bf16[3,2,128,256]{3,2,1,0:T(8,128)(2,1)S(1)}, bf16[3,2,128,256]{3,2,1,0:T(8,128)(2,1)S(1)}) custom-call(s32[24]{0:T(128)S(1)} %select_reduce_fusion.places, f32[2,6]{1,0:T(2,128)S(1)} %copy-done.12, f32[6,128,1]{2,1,0:T(8,128)S(1)} %copy.24.vrows, ...), custom_call_target="tpu_custom_call" | custom-call | flops 1 | bytes 1 | tf_op jit(solution)/shard_map/coupling_sums/pallas_call | solution.py:261
  121.1 1.4 collective-permute-done.19.refs_3_
  122.5 0.5 collective-permute-start.21
  123.0 1.0 collective-permute-start.22
  124.1 2.4 %collective-permute-start.24 = (bf16[3,2,128,256]{3,2,1,0:T(8,128)(2,1)S(1)}, bf16[3,2,128,256]{3,2,1,0:T(8,128)(2,1)S(1)}, u32[]{:S(2)}, u32[]{:S(2)}) collective-permute-start(bf16[3,2,128,256]{3,2,1,0:T(8,128)(2,1)S(1)} %get-tuple-element.165), channel_id=1, source_target_pairs={{0,12},{4,8},{8,4},{12,0},{16,28},{20,24},{24,20},{28,16},{1,13},{... | collective-permute-start | bytes 1179656 | tf_op jit(solution)/shard_map/ppermute | solution.py:70
  126.5 1.7 %collective-permute-done.21.refs_3_ = bf16[3,2,128,1024]{3,2,1,0:T(8,128)(2,1)S(1)} collective-permute-done((bf16[3,2,128,1024]{3,2,1,0:T(8,128)(2,1)S(1)}, bf16[3,2,128,1024]{3,2,1,0:T(8,128)(2,1)S(1)}, u32[]{:S(2)}, u32[]{:S(2)}) %collective-permute-start.21) | collective-permute-done | bytes 1572896 | tf_op jit(solution)/shard_map/ppermute | solution.py:70
  128.2 6.1 %left_products.3.base = f32[3,2,256,1024]{3,2,1,0:T(8,128)S(1)} custom-call(s32[1]{0:T(128)} %bitcast.1.where, bf16[2,256,512]{2,1,0:T(8,128)(2,1)S(1)} %copy-done.4, f32[3,2,256,1024]{3,2,1,0:T(8,128)S(1)} %left_products.2.base, bf16[3,2,128,1024]{3,2,1,0:T(8,128)(2,1)S(1)} %copy-done.11, bf16[3,2,128,1024]{3,2,1,0:T(8,128)(2,1)S(1)} %collective-permute-done.20.refs_1_, ...), custom_call_target="tpu_custom_call" | custom-call | flops 3221225472 | bytes 18874368 | tf_op jit(solution)/shard_map/left_products/pallas_call | solution.py:360
  134.4 4.0 %outputs.2 = (f32[3,2,256,1024]{3,2,1,0:T(8,128)}, f32[3,2,256,1024]{3,2,1,0:T(8,128)}) custom-call(s32[1]{0:T(128)} %bitcast.where, f32[3,2,256,1024]{3,2,1,0:T(8,128)S(1)} %left_products.3.base, f32[3,2,256,1024]{3,2,1,0:T(8,128)S(1)} %bitcast.8, bf16[3,2,128,256]{3,2,1,0:T(8,128)(2,1)S(1)} %get-tuple-element.166.refs_0_, ...), custom_call_target="tpu_custom_call" | custom-call | flops 3145728 | bytes 14155776 | tf_op jit(solution)/shard_map/outputs/pallas_call | solution.py:408
  138.3 5.4 %collective-permute-done.24.refs_3_ = bf16[3,2,128,256]{3,2,1,0:T(8,128)(2,1)S(1)} collective-permute-done((bf16[3,2,128,256]{3,2,1,0:T(8,128)(2,1)S(1)}, bf16[3,2,128,256]{3,2,1,0:T(8,128)(2,1)S(1)}, u32[]{:S(2)}, u32[]{:S(2)}) %collective-permute-start.24) | collective-permute-done | bytes 393248 | tf_op jit(solution)/shard_map/ppermute | solution.py:70
  143.7 3.9 %outputs.3 = (f32[3,2,256,1024]{3,2,1,0:T(8,128)}, f32[3,2,256,1024]{3,2,1,0:T(8,128)}) custom-call(s32[1]{0:T(128)} %bitcast.where, f32[3,2,256,1024]{3,2,1,0:T(8,128)S(1)} %left_products.3.base, f32[3,2,256,1024]{3,2,1,0:T(8,128)S(1)} %bitcast.8, ...), custom_call_target="tpu_custom_call", output_to_operand_aliasing={{0}: (7, {}), {1}: (8, {})} | custom-call | flops 3145728 | bytes 14155776 | tf_op jit(solution)/shard_map/outputs/pallas_call | solution.py:408
  (59 shorter events, 0.1 us)
Async XLA Ops:
  0.6 10.3 %collective-permute-start.1 = (s32[3,6]{1,0:T(4,128)}, s32[3,6]{1,0:T(4,128)S(1)}, u32[]{:S(2)}, u32[]{:S(2)}) collective-permute-start(s32[3,6]{1,0:T(4,128)} %param.18), channel_id=1, source_target_pairs={{0,8},{4,12},{8,0},{12,4},{16,24},{20,28},{24,16},{28,20},{1,9},{5... | collective-permute-start | bytes 224 | tf_op jit(solution)/shard_map/ppermute | solution.py:70
  3.7 7.2 %collective-permute-start = (s32[3,6]{1,0:T(4,128)}, s32[3,6]{1,0:T(4,128)S(1)}, u32[]{:S(2)}, u32[]{:S(2)}) collective-permute-start(s32[3,6]{1,0:T(4,128)} %param.18), channel_id=1, source_target_pairs={{0,4},{4,0},{8,12},{12,8},{16,20},{20,16},{24,28},{28,24},{1,5},{5... | collective-permute-start | bytes 224 | tf_op jit(solution)/shard_map/ppermute | solution.py:70
  5.2 5.8 %collective-permute-start.2 = (s32[3,6]{1,0:T(4,128)}, s32[3,6]{1,0:T(4,128)S(1)}, u32[]{:S(2)}, u32[]{:S(2)}) collective-permute-start(s32[3,6]{1,0:T(4,128)} %param.18), channel_id=1, source_target_pairs={{0,12},{4,8},{8,4},{12,0},{16,28},{20,24},{24,20},{28,16},{1,13},{... | collective-permute-start | bytes 224 | tf_op jit(solution)/shard_map/ppermute | solution.py:70
  5.3 8.2 %copy-start.16 = (f32[6,1024]{1,0:T(8,128)S(1)}, f32[6,1024]{1,0:T(8,128)}, u32[]{:S(2)}) copy-start(f32[6,1024]{1,0:T(8,128)} %param.15) | copy-start | bytes 73732
  5.3 12.3 %copy-start.17 = (s32[3,6]{1,0:T(4,128)S(1)}, s32[3,6]{1,0:T(4,128)}, u32[]{:S(2)}) copy-start(s32[3,6]{1,0:T(4,128)} %param.18) | copy-start | bytes 220
  5.3 12.3 %copy-start.21 = (f32[6]{0:T(128)S(1)}, f32[6]{0:T(128)}, u32[]{:S(2)}) copy-start(f32[6]{0:T(128)} %param.17) | copy-start | bytes 76
  5.3 12.4 %copy-start.1 = (bf16[3,2,256,1024]{3,2,1,0:T(8,128)(2,1)S(1)}, bf16[3,2,256,1024]{3,2,1,0:T(8,128)(2,1)}, u32[]{:S(2)}) copy-start(bf16[3,2,256,1024]{3,2,1,0:T(8,128)(2,1)} %state.2) | copy-start | bytes 9437188
  10.9 0.6 copy-start.18
  11.0 0.6 copy-start.19
  11.0 0.6 copy-start.20
  11.6 22.2 %collective-permute-start.6 = (bf16[2,256,512]{2,1,0:T(8,128)(2,1)}, bf16[2,256,512]{2,1,0:T(8,128)(2,1)}, u32[]{:S(2)}, u32[]{:S(2)}) collective-permute-start(bf16[2,256,512]{2,1,0:T(8,128)(2,1)} %get-tuple-element.109), channel_id=1, source_target_pairs={{0,2},{1,3},{2,0},{3,1},{4,6},{5,7},{6,4},{7,5},{8,10},{9,11},{10,... | collective-permute-start | bytes 1572872 | tf_op jit(solution)/shard_map/ppermute | solution.py:70
  14.1 15.4 %collective-permute-start.3 = (bf16[3,2,128,256]{3,2,1,0:T(8,128)(2,1)}, bf16[3,2,128,256]{3,2,1,0:T(8,128)(2,1)}, u32[]{:S(2)}, u32[]{:S(2)}) collective-permute-start(bf16[3,2,128,256]{3,2,1,0:T(8,128)(2,1)} %get-tuple-element.93), channel_id=1, source_target_pairs={{0,4},{4,0},{8,12},{12,8},{16,20},{20,16},{24,28},{28,24},{1,5},{5... | collective-permute-start | bytes 1179656 | tf_op jit(solution)/shard_map/ppermute | solution.py:70
  15.6 13.9 %collective-permute-start.4 = (bf16[3,2,128,256]{3,2,1,0:T(8,128)(2,1)}, bf16[3,2,128,256]{3,2,1,0:T(8,128)(2,1)}, u32[]{:S(2)}, u32[]{:S(2)}) collective-permute-start(bf16[3,2,128,256]{3,2,1,0:T(8,128)(2,1)} %get-tuple-element.94), channel_id=1, source_target_pairs={{0,8},{4,12},{8,0},{12,4},{16,24},{20,28},{24,16},{28,20},{1,9},{5... | collective-permute-start | bytes 1179656 | tf_op jit(solution)/shard_map/ppermute | solution.py:70
  17.1 16.6 %collective-permute-start.5 = (bf16[3,2,128,256]{3,2,1,0:T(8,128)(2,1)}, bf16[3,2,128,256]{3,2,1,0:T(8,128)(2,1)}, u32[]{:S(2)}, u32[]{:S(2)}) collective-permute-start(bf16[3,2,128,256]{3,2,1,0:T(8,128)(2,1)} %get-tuple-element.95), channel_id=1, source_target_pairs={{0,12},{4,8},{8,4},{12,0},{16,28},{20,24},{24,20},{28,16},{1,13},{... | collective-permute-start | bytes 1179656 | tf_op jit(solution)/shard_map/ppermute | solution.py:70
  17.7 2.8 %copy-start = (f32[3,2,256,1024]{3,2,1,0:T(8,128)S(1)}, f32[3,2,256,1024]{3,2,1,0:T(8,128)}, u32[]{:S(2)}) copy-start(f32[3,2,256,1024]{3,2,1,0:T(8,128)} %slope.2) | copy-start | bytes 18874372
  20.5 13.7 %copy-start.12 = (f32[2,6]{1,0:T(2,128)S(1)}, f32[2,6]{1,0:T(2,128)}, u32[]{:S(2)}) copy-start(f32[2,6]{1,0:T(2,128)} %coupling.7) | copy-start | bytes 148
  21.7 0.8 copy-start.6
  22.5 1.1 copy-start.10
  23.7 0.8 copy-start.13
  24.5 0.8 copy-start.14
  25.3 0.8 copy-start.15
  26.1 18.7 %copy-start.2 = (bf16[2,256,1024]{2,1,0:T(8,128)(2,1)S(1)}, bf16[2,256,1024]{2,1,0:T(8,128)(2,1)}, u32[]{:S(2)}) copy-start(bf16[2,256,1024]{2,1,0:T(8,128)(2,1)} %h_own) | copy-start | bytes 3145732
  33.7 41.2 %collective-permute-start.11 = (bf16[3,2,128,1024]{3,2,1,0:T(8,128)(2,1)}, bf16[3,2,128,1024]{3,2,1,0:T(8,128)(2,1)}, u32[]{:S(2)}, u32[]{:S(2)}) collective-permute-start(bf16[3,2,128,1024]{3,2,1,0:T(8,128)(2,1)} %get-tuple-element.133.refs_0_), channel_id=1, source_target_pairs={{0,2},{1,3},{2,0},{3,1},{4,6},{5,7},{6,4},{7,5},{8,10},{9,11},{10,... | collective-permute-start | bytes 4718600 | tf_op jit(solution)/shard_map/ppermute | solution.py:70
  34.1 1.0 copy-start.8
  38.4 36.5 %collective-permute-start.10 = (bf16[6,2,128,256]{3,2,1,0:T(8,128)(2,1)}, bf16[6,2,128,256]{3,2,1,0:T(8,128)(2,1)}, u32[]{:S(2)}, u32[]{:S(2)}) collective-permute-start(bf16[6,2,128,256]{3,2,1,0:T(8,128)(2,1)} %partial_sums.2), channel_id=1, source_target_pairs={{0,16},{4,20},{8,24},{12,28},{16,0},{20,4},{24,8},{28,12},{1,17},{... | collective-permute-start | bytes 2359304 | tf_op jit(solution)/shard_map/ppermute | solution.py:70
  41.3 18.1 %collective-permute-start.7 = (bf16[3,2,128,256]{3,2,1,0:T(8,128)(2,1)}, bf16[3,2,128,256]{3,2,1,0:T(8,128)(2,1)}, u32[]{:S(2)}, u32[]{:S(2)}) collective-permute-start(bf16[3,2,128,256]{3,2,1,0:T(8,128)(2,1)} %copy-done.15), channel_id=1, source_target_pairs={{0,4},{4,0},{8,12},{12,8},{16,20},{20,16},{24,28},{28,24},{1,5},{5... | collective-permute-start | bytes 1179656 | tf_op jit(solution)/shard_map/ppermute | solution.py:70
  42.8 25.2 %collective-permute-start.8 = (bf16[3,2,128,256]{3,2,1,0:T(8,128)(2,1)}, bf16[3,2,128,256]{3,2,1,0:T(8,128)(2,1)}, u32[]{:S(2)}, u32[]{:S(2)}) collective-permute-start(bf16[3,2,128,256]{3,2,1,0:T(8,128)(2,1)} %copy-done.14), channel_id=1, source_target_pairs={{0,8},{4,12},{8,0},{12,4},{16,24},{20,28},{24,16},{28,20},{1,9},{5... | collective-permute-start | bytes 1179656 | tf_op jit(solution)/shard_map/ppermute | solution.py:70
  44.4 30.6 %collective-permute-start.9 = (bf16[3,2,128,256]{3,2,1,0:T(8,128)(2,1)}, bf16[3,2,128,256]{3,2,1,0:T(8,128)(2,1)}, u32[]{:S(2)}, u32[]{:S(2)}) collective-permute-start(bf16[3,2,128,256]{3,2,1,0:T(8,128)(2,1)} %copy-done.13), channel_id=1, source_target_pairs={{0,12},{4,8},{8,4},{12,0},{16,28},{20,24},{24,20},{28,16},{1,13},{... | collective-permute-start | bytes 1179656 | tf_op jit(solution)/shard_map/ppermute | solution.py:70
  46.3 12.8 %copy-start.3 = (bf16[3,2,128,1024]{3,2,1,0:T(8,128)(2,1)S(1)}, bf16[3,2,128,1024]{3,2,1,0:T(8,128)(2,1)}, u32[]{:S(2)}) copy-start(bf16[3,2,128,1024]{3,2,1,0:T(8,128)(2,1)} %get-tuple-element.133.refs_0_) | copy-start | bytes 4718596
  59.1 16.3 %copy-start.11 = (bf16[3,2,128,1024]{3,2,1,0:T(8,128)(2,1)S(1)}, bf16[3,2,128,1024]{3,2,1,0:T(8,128)(2,1)}, u32[]{:S(2)}) copy-start(bf16[3,2,128,1024]{3,2,1,0:T(8,128)(2,1)} %copy-done.10) | copy-start | bytes 4718596
  59.1 17.9 %copy-start.7 = (bf16[3,2,128,256]{3,2,1,0:T(8,128)(2,1)S(1)}, bf16[3,2,128,256]{3,2,1,0:T(8,128)(2,1)}, u32[]{:S(2)}) copy-start(bf16[3,2,128,256]{3,2,1,0:T(8,128)(2,1)} %copy-done.6) | copy-start | bytes 1179652
  59.1 21.5 %copy-start.9 = (bf16[3,2,128,256]{3,2,1,0:T(8,128)(2,1)S(1)}, bf16[3,2,128,256]{3,2,1,0:T(8,128)(2,1)}, u32[]{:S(2)}) copy-start(bf16[3,2,128,256]{3,2,1,0:T(8,128)(2,1)} %get-tuple-element.89.refs_0_) | copy-start | bytes 1179652
  74.9 9.8 %collective-permute-start.14 = (bf16[1280,1024]{1,0:T(8,128)(2,1)S(1)}, bf16[1280,1024]{1,0:T(8,128)(2,1)S(1)}, u32[]{:S(2)}, u32[]{:S(2)}) collective-permute-start(bf16[1280,1024]{1,0:T(8,128)(2,1)S(1)} %pad_maximum_fusion), channel_id=1, source_target_pairs={{0,1},{1,0},{2,3},{3,2},{4,5},{5,4},{6,7},{7,6},{8,9},{9,8},{10,11... | collective-permute-start | bytes 7864328 | tf_op jit(solution)/shard_map/ppermute | solution.py:70
  75.0 9.8 %collective-permute-start.15 = (bf16[3,2,128,1024]{3,2,1,0:T(8,128)(2,1)}, bf16[3,2,128,1024]{3,2,1,0:T(8,128)(2,1)S(1)}, u32[]{:S(2)}, u32[]{:S(2)}) collective-permute-start(bf16[3,2,128,1024]{3,2,1,0:T(8,128)(2,1)} %collective-permute-done.11.refs_2_), channel_id=1, source_target_pairs={{0,1},{1,0},{2,3},{3,2},{4,5},{5,4},{6,7},{7,6},{8,9},{9,8},{10,11... | collective-permute-start | bytes 4718600 | tf_op jit(solution)/shard_map/ppermute | solution.py:70
  75.5 41.8 %collective-permute-start.13 = (bf16[3,2,128,1024]{3,2,1,0:T(8,128)(2,1)S(1)}, bf16[3,2,128,1024]{3,2,1,0:T(8,128)(2,1)S(1)}, u32[]{:S(2)}, u32[]{:S(2)}) collective-permute-start(bf16[3,2,128,1024]{3,2,1,0:T(8,128)(2,1)S(1)} %copy-done.11), channel_id=1, source_target_pairs={{0,2},{1,3},{2,0},{3,1},{4,6},{5,7},{6,4},{7,5},{8,10},{9,11},{10,... | collective-permute-start | bytes 4718600 | tf_op jit(solution)/shard_map/ppermute | solution.py:70
  77.0 7.8 %collective-permute-start.16 = (bf16[2,256,512]{2,1,0:T(8,128)(2,1)}, bf16[2,256,512]{2,1,0:T(8,128)(2,1)S(1)}, u32[]{:S(2)}, u32[]{:S(2)}) collective-permute-start(bf16[2,256,512]{2,1,0:T(8,128)(2,1)} %collective-permute-done.6.refs_4_), channel_id=1, source_target_pairs={{0,1},{1,0},{2,3},{3,2},{4,5},{5,4},{6,7},{7,6},{8,9},{9,8},{10,11... | collective-permute-start | bytes 1572872 | tf_op jit(solution)/shard_map/ppermute | solution.py:70
  79.4 37.9 %collective-permute-start.12 = (bf16[6,2,128,256]{3,2,1,0:T(8,128)(2,1)S(1)}, bf16[6,2,128,256]{3,2,1,0:T(8,128)(2,1)S(1)}, u32[]{:S(2)}, u32[]{:S(2)}) collective-permute-start(bf16[6,2,128,256]{3,2,1,0:T(8,128)(2,1)S(1)} %partial_sums.3), channel_id=1, source_target_pairs={{0,16},{4,20},{8,24},{12,28},{16,0},{20,4},{24,8},{28,12},{1,17},{... | collective-permute-start | bytes 2359304 | tf_op jit(solution)/shard_map/ppermute | solution.py:70
  84.8 36.3 %collective-permute-start.17 = (bf16[3,2,128,256]{3,2,1,0:T(8,128)(2,1)S(1)}, bf16[3,2,128,256]{3,2,1,0:T(8,128)(2,1)S(1)}, u32[]{:S(2)}, u32[]{:S(2)}) collective-permute-start(bf16[3,2,128,256]{3,2,1,0:T(8,128)(2,1)S(1)} %get-tuple-element.156), channel_id=1, source_target_pairs={{0,4},{4,0},{8,12},{12,8},{16,20},{20,16},{24,28},{28,24},{1,5},{5... | collective-permute-start | bytes 1179656 | tf_op jit(solution)/shard_map/ppermute | solution.py:70
  85.4 35.7 %collective-permute-start.18 = (bf16[3,2,128,256]{3,2,1,0:T(8,128)(2,1)S(1)}, bf16[3,2,128,256]{3,2,1,0:T(8,128)(2,1)S(1)}, u32[]{:S(2)}, u32[]{:S(2)}) collective-permute-start(bf16[3,2,128,256]{3,2,1,0:T(8,128)(2,1)S(1)} %get-tuple-element.157), channel_id=1, source_target_pairs={{0,8},{4,12},{8,0},{12,4},{16,24},{20,28},{24,16},{28,20},{1,9},{5... | collective-permute-start | bytes 1179656 | tf_op jit(solution)/shard_map/ppermute | solution.py:70
  88.3 34.2 %collective-permute-start.19 = (bf16[3,2,128,256]{3,2,1,0:T(8,128)(2,1)S(1)}, bf16[3,2,128,256]{3,2,1,0:T(8,128)(2,1)S(1)}, u32[]{:S(2)}, u32[]{:S(2)}) collective-permute-start(bf16[3,2,128,256]{3,2,1,0:T(8,128)(2,1)S(1)} %get-tuple-element.158), channel_id=1, source_target_pairs={{0,12},{4,8},{8,4},{12,0},{16,28},{20,24},{24,20},{28,16},{1,13},{... | collective-permute-start | bytes 1179656 | tf_op jit(solution)/shard_map/ppermute | solution.py:70
  88.3 10.4 %copy-start.5 = (bf16[2,256,512]{2,1,0:T(8,128)(2,1)S(1)}, bf16[2,256,512]{2,1,0:T(8,128)(2,1)}, u32[]{:S(2)}) copy-start(bf16[2,256,512]{2,1,0:T(8,128)(2,1)} %reshape_squeeze.6.h_own) | copy-start | bytes 1572868
  98.7 29.5 %copy-start.4 = (bf16[2,256,512]{2,1,0:T(8,128)(2,1)S(1)}, bf16[2,256,512]{2,1,0:T(8,128)(2,1)}, u32[]{:S(2)}) copy-start(bf16[2,256,512]{2,1,0:T(8,128)(2,1)} %reshape_squeeze.7.h_own) | copy-start | bytes 1572868
  117.3 17.1 %slice-start = ((s8[6291456]{0:T(1024)(128)(4,1)}), s8[4194304]{0:T(1024)(128)(4,1)S(1)}, s32[]{:S(2)}) async-start(s8[6291456]{0:T(1024)(128)(4,1)} %bitcast.7), calls=%async_computation | async-start | bytes 8388608
  122.5 11.8 %slice-start.1 = ((s8[6291456]{0:T(1024)(128)(4,1)}), s8[2097152]{0:T(1024)(128)(4,1)S(1)}, s32[]{:S(2)}) async-start(s8[6291456]{0:T(1024)(128)(4,1)} %bitcast.7), calls=%async_computation.1 | async-start | bytes 4194304
  122.5 4.0 %collective-permute-start.20 = (bf16[3,2,128,1024]{3,2,1,0:T(8,128)(2,1)S(1)}, bf16[3,2,128,1024]{3,2,1,0:T(8,128)(2,1)S(1)}, u32[]{:S(2)}, u32[]{:S(2)}) collective-permute-start(bf16[3,2,128,1024]{3,2,1,0:T(8,128)(2,1)S(1)} %copy-done.11), channel_id=1, source_target_pairs={{0,1},{1,0},{2,3},{3,2},{4,5},{5,4},{6,7},{7,6},{8,9},{9,8},{10,11... | collective-permute-start | bytes 4718600 | tf_op jit(solution)/shard_map/ppermute | solution.py:70
  122.5 5.7 %collective-permute-start.21 = (bf16[3,2,128,1024]{3,2,1,0:T(8,128)(2,1)S(1)}, bf16[3,2,128,1024]{3,2,1,0:T(8,128)(2,1)S(1)}, u32[]{:S(2)}, u32[]{:S(2)}) collective-permute-start(bf16[3,2,128,1024]{3,2,1,0:T(8,128)(2,1)S(1)} %collective-permute-done.13.refs_2_), channel_id=1, source_target_pairs={{0,1},{1,0},{2,3},{3,2},{4,5},{5,4},{6,7},{7,6},{8,9},{9,8},{10,11... | collective-permute-start | bytes 4718600 | tf_op jit(solution)/shard_map/ppermute | solution.py:70
  123.0 15.3 %collective-permute-start.22 = (bf16[3,2,128,256]{3,2,1,0:T(8,128)(2,1)S(1)}, bf16[3,2,128,256]{3,2,1,0:T(8,128)(2,1)S(1)}, u32[]{:S(2)}, u32[]{:S(2)}) collective-permute-start(bf16[3,2,128,256]{3,2,1,0:T(8,128)(2,1)S(1)} %get-tuple-element.163), channel_id=1, source_target_pairs={{0,4},{4,0},{8,12},{12,8},{16,20},{20,16},{24,28},{28,24},{1,5},{5... | collective-permute-start | bytes 1179656 | tf_op jit(solution)/shard_map/ppermute | solution.py:70
  124.1 14.2 %collective-permute-start.23 = (bf16[3,2,128,256]{3,2,1,0:T(8,128)(2,1)S(1)}, bf16[3,2,128,256]{3,2,1,0:T(8,128)(2,1)S(1)}, u32[]{:S(2)}, u32[]{:S(2)}) collective-permute-start(bf16[3,2,128,256]{3,2,1,0:T(8,128)(2,1)S(1)} %get-tuple-element.164), channel_id=1, source_target_pairs={{0,8},{4,12},{8,0},{12,4},{16,24},{20,28},{24,16},{28,20},{1,9},{5... | collective-permute-start | bytes 1179656 | tf_op jit(solution)/shard_map/ppermute | solution.py:70
  124.1 19.6 %collective-permute-start.24 = (bf16[3,2,128,256]{3,2,1,0:T(8,128)(2,1)S(1)}, bf16[3,2,128,256]{3,2,1,0:T(8,128)(2,1)S(1)}, u32[]{:S(2)}, u32[]{:S(2)}) collective-permute-start(bf16[3,2,128,256]{3,2,1,0:T(8,128)(2,1)S(1)} %get-tuple-element.165), channel_id=1, source_target_pairs={{0,12},{4,8},{8,4},{12,0},{16,28},{20,24},{24,20},{28,16},{1,13},{... | collective-permute-start | bytes 1179656 | tf_op jit(solution)/shard_map/ppermute | solution.py:70

commit v5 on v4

--- a/solution.py
+++ b/solution.py
@@ -479,7 +479,7 @@
         (half_columns, first, first_chunks, half, state, prev_slope, couple_v, hamiltonian)
     )
 
-    h_top = swap(half_columns, "row", row, top)
+    h_top = [swap(half_columns[x : x + 1], "row", row, top) for x in range(2)]
     second, *second_chunks = make_section(
         1, split, state, prev_slope, own_place, half_at, group
     )
@@ -504,6 +504,7 @@
     received.append(swap(sent[0], "hier", hier, group))
     got.append(spread(1))
     across = swap(sections[0], "row", row, top)
+    h_top = jnp.concatenate(h_top)
     near = jnp.concatenate([sections[0].reshape(-1, columns), kept.reshape(-1, columns)])
     blocks = kept.reshape(2, rows, row, split, height)
     h_columns = [blocks[:, :, :, p].reshape(2, rows, row * height) for p in range(split)]

time: 148 us -> 148 us (level)
  waiting for transfers between devices: 39.9 us -> 37.2 us
    ppermute x25 -> x26, waiting for transfers between devices: 39.9 us -> 37.2 us  [swap(): return lax.ppermute(array, axis, [(i, i ^ bit) for i in range(size)])]
    slice x0 -> x1, local copies, waits for them, and re-layouts: none -> 1.84 us  [shards(): h_top = [swap(half_columns[x:x + 1], 'row', row, top) for x in range(2)]]
    ppermute x25 -> x26, starting transfers between devices: 27.6 us -> 28.4 us  [swap(): return lax.ppermute(array, axis, [(i, i ^ bit) for i in range(size)])]
    unnamed x48 -> x42, local copies, waits for them, and re-layouts: 8.73 us -> 7.99 us
  transfers between devices with their start and end apart: 25 -> 26, of which waited for: 7 -> 7; matrix products, arithmetic and copies ran while one was open for 13% -> 14% of each run, Pallas kernels for 32% -> 32%
where the time goes in v5:
time: 148 us
  Pallas kernels  51.4 us (35%)
  waiting for transfers between devices  37.2 us (25%)
  starting transfers between devices  28.4 us (19%)
  local copies, waits for them, and re-layouts  26.5 us (18%)
  other arithmetic  3.02 us (2%)
    ppermute x26, waiting for transfers between devices, swap(): return lax.ppermute(array, axis, [(i, i ^ bit) for i in range(size)])  37.2 us
    ppermute x26, starting transfers between devices, swap(): return lax.ppermute(array, axis, [(i, i ^ bit) for i in range(size)])  28.4 us
    pallas_call x2, Pallas kernels, make_left(): pl.pallas_call(functools.partial(left_kernel, count), grid=(columns // ti...  13.1 us
    pallas_call x1, Pallas kernels, make_right(): pl.pallas_call(functools.partial(right_kernel, split, count), grid=(colum...  9.77 us
    slice x1, local copies, waits for them, and re-layouts, shards(): blocks[:, :, :, p].reshape(2, rows, row * height)  8.65 us
    unnamed x42, local copies, waits for them, and re-layouts  7.99 us
    pallas_call x2, Pallas kernels, make_final(): pl.pallas_call(functools.partial(final_kernel, group), grid_spec=pltpu.Pr...  7.92 us
    pallas_call x2, Pallas kernels, make_coupled(): pl.pallas_call(functools.partial(coupled_kernel, links, sides, group), in...  7.84 us
  transfers between devices with their start and end apart: 26, of which 7 were waited for; matrix products, arithmetic and copies ran while one was open for 14% of the time, Pallas kernels for 32%

profile of v5, /device:TPU:0, one launch (start us, length us, event | category | flops | bytes accessed | tf_op | source)
XLA Modules:
  0.0 147.5 jit_solution(12744734951366986454)
XLA Ops:
  0.6 3.1 %collective-permute-start.1 = (s32[3,6]{1,0:T(4,128)}, s32[3,6]{1,0:T(4,128)S(1)}, u32[]{:S(2)}, u32[]{:S(2)}) collective-permute-start(s32[3,6]{1,0:T(4,128)} %param.18), channel_id=1, source_target_pairs={{0,8},{4,12},{8,0},{12,4},{16,24},{20,28},{24,16},{28,20},{1,9},{5... | collective-permute-start | bytes 224 | tf_op jit(solution)/shard_map/ppermute | solution.py:70
  3.7 1.5 %collective-permute-start = (s32[3,6]{1,0:T(4,128)}, s32[3,6]{1,0:T(4,128)S(1)}, u32[]{:S(2)}, u32[]{:S(2)}) collective-permute-start(s32[3,6]{1,0:T(4,128)} %param.18), channel_id=1, source_target_pairs={{0,4},{4,0},{8,12},{12,8},{16,20},{20,16},{24,28},{28,24},{1,5},{5... | collective-permute-start | bytes 224 | tf_op jit(solution)/shard_map/ppermute | solution.py:70
  5.2 0.0 collective-permute-start.2
  5.3 5.7 %section.2 = (bf16[2,256,512]{2,1,0:T(8,128)(2,1)}, bf16[3,2,128,1024]{3,2,1,0:T(8,128)(2,1)}, bf16[3,2,128,256]{3,2,1,0:T(8,128)(2,1)}, bf16[3,2,128,256]{3,2,1...) custom-call(s32[1]{0:T(128)} %bitcast.where, s32[1]{0:T(128)} %bitcast.2._, ...), custom_call_target="tpu_custom_call" | custom-call | flops 1 | bytes 1 | tf_op jit(solution)/shard_map/section/pallas_call | solution.py:113
  10.9 0.0 collective-permute-done.1
  11.0 0.0 collective-permute-done.2
  11.0 0.6 fusion.1
  11.6 1.9 %collective-permute-start.3 = (bf16[3,2,128,256]{3,2,1,0:T(8,128)(2,1)}, bf16[3,2,128,256]{3,2,1,0:T(8,128)(2,1)}, u32[]{:S(2)}, u32[]{:S(2)}) collective-permute-start(bf16[3,2,128,256]{3,2,1,0:T(8,128)(2,1)} %get-tuple-element.94), channel_id=1, source_target_pairs={{0,4},{4,0},{8,12},{12,8},{16,20},{20,16},{24,28},{28,24},{1,5},{5... | collective-permute-start | bytes 1179656 | tf_op jit(solution)/shard_map/ppermute | solution.py:70
  13.5 1.6 %collective-permute-start.4 = (bf16[3,2,128,256]{3,2,1,0:T(8,128)(2,1)}, bf16[3,2,128,256]{3,2,1,0:T(8,128)(2,1)}, u32[]{:S(2)}, u32[]{:S(2)}) collective-permute-start(bf16[3,2,128,256]{3,2,1,0:T(8,128)(2,1)} %get-tuple-element.95), channel_id=1, source_target_pairs={{0,8},{4,12},{8,0},{12,4},{16,24},{20,28},{24,16},{28,20},{1,9},{5... | collective-permute-start | bytes 1179656 | tf_op jit(solution)/shard_map/ppermute | solution.py:70
  15.0 0.0 collective-permute-start.5
  15.1 1.8 %fusion = (bf16[1,256,512]{2,1,0:T(8,128)(2,1)}, bf16[1,256,512]{2,1,0:T(8,128)(2,1)}) fusion(bf16[2,256,512]{2,1,0:T(8,128)(2,1)} %get-tuple-element.110), kind=kLoop, calls=%fused_computation.10 | loop fusion | bytes 1048576 | tf_op jit(solution)/shard_map/slice | solution.py:482
  16.9 1.9 %collective-permute-start.7 = (bf16[1,256,512]{2,1,0:T(8,128)(2,1)}, bf16[1,256,512]{2,1,0:T(8,128)(2,1)}, u32[]{:S(2)}, u32[]{:S(2)}) collective-permute-start(bf16[1,256,512]{2,1,0:T(8,128)(2,1)} %get-tuple-element.176), channel_id=1, source_target_pairs={{0,2},{1,3},{2,0},{3,1},{4,6},{5,7},{6,4},{7,5},{8,10},{9,11},{10,... | collective-permute-start | bytes 786440 | tf_op jit(solution)/shard_map/ppermute | solution.py:70
  18.8 0.1 collective-permute-start.6
  19.0 0.6 pad_add_fusion
  19.6 0.1 multiply_reduce_fusion.decay
  19.7 0.0 copy-start
  19.7 2.8 %copy-done = f32[3,2,256,1024]{3,2,1,0:T(8,128)S(1)} copy-done((f32[3,2,256,1024]{3,2,1,0:T(8,128)S(1)}, f32[3,2,256,1024]{3,2,1,0:T(8,128)}, u32[]{:S(2)}) %copy-start) | copy-done | bytes 6291480
  22.5 1.3 section.3
  23.8 0.7 copy-done.8
  24.5 1.1 copy-done.10
  25.6 0.8 copy-done.13
  26.4 0.8 copy-done.14
  27.2 0.8 copy-done.15
  27.9 0.9 copy.24.vrows
  28.9 0.9 copy.23.vrows
  29.7 0.8 compare_reduce_fusion
  30.6 0.0 collective-permute-done.7
  30.6 1.2 collective-permute-done.5.refs_3_
  31.8 1.6 %collective-permute-start.12 = (bf16[3,2,128,1024]{3,2,1,0:T(8,128)(2,1)}, bf16[3,2,128,1024]{3,2,1,0:T(8,128)(2,1)}, u32[]{:S(2)}, u32[]{:S(2)}) collective-permute-start(bf16[3,2,128,1024]{3,2,1,0:T(8,128)(2,1)} %get-tuple-element.135.refs_0_), channel_id=1, source_target_pairs={{0,2},{1,3},{2,0},{3,1},{4,6},{5,7},{6,4},{7,5},{8,10},{9,11},{10,... | collective-permute-start | bytes 4718600 | tf_op jit(solution)/shard_map/ppermute | solution.py:70
  33.4 1.5 %collective-permute-start.8 = (bf16[3,2,128,256]{3,2,1,0:T(8,128)(2,1)}, bf16[3,2,128,256]{3,2,1,0:T(8,128)(2,1)}, u32[]{:S(2)}, u32[]{:S(2)}) collective-permute-start(bf16[3,2,128,256]{3,2,1,0:T(8,128)(2,1)} %copy-done.15), channel_id=1, source_target_pairs={{0,4},{4,0},{8,12},{12,8},{16,20},{20,16},{24,28},{28,24},{1,5},{5... | collective-permute-start | bytes 1179656 | tf_op jit(solution)/shard_map/ppermute | solution.py:70
  34.9 1.6 %collective-permute-start.9 = (bf16[3,2,128,256]{3,2,1,0:T(8,128)(2,1)}, bf16[3,2,128,256]{3,2,1,0:T(8,128)(2,1)}, u32[]{:S(2)}, u32[]{:S(2)}) collective-permute-start(bf16[3,2,128,256]{3,2,1,0:T(8,128)(2,1)} %copy-done.14), channel_id=1, source_target_pairs={{0,8},{4,12},{8,0},{12,4},{16,24},{20,28},{24,16},{28,20},{1,9},{5... | collective-permute-start | bytes 1179656 | tf_op jit(solution)/shard_map/ppermute | solution.py:70
  36.5 0.4 collective-permute-start.10
  36.9 1.0 copy-done.6
  37.9 3.4 %partial_sums.2 = bf16[6,2,128,256]{3,2,1,0:T(8,128)(2,1)} custom-call(s32[24]{0:T(128)S(1)} %select_reduce_fusion.places, f32[2,6]{1,0:T(2,128)S(1)} %copy-done.12, f32[6,128,1]{2,1,0:T(8,128)S(1)} %copy.23.vrows, f32[6,256]{1,0:T(8,128)S(1)} %get-tuple-element.120.vcols, bf16[3,2,128,256]{3,2,1,0:T(8,128)(2,1)S(1)} %copy-done.6, ...), custom_call_target="tpu_custom_call" | custom-call | flops 7864320 | bytes 2359296 | tf_op jit(solution)/shard_map/partial_sums/pallas_call | solution.py:240
  41.3 2.6 %collective-permute-start.11 = (bf16[6,2,128,256]{3,2,1,0:T(8,128)(2,1)}, bf16[6,2,128,256]{3,2,1,0:T(8,128)(2,1)}, u32[]{:S(2)}, u32[]{:S(2)}) collective-permute-start(bf16[6,2,128,256]{3,2,1,0:T(8,128)(2,1)} %partial_sums.2), channel_id=1, source_target_pairs={{0,16},{4,20},{8,24},{12,28},{16,0},{20,4},{24,8},{28,12},{1,17},{... | collective-permute-start | bytes 2359304 | tf_op jit(solution)/shard_map/ppermute | solution.py:70
  43.9 1.5 %reshape.30 = bf16[2,256,4,2,128]{4,3,2,1,0:T(2,128)(2,1)} reshape(bf16[2,256,1024]{2,1,0:T(8,128)(2,1)S(1)} %copy-done.2) | data formatting | bytes 2097152 | tf_op jit(solution)/shard_map/reshape | solution.py:509
  45.4 8.7 %slice_reduce_fusion = (bf16[2,256,4,128]{3,2,1,0:T(4,128)(2,1)}, bf16[2,256,4,128]{3,2,1,0:T(4,128)(2,1)}) fusion(bf16[2,256,4,2,128]{4,3,2,1,0:T(2,128)(2,1)} %reshape.30), kind=kLoop, calls=%fused_computation.1 | loop fusion | bytes 2097152 | tf_op jit(solution)/shard_map/slice | solution.py:510
  54.1 2.0 %reshape_squeeze.7.h_own = bf16[2,256,512]{2,1,0:T(8,128)(2,1)} reshape(bf16[2,256,4,128]{3,2,1,0:T(4,128)(2,1)} %get-tuple-element.174) | data formatting | bytes 1048576 | tf_op jit(solution)/shard_map/reshape;squeeze | solution.py:510
  56.1 2.0 %reshape_squeeze.6.h_own = bf16[2,256,512]{2,1,0:T(8,128)(2,1)} reshape(bf16[2,256,4,128]{3,2,1,0:T(4,128)(2,1)} %get-tuple-element.175) | data formatting | bytes 1048576 | tf_op jit(solution)/shard_map/reshape;squeeze | solution.py:510
  58.2 1.2 pad_maximum_fusion.1.refs_4_
  59.4 0.2 pad_maximum_fusion
  59.7 3.4 %collective-permute-done.10.refs_3_ = bf16[3,2,128,256]{3,2,1,0:T(8,128)(2,1)} collective-permute-done((bf16[3,2,128,256]{3,2,1,0:T(8,128)(2,1)}, bf16[3,2,128,256]{3,2,1,0:T(8,128)(2,1)}, u32[]{:S(2)}, u32[]{:S(2)}) %collective-permute-start.10) | collective-permute-done | bytes 393248 | tf_op jit(solution)/shard_map/ppermute | solution.py:70
  63.1 12.5 %collective-permute-done.11.refs_4_ = bf16[6,2,128,256]{3,2,1,0:T(8,128)(2,1)} collective-permute-done((bf16[6,2,128,256]{3,2,1,0:T(8,128)(2,1)}, bf16[6,2,128,256]{3,2,1,0:T(8,128)(2,1)}, u32[]{:S(2)}, u32[]{:S(2)}) %collective-permute-start.11) | collective-permute-done | bytes 786464 | tf_op jit(solution)/shard_map/ppermute | solution.py:70
  75.6 0.5 collective-permute-start.16
  76.1 0.7 collective-permute-start.14
  76.8 2.5 %partial_sums.3 = bf16[6,2,128,256]{3,2,1,0:T(8,128)(2,1)S(1)} custom-call(s32[24]{0:T(128)S(1)} %select_reduce_fusion.places, f32[2,6]{1,0:T(2,128)S(1)} %copy-done.12, f32[6,128,1]{2,1,0:T(8,128)S(1)} %copy.24.vrows, f32[6,256]{1,0:T(8,128)S(1)} %get-tuple-element.120.vcols, bf16[3,2,128,256]{3,2,1,0:T(8,128)(2,1)S(1)} %copy-done.9, ...), custom_call_target="tpu_custom_call" | custom-call | flops 7864320 | bytes 2359296 | tf_op jit(solution)/shard_map/partial_sums/pallas_call | solution.py:240
  79.3 0.1 collective-permute-start.13
  79.4 4.1 %coupling_sums.2 = (bf16[3,2,128,256]{3,2,1,0:T(8,128)(2,1)S(1)}, bf16[3,2,128,256]{3,2,1,0:T(8,128)(2,1)S(1)}, bf16[3,2,128,256]{3,2,1,0:T(8,128)(2,1)S(1)}, bf16[3,2,128,256]{3,2,1,0:T(8,128)(2,1)S(1)}) custom-call(s32[24]{0:T(128)S(1)} %select_reduce_fusion.places, f32[2,6]{1,0:T(2,128)S(1)} %copy-done.12, f32[6,128,1]{2,1,0:T(8,128)S(1)} %copy.23.vrows, ...), custom_call_target="tpu_custom_call" | custom-call | flops 1 | bytes 1 | tf_op jit(solution)/shard_map/coupling_sums/pallas_call | solution.py:261
  83.5 0.0 collective-permute-done.17.refs_5_
  83.5 1.5 %collective-permute-start.18 = (bf16[3,2,128,256]{3,2,1,0:T(8,128)(2,1)S(1)}, bf16[3,2,128,256]{3,2,1,0:T(8,128)(2,1)S(1)}, u32[]{:S(2)}, u32[]{:S(2)}) collective-permute-start(bf16[3,2,128,256]{3,2,1,0:T(8,128)(2,1)S(1)} %get-tuple-element.158), channel_id=1, source_target_pairs={{0,4},{4,0},{8,12},{12,8},{16,20},{20,16},{24,28},{28,24},{1,5},{5... | collective-permute-start | bytes 1179656 | tf_op jit(solution)/shard_map/ppermute | solution.py:70
  85.0 3.9 %collective-permute-start.19 = (bf16[3,2,128,256]{3,2,1,0:T(8,128)(2,1)S(1)}, bf16[3,2,128,256]{3,2,1,0:T(8,128)(2,1)S(1)}, u32[]{:S(2)}, u32[]{:S(2)}) collective-permute-start(bf16[3,2,128,256]{3,2,1,0:T(8,128)(2,1)S(1)} %get-tuple-element.159), channel_id=1, source_target_pairs={{0,8},{4,12},{8,0},{12,4},{16,24},{20,28},{24,16},{28,20},{1,9},{5... | collective-permute-start | bytes 1179656 | tf_op jit(solution)/shard_map/ppermute | solution.py:70
  88.9 9.8 %right_products.1.base = f32[3,2,256,1024]{3,2,1,0:T(8,128)S(1)} custom-call(s32[1]{0:T(128)} %bitcast.1.where, f32[3]{0:T(128)S(1)} %multiply_reduce_fusion.decay, bf16[2,256,1024]{2,1,0:T(8,128)(2,1)S(1)} %copy-done.2, bf16[3,2,128,1024]{3,2,1,0:T(8,128)(2,1)S(1)} %copy-done.3, bf16[3,2,128,1024]{3,2,1,0:T(8,128)(2,1)S(1)} %copy-done.11, ...), custom_call_target="tpu_custom_call" | custom-call | flops 6442450944 | bytes 13631488 | tf_op jit(solution)/shard_map/right_products/pallas_call | solution.py:324
  98.7 6.9 %left_products.2.base = f32[3,2,256,1024]{3,2,1,0:T(8,128)S(1)} custom-call(s32[1]{0:T(128)} %bitcast.1.where, bf16[2,256,512]{2,1,0:T(8,128)(2,1)S(1)} %copy-done.5, f32[3,2,256,1024]{3,2,1,0:T(8,128)S(1)} %right_products.1.base, bf16[3,2,128,1024]{3,2,1,0:T(8,128)(2,1)S(1)} %copy-done.3, ...), custom_call_target="tpu_custom_call" | custom-call | flops 3221225472 | bytes 18874368 | tf_op jit(solution)/shard_map/left_products/pallas_call | solution.py:360
  105.6 11.6 %collective-permute-done.13.refs_4_ = bf16[6,2,128,256]{3,2,1,0:T(8,128)(2,1)S(1)} collective-permute-done((bf16[6,2,128,256]{3,2,1,0:T(8,128)(2,1)S(1)}, bf16[6,2,128,256]{3,2,1,0:T(8,128)(2,1)S(1)}, u32[]{:S(2)}, u32[]{:S(2)}) %collective-permute-start.13) | collective-permute-done | bytes 786464 | tf_op jit(solution)/shard_map/ppermute | solution.py:70
  117.2 3.8 %coupling_sums.3 = (bf16[3,2,128,256]{3,2,1,0:T(8,128)(2,1)S(1)}, bf16[3,2,128,256]{3,2,1,0:T(8,128)(2,1)S(1)}, bf16[3,2,128,256]{3,2,1,0:T(8,128)(2,1)S(1)}, bf16[3,2,128,256]{3,2,1,0:T(8,128)(2,1)S(1)}) custom-call(s32[24]{0:T(128)S(1)} %select_reduce_fusion.places, f32[2,6]{1,0:T(2,128)S(1)} %copy-done.12, f32[6,128,1]{2,1,0:T(8,128)S(1)} %copy.24.vrows, ...), custom_call_target="tpu_custom_call" | custom-call | flops 1 | bytes 1 | tf_op jit(solution)/shard_map/coupling_sums/pallas_call | solution.py:261
  121.0 1.4 collective-permute-done.20.refs_3_
  122.5 0.5 collective-permute-start.22
  123.0 1.7 %collective-permute-start.23 = (bf16[3,2,128,256]{3,2,1,0:T(8,128)(2,1)S(1)}, bf16[3,2,128,256]{3,2,1,0:T(8,128)(2,1)S(1)}, u32[]{:S(2)}, u32[]{:S(2)}) collective-permute-start(bf16[3,2,128,256]{3,2,1,0:T(8,128)(2,1)S(1)} %get-tuple-element.165), channel_id=1, source_target_pairs={{0,4},{4,0},{8,12},{12,8},{16,20},{20,16},{24,28},{28,24},{1,5},{5... | collective-permute-start | bytes 1179656 | tf_op jit(solution)/shard_map/ppermute | solution.py:70
  124.7 1.8 %collective-permute-start.25 = (bf16[3,2,128,256]{3,2,1,0:T(8,128)(2,1)S(1)}, bf16[3,2,128,256]{3,2,1,0:T(8,128)(2,1)S(1)}, u32[]{:S(2)}, u32[]{:S(2)}) collective-permute-start(bf16[3,2,128,256]{3,2,1,0:T(8,128)(2,1)S(1)} %get-tuple-element.167), channel_id=1, source_target_pairs={{0,12},{4,8},{8,4},{12,0},{16,28},{20,24},{24,20},{28,16},{1,13},{... | collective-permute-start | bytes 1179656 | tf_op jit(solution)/shard_map/ppermute | solution.py:70
  126.5 1.7 %collective-permute-done.22.refs_3_ = bf16[3,2,128,1024]{3,2,1,0:T(8,128)(2,1)S(1)} collective-permute-done((bf16[3,2,128,1024]{3,2,1,0:T(8,128)(2,1)S(1)}, bf16[3,2,128,1024]{3,2,1,0:T(8,128)(2,1)S(1)}, u32[]{:S(2)}, u32[]{:S(2)}) %collective-permute-start.22) | collective-permute-done | bytes 1572896 | tf_op jit(solution)/shard_map/ppermute | solution.py:70
  128.1 6.2 %left_products.3.base = f32[3,2,256,1024]{3,2,1,0:T(8,128)S(1)} custom-call(s32[1]{0:T(128)} %bitcast.1.where, bf16[2,256,512]{2,1,0:T(8,128)(2,1)S(1)} %copy-done.4, f32[3,2,256,1024]{3,2,1,0:T(8,128)S(1)} %left_products.2.base, bf16[3,2,128,1024]{3,2,1,0:T(8,128)(2,1)S(1)} %copy-done.11, bf16[3,2,128,1024]{3,2,1,0:T(8,128)(2,1)S(1)} %collective-permute-done.21.refs_1_, ...), custom_call_target="tpu_custom_call" | custom-call | flops 3221225472 | bytes 18874368 | tf_op jit(solution)/shard_map/left_products/pallas_call | solution.py:360
  134.3 4.0 %outputs.2 = (f32[3,2,256,1024]{3,2,1,0:T(8,128)}, f32[3,2,256,1024]{3,2,1,0:T(8,128)}) custom-call(s32[1]{0:T(128)} %bitcast.where, f32[3,2,256,1024]{3,2,1,0:T(8,128)S(1)} %left_products.3.base, f32[3,2,256,1024]{3,2,1,0:T(8,128)S(1)} %bitcast.8, bf16[3,2,128,256]{3,2,1,0:T(8,128)(2,1)S(1)} %get-tuple-element.168.refs_0_, ...), custom_call_target="tpu_custom_call" | custom-call | flops 3145728 | bytes 14155776 | tf_op jit(solution)/shard_map/outputs/pallas_call | solution.py:408
  138.3 5.3 %collective-permute-done.25.refs_3_ = bf16[3,2,128,256]{3,2,1,0:T(8,128)(2,1)S(1)} collective-permute-done((bf16[3,2,128,256]{3,2,1,0:T(8,128)(2,1)S(1)}, bf16[3,2,128,256]{3,2,1,0:T(8,128)(2,1)S(1)}, u32[]{:S(2)}, u32[]{:S(2)}) %collective-permute-start.25) | collective-permute-done | bytes 393248 | tf_op jit(solution)/shard_map/ppermute | solution.py:70
  143.6 3.9 %outputs.3 = (f32[3,2,256,1024]{3,2,1,0:T(8,128)}, f32[3,2,256,1024]{3,2,1,0:T(8,128)}) custom-call(s32[1]{0:T(128)} %bitcast.where, f32[3,2,256,1024]{3,2,1,0:T(8,128)S(1)} %left_products.3.base, f32[3,2,256,1024]{3,2,1,0:T(8,128)S(1)} %bitcast.8, ...), custom_call_target="tpu_custom_call", output_to_operand_aliasing={{0}: (7, {}), {1}: (8, {})} | custom-call | flops 3145728 | bytes 14155776 | tf_op jit(solution)/shard_map/outputs/pallas_call | solution.py:408
  (57 shorter events, 0.2 us)
Async XLA Ops:
  0.6 10.3 %collective-permute-start.1 = (s32[3,6]{1,0:T(4,128)}, s32[3,6]{1,0:T(4,128)S(1)}, u32[]{:S(2)}, u32[]{:S(2)}) collective-permute-start(s32[3,6]{1,0:T(4,128)} %param.18), channel_id=1, source_target_pairs={{0,8},{4,12},{8,0},{12,4},{16,24},{20,28},{24,16},{28,20},{1,9},{5... | collective-permute-start | bytes 224 | tf_op jit(solution)/shard_map/ppermute | solution.py:70
  3.7 7.2 %collective-permute-start = (s32[3,6]{1,0:T(4,128)}, s32[3,6]{1,0:T(4,128)S(1)}, u32[]{:S(2)}, u32[]{:S(2)}) collective-permute-start(s32[3,6]{1,0:T(4,128)} %param.18), channel_id=1, source_target_pairs={{0,4},{4,0},{8,12},{12,8},{16,20},{20,16},{24,28},{28,24},{1,5},{5... | collective-permute-start | bytes 224 | tf_op jit(solution)/shard_map/ppermute | solution.py:70
  5.2 5.7 %collective-permute-start.2 = (s32[3,6]{1,0:T(4,128)}, s32[3,6]{1,0:T(4,128)S(1)}, u32[]{:S(2)}, u32[]{:S(2)}) collective-permute-start(s32[3,6]{1,0:T(4,128)} %param.18), channel_id=1, source_target_pairs={{0,12},{4,8},{8,4},{12,0},{16,28},{20,24},{24,20},{28,16},{1,13},{... | collective-permute-start | bytes 224 | tf_op jit(solution)/shard_map/ppermute | solution.py:70
  5.3 5.7 %copy-start.16 = (f32[6,1024]{1,0:T(8,128)S(1)}, f32[6,1024]{1,0:T(8,128)}, u32[]{:S(2)}) copy-start(f32[6,1024]{1,0:T(8,128)} %param.15) | copy-start | bytes 73732
  5.3 13.7 %copy-start.17 = (s32[3,6]{1,0:T(4,128)S(1)}, s32[3,6]{1,0:T(4,128)}, u32[]{:S(2)}) copy-start(s32[3,6]{1,0:T(4,128)} %param.18) | copy-start | bytes 220
  5.3 14.3 %copy-start.18 = (f32[6]{0:T(128)S(1)}, f32[6]{0:T(128)}, u32[]{:S(2)}) copy-start(f32[6]{0:T(128)} %param.17) | copy-start | bytes 76
  5.3 14.4 %copy-start.1 = (bf16[3,2,256,1024]{3,2,1,0:T(8,128)(2,1)S(1)}, bf16[3,2,256,1024]{3,2,1,0:T(8,128)(2,1)}, u32[]{:S(2)}) copy-start(bf16[3,2,256,1024]{3,2,1,0:T(8,128)(2,1)} %state.2) | copy-start | bytes 9437188
  11.6 19.0 %collective-permute-start.3 = (bf16[3,2,128,256]{3,2,1,0:T(8,128)(2,1)}, bf16[3,2,128,256]{3,2,1,0:T(8,128)(2,1)}, u32[]{:S(2)}, u32[]{:S(2)}) collective-permute-start(bf16[3,2,128,256]{3,2,1,0:T(8,128)(2,1)} %get-tuple-element.94), channel_id=1, source_target_pairs={{0,4},{4,0},{8,12},{12,8},{16,20},{20,16},{24,28},{28,24},{1,5},{5... | collective-permute-start | bytes 1179656 | tf_op jit(solution)/shard_map/ppermute | solution.py:70
  13.5 17.1 %collective-permute-start.4 = (bf16[3,2,128,256]{3,2,1,0:T(8,128)(2,1)}, bf16[3,2,128,256]{3,2,1,0:T(8,128)(2,1)}, u32[]{:S(2)}, u32[]{:S(2)}) collective-permute-start(bf16[3,2,128,256]{3,2,1,0:T(8,128)(2,1)} %get-tuple-element.95), channel_id=1, source_target_pairs={{0,8},{4,12},{8,0},{12,4},{16,24},{20,28},{24,16},{28,20},{1,9},{5... | collective-permute-start | bytes 1179656 | tf_op jit(solution)/shard_map/ppermute | solution.py:70
  15.0 16.8 %collective-permute-start.5 = (bf16[3,2,128,256]{3,2,1,0:T(8,128)(2,1)}, bf16[3,2,128,256]{3,2,1,0:T(8,128)(2,1)}, u32[]{:S(2)}, u32[]{:S(2)}) collective-permute-start(bf16[3,2,128,256]{3,2,1,0:T(8,128)(2,1)} %get-tuple-element.96), channel_id=1, source_target_pairs={{0,12},{4,8},{8,4},{12,0},{16,28},{20,24},{24,20},{28,16},{1,13},{... | collective-permute-start | bytes 1179656 | tf_op jit(solution)/shard_map/ppermute | solution.py:70
  16.9 13.6 %collective-permute-start.7 = (bf16[1,256,512]{2,1,0:T(8,128)(2,1)}, bf16[1,256,512]{2,1,0:T(8,128)(2,1)}, u32[]{:S(2)}, u32[]{:S(2)}) collective-permute-start(bf16[1,256,512]{2,1,0:T(8,128)(2,1)} %get-tuple-element.176), channel_id=1, source_target_pairs={{0,2},{1,3},{2,0},{3,1},{4,6},{5,7},{6,4},{7,5},{8,10},{9,11},{10,... | collective-permute-start | bytes 786440 | tf_op jit(solution)/shard_map/ppermute | solution.py:70
  18.8 11.8 %collective-permute-start.6 = (bf16[1,256,512]{2,1,0:T(8,128)(2,1)}, bf16[1,256,512]{2,1,0:T(8,128)(2,1)}, u32[]{:S(2)}, u32[]{:S(2)}) collective-permute-start(bf16[1,256,512]{2,1,0:T(8,128)(2,1)} %get-tuple-element.177), channel_id=1, source_target_pairs={{0,2},{1,3},{2,0},{3,1},{4,6},{5,7},{6,4},{7,5},{8,10},{9,11},{10,... | collective-permute-start | bytes 786440 | tf_op jit(solution)/shard_map/ppermute | solution.py:70
  19.7 2.8 %copy-start = (f32[3,2,256,1024]{3,2,1,0:T(8,128)S(1)}, f32[3,2,256,1024]{3,2,1,0:T(8,128)}, u32[]{:S(2)}) copy-start(f32[3,2,256,1024]{3,2,1,0:T(8,128)} %slope.2) | copy-start | bytes 18874372
  22.5 14.4 %copy-start.12 = (f32[2,6]{1,0:T(2,128)S(1)}, f32[2,6]{1,0:T(2,128)}, u32[]{:S(2)}) copy-start(f32[2,6]{1,0:T(2,128)} %coupling.7) | copy-start | bytes 148
  23.7 0.7 copy-start.8
  24.5 1.1 copy-start.10
  25.6 0.8 copy-start.13
  26.4 0.8 copy-start.14
  27.2 0.8 copy-start.15
  27.9 16.0 %copy-start.2 = (bf16[2,256,1024]{2,1,0:T(8,128)(2,1)S(1)}, bf16[2,256,1024]{2,1,0:T(8,128)(2,1)}, u32[]{:S(2)}) copy-start(bf16[2,256,1024]{2,1,0:T(8,128)(2,1)} %h_own) | copy-start | bytes 3145732
  31.8 43.8 %collective-permute-start.12 = (bf16[3,2,128,1024]{3,2,1,0:T(8,128)(2,1)}, bf16[3,2,128,1024]{3,2,1,0:T(8,128)(2,1)}, u32[]{:S(2)}, u32[]{:S(2)}) collective-permute-start(bf16[3,2,128,1024]{3,2,1,0:T(8,128)(2,1)} %get-tuple-element.135.refs_0_), channel_id=1, source_target_pairs={{0,2},{1,3},{2,0},{3,1},{4,6},{5,7},{6,4},{7,5},{8,10},{9,11},{10,... | collective-permute-start | bytes 4718600 | tf_op jit(solution)/shard_map/ppermute | solution.py:70
  33.4 26.2 %collective-permute-start.8 = (bf16[3,2,128,256]{3,2,1,0:T(8,128)(2,1)}, bf16[3,2,128,256]{3,2,1,0:T(8,128)(2,1)}, u32[]{:S(2)}, u32[]{:S(2)}) collective-permute-start(bf16[3,2,128,256]{3,2,1,0:T(8,128)(2,1)} %copy-done.15), channel_id=1, source_target_pairs={{0,4},{4,0},{8,12},{12,8},{16,20},{20,16},{24,28},{28,24},{1,5},{5... | collective-permute-start | bytes 1179656 | tf_op jit(solution)/shard_map/ppermute | solution.py:70
  34.9 24.7 %collective-permute-start.9 = (bf16[3,2,128,256]{3,2,1,0:T(8,128)(2,1)}, bf16[3,2,128,256]{3,2,1,0:T(8,128)(2,1)}, u32[]{:S(2)}, u32[]{:S(2)}) collective-permute-start(bf16[3,2,128,256]{3,2,1,0:T(8,128)(2,1)} %copy-done.14), channel_id=1, source_target_pairs={{0,8},{4,12},{8,0},{12,4},{16,24},{20,28},{24,16},{28,20},{1,9},{5... | collective-permute-start | bytes 1179656 | tf_op jit(solution)/shard_map/ppermute | solution.py:70
  36.5 26.6 %collective-permute-start.10 = (bf16[3,2,128,256]{3,2,1,0:T(8,128)(2,1)}, bf16[3,2,128,256]{3,2,1,0:T(8,128)(2,1)}, u32[]{:S(2)}, u32[]{:S(2)}) collective-permute-start(bf16[3,2,128,256]{3,2,1,0:T(8,128)(2,1)} %copy-done.13), channel_id=1, source_target_pairs={{0,12},{4,8},{8,4},{12,0},{16,28},{20,24},{24,20},{28,16},{1,13},{... | collective-permute-start | bytes 1179656 | tf_op jit(solution)/shard_map/ppermute | solution.py:70
  36.9 1.0 copy-start.6
  41.3 34.3 %collective-permute-start.11 = (bf16[6,2,128,256]{3,2,1,0:T(8,128)(2,1)}, bf16[6,2,128,256]{3,2,1,0:T(8,128)(2,1)}, u32[]{:S(2)}, u32[]{:S(2)}) collective-permute-start(bf16[6,2,128,256]{3,2,1,0:T(8,128)(2,1)} %partial_sums.2), channel_id=1, source_target_pairs={{0,16},{4,20},{8,24},{12,28},{16,0},{20,4},{24,8},{28,12},{1,17},{... | collective-permute-start | bytes 2359304 | tf_op jit(solution)/shard_map/ppermute | solution.py:70
  45.4 14.0 %copy-start.3 = (bf16[3,2,128,1024]{3,2,1,0:T(8,128)(2,1)S(1)}, bf16[3,2,128,1024]{3,2,1,0:T(8,128)(2,1)}, u32[]{:S(2)}) copy-start(bf16[3,2,128,1024]{3,2,1,0:T(8,128)(2,1)} %get-tuple-element.135.refs_0_) | copy-start | bytes 4718596
  58.1 18.0 %copy-start.11 = (bf16[3,2,128,1024]{3,2,1,0:T(8,128)(2,1)S(1)}, bf16[3,2,128,1024]{3,2,1,0:T(8,128)(2,1)}, u32[]{:S(2)}) copy-start(bf16[3,2,128,1024]{3,2,1,0:T(8,128)(2,1)} %copy-done.10) | copy-start | bytes 4718596
  58.2 18.7 %copy-start.9 = (bf16[3,2,128,256]{3,2,1,0:T(8,128)(2,1)S(1)}, bf16[3,2,128,256]{3,2,1,0:T(8,128)(2,1)}, u32[]{:S(2)}) copy-start(bf16[3,2,128,256]{3,2,1,0:T(8,128)(2,1)} %copy-done.8) | copy-start | bytes 1179652
  59.4 20.0 %copy-start.7 = (bf16[3,2,128,256]{3,2,1,0:T(8,128)(2,1)S(1)}, bf16[3,2,128,256]{3,2,1,0:T(8,128)(2,1)}, u32[]{:S(2)}) copy-start(bf16[3,2,128,256]{3,2,1,0:T(8,128)(2,1)} %get-tuple-element.90.refs_0_) | copy-start | bytes 1179652
  75.6 7.9 %collective-permute-start.15 = (bf16[1280,1024]{1,0:T(8,128)(2,1)S(1)}, bf16[1280,1024]{1,0:T(8,128)(2,1)S(1)}, u32[]{:S(2)}, u32[]{:S(2)}) collective-permute-start(bf16[1280,1024]{1,0:T(8,128)(2,1)S(1)} %pad_maximum_fusion), channel_id=1, source_target_pairs={{0,1},{1,0},{2,3},{3,2},{4,5},{5,4},{6,7},{7,6},{8,9},{9,8},{10,11... | collective-permute-start | bytes 7864328 | tf_op jit(solution)/shard_map/ppermute | solution.py:70
  75.6 7.9 %collective-permute-start.16 = (bf16[3,2,128,1024]{3,2,1,0:T(8,128)(2,1)}, bf16[3,2,128,1024]{3,2,1,0:T(8,128)(2,1)S(1)}, u32[]{:S(2)}, u32[]{:S(2)}) collective-permute-start(bf16[3,2,128,1024]{3,2,1,0:T(8,128)(2,1)} %collective-permute-done.12.refs_2_), channel_id=1, source_target_pairs={{0,1},{1,0},{2,3},{3,2},{4,5},{5,4},{6,7},{7,6},{8,9},{9,8},{10,11... | collective-permute-start | bytes 4718600 | tf_op jit(solution)/shard_map/ppermute | solution.py:70
  76.1 41.1 %collective-permute-start.14 = (bf16[3,2,128,1024]{3,2,1,0:T(8,128)(2,1)S(1)}, bf16[3,2,128,1024]{3,2,1,0:T(8,128)(2,1)S(1)}, u32[]{:S(2)}, u32[]{:S(2)}) collective-permute-start(bf16[3,2,128,1024]{3,2,1,0:T(8,128)(2,1)S(1)} %copy-done.11), channel_id=1, source_target_pairs={{0,2},{1,3},{2,0},{3,1},{4,6},{5,7},{6,4},{7,5},{8,10},{9,11},{10,... | collective-permute-start | bytes 4718600 | tf_op jit(solution)/shard_map/ppermute | solution.py:70
  76.8 6.7 %collective-permute-start.17 = (bf16[2,256,512]{2,1,0:T(8,128)(2,1)S(1)}, bf16[2,256,512]{2,1,0:T(8,128)(2,1)S(1)}, u32[]{:S(2)}, u32[]{:S(2)}) collective-permute-start(bf16[2,256,512]{2,1,0:T(8,128)(2,1)S(1)} %pad_maximum_fusion.1.refs_4_), channel_id=1, source_target_pairs={{0,1},{1,0},{2,3},{3,2},{4,5},{5,4},{6,7},{7,6},{8,9},{9,8},{10,11... | collective-permute-start | bytes 1572872 | tf_op jit(solution)/shard_map/ppermute | solution.py:70
  79.3 37.9 %collective-permute-start.13 = (bf16[6,2,128,256]{3,2,1,0:T(8,128)(2,1)S(1)}, bf16[6,2,128,256]{3,2,1,0:T(8,128)(2,1)S(1)}, u32[]{:S(2)}, u32[]{:S(2)}) collective-permute-start(bf16[6,2,128,256]{3,2,1,0:T(8,128)(2,1)S(1)} %partial_sums.3), channel_id=1, source_target_pairs={{0,16},{4,20},{8,24},{12,28},{16,0},{20,4},{24,8},{28,12},{1,17},{... | collective-permute-start | bytes 2359304 | tf_op jit(solution)/shard_map/ppermute | solution.py:70
  83.5 37.5 %collective-permute-start.18 = (bf16[3,2,128,256]{3,2,1,0:T(8,128)(2,1)S(1)}, bf16[3,2,128,256]{3,2,1,0:T(8,128)(2,1)S(1)}, u32[]{:S(2)}, u32[]{:S(2)}) collective-permute-start(bf16[3,2,128,256]{3,2,1,0:T(8,128)(2,1)S(1)} %get-tuple-element.158), channel_id=1, source_target_pairs={{0,4},{4,0},{8,12},{12,8},{16,20},{20,16},{24,28},{28,24},{1,5},{5... | collective-permute-start | bytes 1179656 | tf_op jit(solution)/shard_map/ppermute | solution.py:70
  85.0 36.0 %collective-permute-start.19 = (bf16[3,2,128,256]{3,2,1,0:T(8,128)(2,1)S(1)}, bf16[3,2,128,256]{3,2,1,0:T(8,128)(2,1)S(1)}, u32[]{:S(2)}, u32[]{:S(2)}) collective-permute-start(bf16[3,2,128,256]{3,2,1,0:T(8,128)(2,1)S(1)} %get-tuple-element.159), channel_id=1, source_target_pairs={{0,8},{4,12},{8,0},{12,4},{16,24},{20,28},{24,16},{28,20},{1,9},{5... | collective-permute-start | bytes 1179656 | tf_op jit(solution)/shard_map/ppermute | solution.py:70
  88.9 33.6 %collective-permute-start.20 = (bf16[3,2,128,256]{3,2,1,0:T(8,128)(2,1)S(1)}, bf16[3,2,128,256]{3,2,1,0:T(8,128)(2,1)S(1)}, u32[]{:S(2)}, u32[]{:S(2)}) collective-permute-start(bf16[3,2,128,256]{3,2,1,0:T(8,128)(2,1)S(1)} %get-tuple-element.160), channel_id=1, source_target_pairs={{0,12},{4,8},{8,4},{12,0},{16,28},{20,24},{24,20},{28,16},{1,13},{... | collective-permute-start | bytes 1179656 | tf_op jit(solution)/shard_map/ppermute | solution.py:70
  88.9 9.8 %copy-start.5 = (bf16[2,256,512]{2,1,0:T(8,128)(2,1)S(1)}, bf16[2,256,512]{2,1,0:T(8,128)(2,1)}, u32[]{:S(2)}) copy-start(bf16[2,256,512]{2,1,0:T(8,128)(2,1)} %reshape_squeeze.6.h_own) | copy-start | bytes 1572868
  98.7 29.4 %copy-start.4 = (bf16[2,256,512]{2,1,0:T(8,128)(2,1)S(1)}, bf16[2,256,512]{2,1,0:T(8,128)(2,1)}, u32[]{:S(2)}) copy-start(bf16[2,256,512]{2,1,0:T(8,128)(2,1)} %reshape_squeeze.7.h_own) | copy-start | bytes 1572868
  117.2 17.1 %slice-start = ((s8[6291456]{0:T(1024)(128)(4,1)}), s8[4194304]{0:T(1024)(128)(4,1)S(1)}, s32[]{:S(2)}) async-start(s8[6291456]{0:T(1024)(128)(4,1)} %bitcast.7), calls=%async_computation | async-start | bytes 8388608
  122.4 11.8 %slice-start.1 = ((s8[6291456]{0:T(1024)(128)(4,1)}), s8[2097152]{0:T(1024)(128)(4,1)S(1)}, s32[]{:S(2)}) async-start(s8[6291456]{0:T(1024)(128)(4,1)} %bitcast.7), calls=%async_computation.1 | async-start | bytes 4194304
  122.5 4.0 %collective-permute-start.21 = (bf16[3,2,128,1024]{3,2,1,0:T(8,128)(2,1)S(1)}, bf16[3,2,128,1024]{3,2,1,0:T(8,128)(2,1)S(1)}, u32[]{:S(2)}, u32[]{:S(2)}) collective-permute-start(bf16[3,2,128,1024]{3,2,1,0:T(8,128)(2,1)S(1)} %copy-done.11), channel_id=1, source_target_pairs={{0,1},{1,0},{2,3},{3,2},{4,5},{5,4},{6,7},{7,6},{8,9},{9,8},{10,11... | collective-permute-start | bytes 4718600 | tf_op jit(solution)/shard_map/ppermute | solution.py:70
  122.5 5.7 %collective-permute-start.22 = (bf16[3,2,128,1024]{3,2,1,0:T(8,128)(2,1)S(1)}, bf16[3,2,128,1024]{3,2,1,0:T(8,128)(2,1)S(1)}, u32[]{:S(2)}, u32[]{:S(2)}) collective-permute-start(bf16[3,2,128,1024]{3,2,1,0:T(8,128)(2,1)S(1)} %collective-permute-done.14.refs_2_), channel_id=1, source_target_pairs={{0,1},{1,0},{2,3},{3,2},{4,5},{5,4},{6,7},{7,6},{8,9},{9,8},{10,11... | collective-permute-start | bytes 4718600 | tf_op jit(solution)/shard_map/ppermute | solution.py:70
  123.0 15.3 %collective-permute-start.23 = (bf16[3,2,128,256]{3,2,1,0:T(8,128)(2,1)S(1)}, bf16[3,2,128,256]{3,2,1,0:T(8,128)(2,1)S(1)}, u32[]{:S(2)}, u32[]{:S(2)}) collective-permute-start(bf16[3,2,128,256]{3,2,1,0:T(8,128)(2,1)S(1)} %get-tuple-element.165), channel_id=1, source_target_pairs={{0,4},{4,0},{8,12},{12,8},{16,20},{20,16},{24,28},{28,24},{1,5},{5... | collective-permute-start | bytes 1179656 | tf_op jit(solution)/shard_map/ppermute | solution.py:70
  124.6 13.6 %collective-permute-start.24 = (bf16[3,2,128,256]{3,2,1,0:T(8,128)(2,1)S(1)}, bf16[3,2,128,256]{3,2,1,0:T(8,128)(2,1)S(1)}, u32[]{:S(2)}, u32[]{:S(2)}) collective-permute-start(bf16[3,2,128,256]{3,2,1,0:T(8,128)(2,1)S(1)} %get-tuple-element.166), channel_id=1, source_target_pairs={{0,8},{4,12},{8,0},{12,4},{16,24},{20,28},{24,16},{28,20},{1,9},{5... | collective-permute-start | bytes 1179656 | tf_op jit(solution)/shard_map/ppermute | solution.py:70
  124.7 18.9 %collective-permute-start.25 = (bf16[3,2,128,256]{3,2,1,0:T(8,128)(2,1)S(1)}, bf16[3,2,128,256]{3,2,1,0:T(8,128)(2,1)S(1)}, u32[]{:S(2)}, u32[]{:S(2)}) collective-permute-start(bf16[3,2,128,256]{3,2,1,0:T(8,128)(2,1)S(1)} %get-tuple-element.167), channel_id=1, source_target_pairs={{0,12},{4,8},{8,4},{12,0},{16,28},{20,24},{24,20},{28,16},{1,13},{... | collective-permute-start | bytes 1179656 | tf_op jit(solution)/shard_map/ppermute | solution.py:70
